TPU v7x, 32 devices: a whole 2x2x4 slice. The times are simulated.
32 devices in a mesh: seq: 4 (over z), dp: 8 (over y, x, core).
Axes of the slice: x: 2, y: 2, z: 4, core: 2. Of those that a mesh axis runs over, the one named last changes fastest.
Arguments:
- tokens: bfloat16 [8, 2048, 1024], P('dp', 'seq'), may hold values from -6 to 6
- lengths: int32 [8, 4], P('dp'), may hold values from 0 to 2048, as said below
- cotangent: bfloat16 [8, 2048, 1024], P('dp', 'seq'), may hold values from -6 to 6
- mixer_input: bfloat16 [1024, 3072], P('dp'), may hold values from -0.1875 to 0.1875
- mixer_output: bfloat16 [1024, 1024], P('dp'), may hold values from -1.5 to 1.5
- expand_weight: bfloat16 [1024, 4096], P('dp'), may hold values from -0.1875 to 0.1875
- reduce_weight: bfloat16 [4096, 1024], P('dp'), may hold values from -0.09375 to 0.09375
- first_gain: bfloat16 [1024], P('dp'), may hold values from 0.5 to 1.5
- first_shift: bfloat16 [1024], P('dp'), may hold values from -4 to 4
- second_gain: bfloat16 [1024], P('dp'), may hold values from 0.5 to 1.5
- second_shift: bfloat16 [1024], P('dp'), may hold values from -4 to 4
- output_bias: bfloat16 [1024], P('dp'), may hold values from -4 to 4
- expand_bias: bfloat16 [4096], P('dp'), may hold values from -4 to 4
- reduce_bias: bfloat16 [1024], P('dp'), may hold values from -4 to 4
Outputs:
- layer_output: bfloat16 [8, 2048, 1024], P('dp', 'seq')
- tokens_gradient: float32 [8, 2048, 1024], P('dp', 'seq')
- mixer_input_gradient: float32 [1024, 3072], P('dp')
- mixer_output_gradient: float32 [1024, 1024], P('dp')
- expand_weight_gradient: float32 [1024, 4096], P('dp')
- reduce_weight_gradient: float32 [4096, 1024], P('dp')
- first_gain_gradient: float32 [1024], P('dp')
- first_shift_gradient: float32 [1024], P('dp')
- second_gain_gradient: float32 [1024], P('dp')
- second_shift_gradient: float32 [1024], P('dp')
- output_bias_gradient: float32 [1024], P('dp')
- expand_bias_gradient: float32 [4096], P('dp')
- reduce_bias_gradient: float32 [1024], P('dp')
Inputs may be any that keep to these rules, and one draw needn't show every extreme that they name: `lengths`: entries are 0 or 64 to 2048; a bucket's entries sum to at most 2048; in every bucket one sequence begins in the first quarter of the slots and ends in the last quarter; some bucket holds one sequence of 2048.
All inputs are finite; a program needn't handle non-finite values.
Results may differ from a plain program's by a relative error of at most 0.0096.
Values may be sent and summed in bfloat16 or wider, within the bound.
A program may use at most 256 MiB of HBM per device.

v0:
```python
from functools import partial

import jax
import jax.numpy as jnp
from jax import lax
from jax.sharding import PartitionSpec as P

HEADS = 16


norm_eps = 1e-05
masked_score = -1e30
grouping = 4


def layer_normalize(values, gain, shift):
    center = values - jnp.mean(values, axis=-1, keepdims=True)
    spread = jnp.mean(center * center, axis=-1, keepdims=True)
    return center * lax.rsqrt(spread + norm_eps) * gain + shift


def smooth_gate(values):
    return jax.nn.gelu(values, approximate=True)


def plain_product(left, right):
    return jnp.dot(left, right, preferred_element_type=jnp.float32)


def left_product(left, right):
    return lax.dot_general(
        left, right, (((0,), (0,)), ((), ())), preferred_element_type=jnp.float32
    )


def right_product(left, right):
    return lax.dot_general(
        left, right, (((1,), (1,)), ((), ())), preferred_element_type=jnp.float32
    )


def visible_mask(lengths_row, query_place, key_place):
    ends = jnp.cumsum(lengths_row)
    query_doc = jnp.sum((query_place[:, None] >= ends[None, :]).astype(jnp.int32), axis=1)
    key_doc = jnp.sum((key_place[:, None] >= ends[None, :]).astype(jnp.int32), axis=1)
    key_live = key_place < ends[-1]
    same_doc = (
        key_live[None, :]
        & (query_doc[:, None] == key_doc[None, :])
        & (key_place[None, :] <= query_place[:, None])
    )
    return same_doc | (key_place[None, :] == query_place[:, None])


def split_heads(array, groups):
    return jnp.moveaxis(array.reshape(array.shape[0], groups, grouping, -1), 1, 0)


def merge_heads(array):
    moved = jnp.moveaxis(array, 0, 1)
    return moved.reshape(moved.shape[0], -1)


def group_forward(parts, allowed, scale):
    queries, keys_all, values_all = parts
    scores = (
        jnp.einsum("qhd,khd->hqk", queries, keys_all, preferred_element_type=jnp.float32) * scale
    )
    scores = jnp.where(allowed[None], scores, masked_score)
    highest = jnp.max(scores, axis=-1, keepdims=True)
    powers = jnp.exp(scores - highest)
    totals = jnp.sum(powers, axis=-1, keepdims=True)
    shares = (powers / totals).astype(jnp.bfloat16)
    attended = jnp.einsum("hqk,khd->qhd", shares, values_all, preferred_element_type=jnp.float32)
    return (attended, highest + jnp.log(totals))


def group_backward(parts, allowed, scale):
    queries, keys_all, values_all, logsum, grad_out = parts
    scores = (
        jnp.einsum("qhd,khd->hqk", queries, keys_all, preferred_element_type=jnp.float32) * scale
    )
    scores = jnp.where(allowed[None], scores, masked_score)
    shares = jnp.exp(scores - logsum)
    shares_low = shares.astype(jnp.bfloat16)
    grad_shares = jnp.einsum(
        "qhd,khd->hqk", grad_out, values_all, preferred_element_type=jnp.float32
    )
    center = jnp.sum(grad_shares * shares, axis=-1, keepdims=True)
    grad_scores = (shares * (grad_shares - center)).astype(jnp.bfloat16)
    grad_queries = (
        jnp.einsum("hqk,khd->qhd", grad_scores, keys_all, preferred_element_type=jnp.float32)
        * scale
    )
    grad_keys = (
        jnp.einsum("hqk,qhd->khd", grad_scores, queries, preferred_element_type=jnp.float32) * scale
    )
    grad_values = jnp.einsum(
        "hqk,qhd->khd", shares_low, grad_out, preferred_element_type=jnp.float32
    )
    return (grad_queries, grad_keys, grad_values)


def on_device(
    tokens,
    lengths,
    cotangent,
    mixer_input,
    mixer_output,
    expand_weight,
    reduce_weight,
    first_gain,
    first_shift,
    second_gain,
    second_shift,
    output_bias,
    expand_bias,
    reduce_bias,
):
    forward_set = (
        lax.all_gather(mixer_input, "dp", axis=0, tiled=True),
        lax.all_gather(mixer_output, "dp", axis=0, tiled=True),
        lax.all_gather(expand_weight, "dp", axis=0, tiled=True),
        lax.all_gather(reduce_weight, "dp", axis=0, tiled=True),
        lax.all_gather(first_gain, "dp", axis=0, tiled=True),
        lax.all_gather(first_shift, "dp", axis=0, tiled=True),
        lax.all_gather(second_gain, "dp", axis=0, tiled=True),
        lax.all_gather(second_shift, "dp", axis=0, tiled=True),
        lax.all_gather(output_bias, "dp", axis=0, tiled=True),
        lax.all_gather(expand_bias, "dp", axis=0, tiled=True),
        lax.all_gather(reduce_bias, "dp", axis=0, tiled=True),
    )
    input_full, output_full, expand_full, reduce_full = forward_set[:4]
    small_set = tuple((piece.astype(jnp.float32) for piece in forward_set[4:]))
    gain_one, shift_one, gain_two, shift_two, output_add, expand_add, reduce_add = small_set
    rows = tokens.shape[1]
    width = tokens.shape[2]
    slots = rows * lax.axis_size("seq")
    groups = HEADS // grouping
    scale = (width // HEADS) ** (-0.5)
    query_place = lax.axis_index("seq") * rows + jnp.arange(rows, dtype=jnp.int32)
    key_place = jnp.arange(slots, dtype=jnp.int32)
    bucket = 0
    inputs = tokens[bucket].astype(jnp.float32)
    normed_one = layer_normalize(inputs, gain_one, shift_one).astype(jnp.bfloat16)
    mixed = plain_product(normed_one, input_full).astype(jnp.bfloat16)
    queries = mixed[:, :width]
    keys_local = mixed[:, width : 2 * width]
    values_local = mixed[:, 2 * width :]
    keys_all = lax.all_gather(keys_local, "seq", axis=0, tiled=True)
    values_all = lax.all_gather(values_local, "seq", axis=0, tiled=True)
    allowed = visible_mask(lengths[bucket], query_place, key_place)
    head_queries = split_heads(queries, groups)
    head_keys = split_heads(keys_all, groups)
    head_values = split_heads(values_all, groups)
    attended, logsum = lax.map(
        partial(group_forward, allowed=allowed, scale=scale), (head_queries, head_keys, head_values)
    )
    attention = merge_heads(attended).astype(jnp.bfloat16)
    resid = inputs + plain_product(attention, output_full) + output_add
    normed_two = layer_normalize(resid, gain_two, shift_two).astype(jnp.bfloat16)
    expanded = plain_product(normed_two, expand_full) + expand_add
    active = smooth_gate(expanded).astype(jnp.bfloat16)
    result = resid + plain_product(active, reduce_full) + reduce_add
    outputs = [result.astype(jnp.bfloat16)]
    saved = [
        (
            inputs,
            normed_one,
            queries,
            keys_local,
            values_local,
            head_queries,
            head_keys,
            head_values,
            logsum,
            allowed,
            attention,
            resid,
            normed_two,
            expanded,
            active,
        )
    ]
    backward_set = (
        lax.all_gather(mixer_input, "dp", axis=0, tiled=True),
        lax.all_gather(mixer_output, "dp", axis=0, tiled=True),
        lax.all_gather(expand_weight, "dp", axis=0, tiled=True),
        lax.all_gather(reduce_weight, "dp", axis=0, tiled=True),
        lax.all_gather(first_gain, "dp", axis=0, tiled=True),
        lax.all_gather(first_shift, "dp", axis=0, tiled=True),
        lax.all_gather(second_gain, "dp", axis=0, tiled=True),
        lax.all_gather(second_shift, "dp", axis=0, tiled=True),
        lax.all_gather(output_bias, "dp", axis=0, tiled=True),
        lax.all_gather(expand_bias, "dp", axis=0, tiled=True),
        lax.all_gather(reduce_bias, "dp", axis=0, tiled=True),
    )
    input_back, output_back, expand_back, reduce_back = backward_set[:4]
    back_small = tuple((piece.astype(jnp.float32) for piece in backward_set[4:]))
    gain_one_back, shift_one_back, gain_two_back, shift_two_back = back_small[:4]
    bucket = 0
    (
        inputs,
        normed_one,
        queries,
        keys_local,
        values_local,
        head_queries,
        head_keys,
        head_values,
        logsum,
        allowed,
        attention,
        resid,
        normed_two,
        expanded,
        active,
    ) = saved[bucket]
    live = (query_place < jnp.sum(lengths[bucket])).astype(jnp.float32)
    grad_result = cotangent[bucket].astype(jnp.float32) * live[:, None]
    result_low = grad_result.astype(jnp.bfloat16)
    reduce_sum = left_product(active, result_low)
    reduce_bias_sum = jnp.sum(grad_result, axis=0)
    grad_active = right_product(result_low, reduce_back)
    gate_value, gate_back = jax.vjp(smooth_gate, expanded)
    grad_expanded = gate_back(grad_active)[0]
    expand_bias_sum = jnp.sum(grad_expanded, axis=0)
    expanded_low = grad_expanded.astype(jnp.bfloat16)
    expand_sum = left_product(normed_two, expanded_low)
    grad_normed_two = right_product(expanded_low, expand_back)
    norm_value, second_back = jax.vjp(layer_normalize, resid, gain_two_back, shift_two_back)
    resid_part, gain_part, shift_part = second_back(grad_normed_two)
    gain_two_sum = gain_part
    shift_two_sum = shift_part
    grad_resid = grad_result + resid_part
    output_bias_sum = jnp.sum(grad_resid, axis=0)
    resid_low = grad_resid.astype(jnp.bfloat16)
    output_sum = left_product(attention, resid_low)
    grad_attention = right_product(resid_low, output_back).astype(jnp.bfloat16)
    grad_queries, grad_keys, grad_values = lax.map(
        partial(group_backward, allowed=allowed, scale=scale),
        (head_queries, head_keys, head_values, logsum, split_heads(grad_attention, groups)),
    )
    keys_grad = lax.psum_scatter(merge_heads(grad_keys), "seq", scatter_dimension=0, tiled=True)
    values_grad = lax.psum_scatter(merge_heads(grad_values), "seq", scatter_dimension=0, tiled=True)
    grad_mixed = jnp.concatenate(
        [merge_heads(grad_queries), keys_grad, values_grad], axis=1
    ).astype(jnp.bfloat16)
    input_sum = left_product(normed_one, grad_mixed)
    grad_normed_one = right_product(grad_mixed, input_back)
    first_value, first_back = jax.vjp(layer_normalize, inputs, gain_one_back, shift_one_back)
    inputs_part, gain_part, shift_part = first_back(grad_normed_one)
    input_grads = [grad_resid + inputs_part]
    shards = (
        lax.psum_scatter(input_sum, "dp", scatter_dimension=0, tiled=True),
        lax.psum_scatter(output_sum, "dp", scatter_dimension=0, tiled=True),
        lax.psum_scatter(expand_sum, "dp", scatter_dimension=0, tiled=True),
        lax.psum_scatter(reduce_sum, "dp", scatter_dimension=0, tiled=True),
        lax.psum_scatter(gain_part, "dp", scatter_dimension=0, tiled=True),
        lax.psum_scatter(shift_part, "dp", scatter_dimension=0, tiled=True),
        lax.psum_scatter(gain_two_sum, "dp", scatter_dimension=0, tiled=True),
        lax.psum_scatter(shift_two_sum, "dp", scatter_dimension=0, tiled=True),
        lax.psum_scatter(output_bias_sum, "dp", scatter_dimension=0, tiled=True),
        lax.psum_scatter(expand_bias_sum, "dp", scatter_dimension=0, tiled=True),
        lax.psum_scatter(reduce_bias_sum, "dp", scatter_dimension=0, tiled=True),
    )
    (
        input_part,
        output_part,
        expand_part,
        reduce_part,
        gain_one_part,
        shift_one_part,
        gain_two_part,
        shift_two_part,
        output_bias_part,
        expand_bias_part,
        reduce_bias_part,
    ) = shards
    totals = lax.psum(
        (
            input_part,
            output_part,
            expand_part,
            reduce_part,
            gain_one_part,
            shift_one_part,
            gain_two_part,
            shift_two_part,
            output_bias_part,
            expand_bias_part,
            reduce_bias_part,
        ),
        "seq",
    )
    return (
        jnp.stack(outputs),
        jnp.stack(input_grads),
        totals[0],
        totals[1],
        totals[2],
        totals[3],
        totals[4],
        totals[5],
        totals[6],
        totals[7],
        totals[8],
        totals[9],
        totals[10],
    )


def solution(mesh):
    return jax.shard_map(
        on_device,
        mesh=mesh,
        in_specs=(
            P("dp", "seq", None),
            P("dp", None),
            P("dp", "seq", None),
            P("dp", None),
            P("dp", None),
            P("dp", None),
            P("dp", None),
            P("dp"),
            P("dp"),
            P("dp"),
            P("dp"),
            P("dp"),
            P("dp"),
            P("dp"),
        ),
        out_specs=(
            P("dp", "seq", None),
            P("dp", "seq", None),
            P("dp", None),
            P("dp", None),
            P("dp", None),
            P("dp", None),
            P("dp"),
            P("dp"),
            P("dp"),
            P("dp"),
            P("dp"),
            P("dp"),
            P("dp"),
        ),
        check_vma=False,
    )
```

profile of v0, /device:TPU:0, one launch (start us, length us, event | category | flops | bytes accessed | tf_op | source)
XLA Modules:
  0.0 1515.4 jit_solution(10845592738842491996)
XLA Ops:
  8.0 10.3 all-gather
  18.3 8.6 all-gather.1
  30.6 27.6 %all-gather.14.cloned.1.call-done = bf16[1024,3072]{1,0:T(8,128)(2,1)} async-done(((bf16[128,3072]{1,0:T(8,128)(2,1)}), bf16[1024,3072]{1,0:T(8,128)(2,1)}) %all-gather.14.cloned.1.call-update) | async-done | bytes 6291472 | tf_op jit(solution)/shard_map/all_gather | solution.py:121
  58.2 6.7 convolution_convert_fusion
  72.6 8.7 all-gather.3
  81.9 7.8 all-gather.4
  90.3 8.7 all-gather.2
  99.6 8.1 all-gather.5
  108.9 38.6 %all-gather.18.cloned.1.call-done = bf16[2048,1024]{1,0:T(8,128)(2,1)} async-done(((bf16[512,1024]{1,0:T(8,128)(2,1)}), bf16[2048,1024]{1,0:T(8,128)(2,1)}) %all-gather.18.cloned.1.call-update) | async-done | bytes 4194320 | tf_op jit(solution)/shard_map/all_gather | solution.py:150
  147.5 6.5 copy.41
  154.0 74.9 %all-gather.16.cloned.1.call-done = bf16[2048,1024]{1,0:T(8,128)(2,1)} async-done(((bf16[512,1024]{1,0:T(8,128)(2,1)}), bf16[2048,1024]{1,0:T(8,128)(2,1)}) %all-gather.16.cloned.1.call-update) | async-done | bytes 4194320 | tf_op jit(solution)/shard_map/all_gather | solution.py:151
  229.0 6.5 copy.39
  235.6 68.7 %while.28 = (s32[]{:T(128)}, bf16[4,512,4,64]{1,3,2,0:T(8,128)(2,1)S(1)}, f32[4,4,512,1]{2,1,3,0:T(4,128)S(1)}, bf16[4,2048,4,64]{1,3,2,0:T(8,128)(2,1)}, bf16[4...) while((s32[]{:T(128)}, ...), condition=%wide.region_8.9_spmd.clone, body=%wide.region_5.8_spmd.clone.sunk | while | flops 1130362880 | bytes 57491576 | solution.py:156
  237.5 4.5 fusion.150
  242.0 4.4 fusion.151
  246.4 6.3 fusion.152
  254.7 4.5 fusion.150
  259.2 4.4 fusion.151
  263.6 6.3 fusion.152
  271.9 4.5 fusion.150
  276.4 4.4 fusion.151
  280.8 6.3 fusion.152
  289.1 4.5 fusion.150
  293.6 4.4 fusion.151
  298.0 6.3 fusion.152
  309.5 3.9 all-gather.22.cloned.1.call-done
  313.4 10.4 fusion.107
  323.8 45.7 %all-gather.24.cloned.1.call-done = bf16[4096,1024]{1,0:T(8,128)(2,1)} async-done(((bf16[512,1024]{1,0:T(8,128)(2,1)}), bf16[4096,1024]{1,0:T(8,128)(2,1)}) %all-gather.24.cloned.1.call-update) | async-done | bytes 8388624 | tf_op jit(solution)/shard_map/all_gather | solution.py:124
  369.6 14.3 fusion.115
  383.9 5.5 multiply_reduce_fusion.1
  393.7 196.7 %while.29 = (s32[]{:T(128)}, bf16[4,512,4,64]{1,3,2,0:T(8,128)(2,1)S(1)}, f32[4,2048,4,64]{1,3,2,0:T(8,128)}, f32[4,2048,4,64]{1,3,2,0:T(8,128)}, bf16[4,2048,4,...) while((s32[]{:T(128)}, ...), condition=%wide.region_16.17_spmd.clone, body=%wide.region_14.16_spmd.clone.sunk | while | flops 2754213888 | bytes 206122160 | solution.py:240
  399.4 5.7 copy-done
  405.2 6.0 fusion.165
  411.2 12.8 multiply_reduce_fusion.5
  424.0 12.1 multiply_convert_fusion.5
  448.5 5.7 copy-done
  454.3 6.0 fusion.165
  460.3 12.8 multiply_reduce_fusion.5
  473.1 12.1 multiply_convert_fusion.5
  485.2 3.9 fusion.163
  497.5 5.7 copy-done
  503.3 6.1 fusion.165
  509.4 12.8 multiply_reduce_fusion.5
  522.2 12.1 multiply_convert_fusion.5
  546.6 5.7 copy-done
  552.4 6.0 fusion.165
  558.4 12.8 multiply_reduce_fusion.5
  571.2 12.1 multiply_convert_fusion.5
  593.3 4.6 fusion.91
  599.1 15.8 %fusion.94 = f32[4096,1024]{1,0:T(8,128)} fusion(bf16[1,512,1024]{2,1,0:T(8,128)(2,1)S(1)} %copy-done.12, f32[512]{0:T(512)S(1)} %copy-done.30, f32[512,4096]{1,0:T(8,128)} %fusion.107, f32[4096]{0:T(1024)S(1)} %bitcast.234), kind=kOutput, calls=%fused_computation.118 | convolution fusion | flops 4317511680 | bytes 26232832 | tf_op jit(solution)/shard_map/dot_general | solution.py:31
  615.6 13.5 fusion.84
  629.4 105.7 %reduce-scatter.9.cloned.1.call-done = f32[512,1024]{0,1:T(8,128)} async-done(((f32[2048,1024]{0,1:T(8,128)}), f32[512,1024]{0,1:T(8,128)}) %reduce-scatter.9.cloned.1.call-update) | async-done | bytes 2097168 | tf_op jit(solution)/shard_map/reduce_scatter | solution.py:245
  737.8 144.9 %reduce-scatter.7.cloned.1.call-done = f32[512,1024]{0,1:T(8,128)} async-done(((f32[2048,1024]{0,1:T(8,128)}), f32[512,1024]{0,1:T(8,128)}) %reduce-scatter.7.cloned.1.call-update) | async-done | bytes 2097168 | tf_op jit(solution)/shard_map/reduce_scatter | solution.py:244
  885.4 10.7 fusion.89
  896.2 41.9 %reduce-scatter.13.cloned.1.call-done = f32[128,1024]{1,0:T(8,128)} async-done(((f32[1024,1024]{1,0:T(8,128)}), f32[128,1024]{1,0:T(8,128)}) %reduce-scatter.13.cloned.1.call-update) | async-done | bytes 524304 | tf_op jit(solution)/shard_map/reduce_scatter | solution.py:256
  938.1 119.8 %reduce-scatter.17.cloned.1.call-done = f32[512,1024]{1,0:T(8,128)} async-done(((f32[4096,1024]{1,0:T(8,128)}), f32[512,1024]{1,0:T(8,128)}) %reduce-scatter.17.cloned.1.call-update) | async-done | bytes 2097168 | tf_op jit(solution)/shard_map/reduce_scatter | solution.py:258
  1057.9 120.0 %reduce-scatter.15.cloned.1.call-done = f32[128,4096]{1,0:T(8,128)} async-done(((f32[1024,4096]{1,0:T(8,128)}), f32[128,4096]{1,0:T(8,128)}) %reduce-scatter.15.cloned.1.call-update) | async-done | bytes 2097168 | tf_op jit(solution)/shard_map/reduce_scatter | solution.py:257
  1177.9 96.2 %reduce-scatter.11.cloned.1.call-done = f32[128,3072]{1,0:T(8,128)} async-done(((f32[1024,3072]{1,0:T(8,128)}), f32[128,3072]{1,0:T(8,128)}) %reduce-scatter.11.cloned.1.call-update) | async-done | bytes 1572880 | tf_op jit(solution)/shard_map/reduce_scatter | solution.py:255
  1276.0 8.6 all-gather.6
  1284.6 12.9 fusion.88
  1297.6 6.8 fusion.111
  1307.8 25.7 %all-reduce.7 = (f32[1024]{0:T(1024)S(1)}, f32[1024]{0:T(1024)S(1)}, f32[1024]{0:T(1024)S(1)}, f32[1024]{0:T(1024)S(1)}, f32[1024]{0:T(1024)S(1)}, /*index=5*/f32[4096]{0:T(1024)S(1)}, f32[1024]{0:T(1024)S(1)}) all-reduce(f32[1024]{0:T(1024)S(1)} %get-tuple-element.170, ...), channel_id=8, replica_groups=mesh['seq'=4,'dp'=8] {'dp'}, use_global_device_ids=true, to_apply=%region_30.31.clone | all-reduce | flops 10240 | bytes 81920
  1334.0 15.5 %all-reduce.8 = (f32[128]{0:T(128)}, f32[128]{0:T(128)}, f32[128]{0:T(128)}, f32[128]{0:T(128)}, f32[128]{0:T(128)}, /*index=5*/f32[512]{0:T(512)}, f32[128]{0:T(128)}) all-reduce(f32[128]{0:T(128)S(1)} %dynamic-slice.1, f32[128]{0:T(128)S(1)} %dynamic-slice.3, f32[128]{0:T(128)S(1)} %dynamic-slice.5, ...), channel_id=1, replica_groups=mesh['seq'=4,'dp'=8] {'seq'}, use_global_device_ids=true, to_apply=%region_31.32 | all-reduce | flops 1280 | bytes 10240 | tf_op jit(solution)/shard_map/psum | solution.py:280
  1349.5 151.8 %all-reduce.12.cloned.1.call-done = (f32[128,3072]{1,0:T(8,128)}, f32[128,1024]{1,0:T(8,128)}, f32[128,4096]{1,0:T(8,128)}, f32[512,1024]{1,0:T(8,128)}) async-done(((f32[128,3072]{1,0:T(8,128)}, f32[128,1024]{1,0:T(8,128)}, f32[128,4096]{1,0:T(8,128)}, f32[512,1024]{1,0:T(8,128)}), (f32[128,3072]{1,0:T(8,128)}, f32[128,1024]{1,0:T(8,128)}, f32[128,4096]{1,0:T(8,128)}, ...) | async-done | bytes 6291472 | tf_op jit(solution)/shard_map/psum | solution.py:280
  (228 shorter events, 100.1 us)
Async XLA Ops:
  7.2 51.0 %all-gather.14.cloned.1.call-start = ((), (), s32[]{:S(2)}) async-start(), calls=%async_computation.6 | async-start | bytes 7077888 | tf_op jit(solution)/shard_map/all_gather | solution.py:121
  7.9 139.6 %all-gather.18.cloned.1.call-start = ((), (), s32[]{:S(2)}) async-start(), calls=%async_computation.8 | async-start | bytes 5242880 | tf_op jit(solution)/shard_map/all_gather | solution.py:150
  18.3 39.9 %copy-start.23 = (f32[8,1,128]{2,1,0:T(1,128)}, f32[8,1,128]{2,1,0:T(1,128)S(1)}, u32[]{:S(2)}) copy-start(f32[8,1,128]{2,1,0:T(1,128)S(1)} %convert_element_type.121) | copy-start | bytes 12292
  26.9 31.3 %copy-start.46 = (f32[8,1,128]{2,1,0:T(1,128)}, f32[8,1,128]{2,1,0:T(1,128)S(1)}, u32[]{:S(2)}) copy-start(f32[8,1,128]{2,1,0:T(1,128)S(1)} %convert_element_type.122) | copy-start | bytes 12292
  28.3 29.8 %copy-start.25 = (f32[512]{0:T(512)}, f32[512]{0:T(512)S(1)}, u32[]{:S(2)}) copy-start(f32[512]{0:T(512)S(1)} %broadcast_multiply_fusion.1) | copy-start | bytes 6148
  30.6 27.6 %copy-start.27 = (f32[512]{0:T(512)}, f32[512]{0:T(512)S(1)}, u32[]{:S(2)}) copy-start(f32[512]{0:T(512)S(1)} %fusion.100) | copy-start | bytes 6148
  64.8 4.3 copy-start.56
  64.8 7.8 copy-start.50
  64.8 7.8 copy-start.51
  64.9 17.1 %copy-start.52 = (bf16[128]{0:T(256)(128)(2,1)S(1)}, bf16[128]{0:T(256)(128)(2,1)}, u32[]{:S(2)}) copy-start(bf16[128]{0:T(256)(128)(2,1)} %param.28) | copy-start | bytes 772
  64.9 25.4 %copy-start.53 = (bf16[128]{0:T(256)(128)(2,1)S(1)}, bf16[128]{0:T(256)(128)(2,1)}, u32[]{:S(2)}) copy-start(bf16[128]{0:T(256)(128)(2,1)} %param.29) | copy-start | bytes 772
  66.6 162.4 %all-gather.16.cloned.1.call-start = ((), (), s32[]{:S(2)}) async-start(), calls=%async_computation.7 | async-start | bytes 5242880 | tf_op jit(solution)/shard_map/all_gather | solution.py:151
  67.3 237.1 %all-gather.20.cloned.1.call-start = ((), (), s32[]{:S(2)}) async-start(), calls=%async_computation.9 | async-start | bytes 2359296 | tf_op jit(solution)/shard_map/all_gather | solution.py:122
  67.9 245.5 %all-gather.22.cloned.1.call-start = ((), (), s32[]{:S(2)}) async-start(), calls=%async_computation.10 | async-start | bytes 9437184 | tf_op jit(solution)/shard_map/all_gather | solution.py:123
  68.5 301.1 %all-gather.24.cloned.1.call-start = ((), (), s32[]{:S(2)}) async-start(), calls=%async_computation.11 | async-start | bytes 9437184 | tf_op jit(solution)/shard_map/all_gather | solution.py:124
  69.0 666.0 %reduce-scatter.9.cloned.1.call-start = ((), (), s32[]{:S(2)}) async-start(), calls=%async_computation.13 | async-start | bytes 10485760 | tf_op jit(solution)/shard_map/reduce_scatter | solution.py:245
  235.6 70.1 %copy-start.1 = (bf16[1,512,1024]{2,1,0:T(8,128)(2,1)S(1)}, bf16[1,512,1024]{2,1,0:T(8,128)(2,1)}, u32[]{:S(2)}) copy-start(bf16[1,512,1024]{2,1,0:T(8,128)(2,1)} %param.18) | copy-start | bytes 3145732
  235.6 70.1 %copy-start.22 = (f32[8,1,128]{2,1,0:T(1,128)S(1)}, f32[8,1,128]{2,1,0:T(1,128)}, u32[]{:S(2)}) copy-start(f32[8,1,128]{2,1,0:T(1,128)} %convert_element_type.123) | copy-start | bytes 12292
  305.7 7.7 copy-start.40
  305.7 7.7 copy-start.48
  309.1 80.3 %copy-start.5 = (f32[512,1024]{1,0:T(8,128)}, f32[512,1024]{1,0:T(8,128)S(1)}, u32[]{:S(2)}) copy-start(f32[512,1024]{1,0:T(8,128)S(1)} %get-tuple-element.252) | copy-start | bytes 6291460
  309.1 80.3 %copy-start.35 = (f32[512]{0:T(512)}, f32[512]{0:T(512)S(1)}, u32[]{:S(2)}) copy-start(f32[512]{0:T(512)S(1)} %broadcast_multiply_fusion) | copy-start | bytes 6148
  309.5 79.9 %copy-start.42 = (f32[512]{0:T(512)}, f32[512]{0:T(512)S(1)}, u32[]{:S(2)}) copy-start(f32[512]{0:T(512)S(1)} %fusion.101) | copy-start | bytes 6148
  313.4 56.2 %copy-start.10 = (bf16[1,512,1024]{2,1,0:T(8,128)(2,1)S(1)}, bf16[1,512,1024]{2,1,0:T(8,128)(2,1)}, u32[]{:S(2)}) copy-start(bf16[1,512,1024]{2,1,0:T(8,128)(2,1)} %param.20) | copy-start | bytes 3145732
  313.4 56.2 %copy-start.29 = (f32[512]{0:T(512)S(1)}, f32[512]{0:T(512)}, u32[]{:S(2)}) copy-start(f32[512]{0:T(512)} %compare_convert_fusion) | copy-start | bytes 6148
  313.4 56.2 %copy-start.37 = (f32[8,1,512]{2,1,0:T(1,128)S(1)}, f32[8,1,512]{2,1,0:T(1,128)}, u32[]{:S(2)}) copy-start(f32[8,1,512]{2,1,0:T(1,128)} %convert_element_type.126) | copy-start | bytes 49156
  369.5 14.3 copy-start.55
  383.8 5.5 copy-start.58
  389.3 2.1 copy-start.11
  389.3 2.3 copy-start.14
  390.1 1.3 copy-start.3
  390.1 1.3 copy-start.31
  391.7 2.0 copy-start.7
  399.4 5.8 copy-start
  448.5 5.8 copy-start
  497.5 5.8 copy-start
  546.6 5.8 copy-start
  591.4 291.3 %reduce-scatter.7.cloned.1.call-start = ((), (), s32[]{:S(2)}) async-start(), calls=%async_computation.12 | async-start | bytes 10485760 | tf_op jit(solution)/shard_map/reduce_scatter | solution.py:244
  591.4 1.6 copy-start.4
  591.4 1.9 copy-start.9
  591.4 1.9 copy-start.30
  591.4 1.9 copy-start.32
  592.1 346.0 %reduce-scatter.13.cloned.1.call-start = ((), (), s32[]{:S(2)}) async-start(), calls=%async_computation.15 | async-start | bytes 4718592 | tf_op jit(solution)/shard_map/reduce_scatter | solution.py:256
  597.9 460.0 %reduce-scatter.17.cloned.1.call-start = ((), (), s32[]{:S(2)}) async-start(), calls=%async_computation.17 | async-start | bytes 18874368 | tf_op jit(solution)/shard_map/reduce_scatter | solution.py:258
  614.9 563.0 %reduce-scatter.15.cloned.1.call-start = ((), (), s32[]{:S(2)}) async-start(), calls=%async_computation.16 | async-start | bytes 18874368 | tf_op jit(solution)/shard_map/reduce_scatter | solution.py:257
  629.1 256.2 %copy-start.2 = (bf16[1,512,1024]{2,1,0:T(8,128)(2,1)S(1)}, bf16[1,512,1024]{2,1,0:T(8,128)(2,1)}, u32[]{:S(2)}) copy-start(bf16[1,512,1024]{2,1,0:T(8,128)(2,1)} %param.18) | copy-start | bytes 3145732
  629.2 256.2 %copy-start.24 = (f32[8,1,128]{2,1,0:T(1,128)S(1)}, f32[8,1,128]{2,1,0:T(1,128)}, u32[]{:S(2)}) copy-start(f32[8,1,128]{2,1,0:T(1,128)} %copy-done.23) | copy-start | bytes 12292
  629.2 256.2 %copy-start.26 = (f32[512]{0:T(512)S(1)}, f32[512]{0:T(512)}, u32[]{:S(2)}) copy-start(f32[512]{0:T(512)} %copy-done.25) | copy-start | bytes 6148
  629.2 256.2 %copy-start.28 = (f32[512]{0:T(512)S(1)}, f32[512]{0:T(512)}, u32[]{:S(2)}) copy-start(f32[512]{0:T(512)} %copy-done.27) | copy-start | bytes 6148
  629.2 256.2 %copy-start.47 = (f32[8,1,128]{2,1,0:T(1,128)S(1)}, f32[8,1,128]{2,1,0:T(1,128)}, u32[]{:S(2)}) copy-start(f32[8,1,128]{2,1,0:T(1,128)} %copy-done.46) | copy-start | bytes 12292
  629.2 644.9 %reduce-scatter.11.cloned.1.call-start = ((), (), s32[]{:S(2)}) async-start(), calls=%async_computation.14 | async-start | bytes 14155776 | tf_op jit(solution)/shard_map/reduce_scatter | solution.py:255
  896.1 378.0 %copy-start.57 = (u32[32]{0:T(128)S(1)}, u32[32]{0:T(128)}, u32[]{:S(2)}) copy-start(u32[32]{0:T(128)} %constant.93) | copy-start | bytes 388
  896.1 379.9 %copy-start.54 = (bf16[128]{0:T(256)(128)(2,1)S(1)}, bf16[128]{0:T(256)(128)(2,1)}, u32[]{:S(2)}) copy-start(bf16[128]{0:T(256)(128)(2,1)} %param.31) | copy-start | bytes 772
  896.2 605.1 %all-reduce.12.cloned.1.call-start = ((), (), s32[]{:S(2)}) async-start(), calls=%async_computation.18 | async-start | bytes 12582912 | tf_op jit(solution)/shard_map/psum | solution.py:280
  1284.6 13.0 copy-start.17
  1284.6 13.0 copy-start.19
  1284.6 13.0 copy-start.21
  1297.6 6.8 copy-start.34
  1297.6 7.8 copy-start.13
  1305.4 2.4 copy-start.39
  1305.4 2.4 copy-start.44
  1305.5 2.4 copy-start.45
  1501.3 4.7 copy-start.16
  1501.3 6.1 copy-start.15
  (11 other events, 10.0 us)
Sparse Core Ops, SparseCore 0:
  9.9 48.2 all-gather.13
  66.7 80.7 all-gather.17
  149.6 79.2 all-gather.15
  230.7 26.4 all-gather.19
  258.9 54.4 all-gather.21
  315.1 54.3 all-gather.23
  590.6 144.4 reduce-scatter.8
  737.4 145.1 reduce-scatter.6
  886.0 52.0 reduce-scatter.12
  942.0 115.9 reduce-scatter.16
  1061.9 115.9 reduce-scatter.14
  1181.7 92.3 reduce-scatter.10
  1276.9 224.3 all-reduce.11
where the time goes:
time: 1520 us
  waiting for transfers between devices  975 us (64%)
  matrix products  266 us (18%)
  blocking collectives  102 us (7%)
  other arithmetic  98.6 us (6%)
  local copies, waits for them, and re-layouts  56.4 us (4%)
  between operations  16 us (1%)
    psum x1, waiting for transfers between devices, on_device(): lax.psum((input_part, output_part, expand_part, reduce_part, gain_one_par...  152 us
    reduce_scatter x1, waiting for transfers between devices, on_device(): lax.psum_scatter(merge_heads(grad_keys), 'seq', scatter_dimension=0, tile...  145 us
    reduce_scatter x1, waiting for transfers between devices, on_device(): lax.psum_scatter(expand_sum, 'dp', scatter_dimension=0, tiled=True)  120 us
    reduce_scatter x1, waiting for transfers between devices, on_device(): lax.psum_scatter(reduce_sum, 'dp', scatter_dimension=0, tiled=True)  120 us
    reduce_scatter x1, waiting for transfers between devices, on_device(): lax.psum_scatter(merge_heads(grad_values), 'seq', scatter_dimension=0, ti...  106 us
    reduce_scatter x1, waiting for transfers between devices, on_device(): lax.psum_scatter(input_sum, 'dp', scatter_dimension=0, tiled=True)  96.2 us
    all_gather x1, waiting for transfers between devices, on_device(): values_all = lax.all_gather(values_local, 'seq', axis=0, tiled=True)  74.9 us
    dot_general x4, matrix products, group_backward(): jnp.einsum('qhd,khd->hqk', grad_out, values_all, preferred_element_type=j...  51.2 us
  transfers between devices with their start and end apart: 13, of which 12 were waited for; matrix products, arithmetic and copies ran while one was open for 12% of the time, Pallas kernels for 0%

commit v1 on v0

v1 whole, which is shorter than its diff:
```python
import functools

import jax
import jax.numpy as jnp
from jax import lax
from jax.experimental import pallas as pl
from jax.experimental.pallas import tpu as pltpu
from jax.sharding import PartitionSpec as P

HEADS = 16
EPS = 1e-05
NEG = -1e30
F32 = jnp.float32
BF = jnp.bfloat16


def _dot(a, b, ca, cb):
    return lax.dot_general(a, b, (((ca,), (cb,)), ((), ())), preferred_element_type=F32)


def mm(a, b):
    return _dot(a, b, 1, 0)


def mm_left(a, b):
    return _dot(a, b, 0, 0)


def mm_right(a, b):
    return _dot(a, b, 1, 1)


def fwd_kernel(st_ref, q_ref, k_ref, v_ref, o_ref, lse_ref, qt_ref, vt_ref, *, bq, bk, scale):
    n = q_ref.shape[0]
    d = q_ref.shape[1] // 2
    qt_ref[...] = jnp.transpose(q_ref[...])
    vt_ref[...] = jnp.transpose(v_ref[...])
    for i in range(n // bq):
        cs = slice(i * bq, (i + 1) * bq)
        st = st_ref[:, cs]
        outs = []
        for h in range(2):
            row = lax.broadcasted_iota(jnp.int32, (2 * d, bq), 0)
            qm = jnp.where((row >= h * d) & (row < (h + 1) * d), qt_ref[:, cs], jnp.zeros((), BF))
            m = jnp.full((1, bq), NEG, F32)
            l = jnp.zeros((1, bq), F32)
            acc = jnp.zeros((d, bq), F32)
            for j in range(0, (i + 1) * bq, bk):
                s = _dot(k_ref[j : j + bk, :], qm, 1, 0) * scale
                key = lax.broadcasted_iota(jnp.int32, (bk, bq), 0) + j
                ok = key >= st
                if j + bk > i * bq:
                    ok = ok & (key <= lax.broadcasted_iota(jnp.int32, (bk, bq), 1) + i * bq)
                s = jnp.where(ok, s, NEG)
                mn = jnp.maximum(m, jnp.max(s, axis=0, keepdims=True))
                p = jnp.exp(s - mn)
                a = jnp.exp(m - mn)
                l = a * l + jnp.sum(p, axis=0, keepdims=True)
                acc = a * acc + _dot(vt_ref[h * d : (h + 1) * d, j : j + bk], p.astype(BF), 1, 0)
                m = mn
            outs.append(acc / l)
            lse_ref[0, h : h + 1, cs] = m + jnp.log(l)
        o_ref[cs, :] = jnp.transpose(jnp.concatenate(outs, axis=0)).astype(BF)


def flash_fwd(starts, qkv, heads, d, bq=512, bk=512):
    n, w, pairs = starts.shape[1], 2 * d, heads // 2
    blk = lambda c: pl.BlockSpec((n, w), lambda p: (0, c + p))
    return pl.pallas_call(
        functools.partial(fwd_kernel, bq=bq, bk=bk, scale=d**-0.5),
        grid=(pairs,),
        in_specs=[pl.BlockSpec((1, n), lambda p: (0, 0)), blk(0), blk(pairs), blk(2 * pairs)],
        out_specs=[blk(0), pl.BlockSpec((1, 2, n), lambda p: (p, 0, 0))],
        out_shape=[
            jax.ShapeDtypeStruct((n, pairs * w), BF),
            jax.ShapeDtypeStruct((pairs, 2, n), F32),
        ],
        scratch_shapes=[pltpu.VMEM((w, n), BF), pltpu.VMEM((w, n), BF)],
        compiler_params=pltpu.CompilerParams(vmem_limit_bytes=48 << 20),
        cost_estimate=pl.CostEstimate(
            flops=8 * n * n * d * heads, bytes_accessed=8 * n * w * pairs, transcendentals=n * n * heads
        ),
    )(starts, qkv, qkv, qkv)


def bwd_kernel(
    st_ref, q_ref, k_ref, v_ref, do_ref, o_ref, lse_ref, dq_ref, dk_ref, dv_ref,
    qm_ref, dom_ref, qt_ref, dot_ref, kt_ref, dqt_ref, delta_ref, *, bq, bk, scale
):
    n, w = q_ref.shape
    d = w // 2
    lane = lax.broadcasted_iota(jnp.int32, (n, w), 1)
    z = jnp.zeros((), BF)
    for h in range(2):
        sel = (lane >= h * d) & (lane < (h + 1) * d)
        qm = jnp.where(sel, q_ref[...], z)
        dom = jnp.where(sel, do_ref[...], z)
        qm_ref[h] = qm
        dom_ref[h] = dom
        qt_ref[h] = jnp.transpose(qm)
        dot_ref[h] = jnp.transpose(dom)
    kt_ref[...] = jnp.transpose(k_ref[...])
    prod = jnp.transpose(do_ref[...].astype(F32) * o_ref[...].astype(F32))
    for h in range(2):
        delta_ref[h : h + 1, :] = jnp.sum(prod[h * d : (h + 1) * d], axis=0, keepdims=True)
    dqt_ref[...] = jnp.zeros_like(dqt_ref)
    for j in range(0, n, bk):
        dk = jnp.zeros((bk, w), F32)
        dv = jnp.zeros((bk, w), F32)
        for i in range(j // bq, n // bq):
            cs = slice(i * bq, (i + 1) * bq)
            st = st_ref[:, cs]
            key = lax.broadcasted_iota(jnp.int32, (bk, bq), 0) + j
            ok = key >= st
            if j + bk > i * bq:
                ok = ok & (key <= lax.broadcasted_iota(jnp.int32, (bk, bq), 1) + i * bq)
            for h in range(2):
                s = _dot(k_ref[j : j + bk, :], qt_ref[h, :, cs], 1, 0) * scale
                s = jnp.where(ok, s, NEG)
                p = jnp.exp(s - lse_ref[0, h : h + 1, cs])
                dp = _dot(v_ref[j : j + bk, :], dot_ref[h, :, cs], 1, 0)
                ds = (p * (dp - delta_ref[h : h + 1, cs])).astype(BF)
                dv = dv + _dot(p.astype(BF), dom_ref[h, cs, :], 1, 0)
                dk = dk + _dot(ds, qm_ref[h, cs, :], 1, 0)
                dqt_ref[h * d : (h + 1) * d, cs] += _dot(kt_ref[h * d : (h + 1) * d, j : j + bk], ds, 1, 0)
        dk_ref[j : j + bk, :] = (dk * scale).astype(BF)
        dv_ref[j : j + bk, :] = dv.astype(BF)
    dq_ref[...] = (jnp.transpose(dqt_ref[...]) * scale).astype(BF)


def flash_bwd(starts, qkv, grad, out, lse, heads, d, bq=256, bk=512):
    n, w, pairs = starts.shape[1], 2 * d, heads // 2
    blk = lambda c: pl.BlockSpec((n, w), lambda p: (0, c + p))
    return pl.pallas_call(
        functools.partial(bwd_kernel, bq=bq, bk=bk, scale=d**-0.5),
        grid=(pairs,),
        in_specs=[
            pl.BlockSpec((1, n), lambda p: (0, 0)), blk(0), blk(pairs), blk(2 * pairs), blk(0), blk(0),
            pl.BlockSpec((1, 2, n), lambda p: (p, 0, 0)),
        ],
        out_specs=[blk(0)] * 3,
        out_shape=[jax.ShapeDtypeStruct((n, pairs * w), BF)] * 3,
        scratch_shapes=[
            pltpu.VMEM((2, n, w), BF), pltpu.VMEM((2, n, w), BF), pltpu.VMEM((2, w, n), BF),
            pltpu.VMEM((2, w, n), BF), pltpu.VMEM((w, n), BF), pltpu.VMEM((w, n), F32), pltpu.VMEM((2, n), F32),
        ],
        compiler_params=pltpu.CompilerParams(vmem_limit_bytes=56 << 20),
        cost_estimate=pl.CostEstimate(
            flops=20 * n * n * d * heads, bytes_accessed=16 * n * w * pairs, transcendentals=n * n * heads
        ),
    )(starts, qkv, qkv, qkv, grad, out, lse)


def layer_normalize(values, gain, shift):
    center = values - jnp.mean(values, axis=-1, keepdims=True)
    spread = jnp.mean(center * center, axis=-1, keepdims=True)
    return center * lax.rsqrt(spread + EPS) * gain + shift


def smooth_gate(values):
    return jax.nn.gelu(values, approximate=True)


def rows(array, start, size):
    return lax.dynamic_slice_in_dim(array, start, size, 0)


def cols(array, start, size):
    return lax.dynamic_slice_in_dim(array, start, size, 1)


def put(array, piece, row, col):
    return lax.dynamic_update_slice(array, piece, (row, col))


def bf_round(x):
    return lax.reduce_precision(x, 8, 7)


class Links:
    def __init__(self, ns, nd):
        self.ns, self.nd = ns, nd

    def go(self, array, target):
        pairs = []
        for s in range(self.ns):
            for d in range(self.nd):
                ts, td = target(s, d)
                pairs.append((s * self.nd + d, ts * self.nd + td))
        return lax.ppermute(array, ("seq", "dp"), pairs)

    def dp(self, array, k):
        return self.go(array, lambda s, d: (s, d ^ k))

    def core(self, array):
        return self.dp(array, 1)

    def near(self, array):
        return self.go(array, lambda s, d: (s ^ 1, d))

    def far(self, array):
        return self.go(array, lambda s, d: (s ^ 2, d))

    def both(self, array):
        return self.go(array, lambda s, d: (s ^ 1, d ^ 1))

    def swap(self, array):
        return self.go(array, lambda s, d: (2 * (d % 2) + s % 2, d - d % 2 + s // 2))


def on_device(
    tokens, lengths, cotangent, mixer_input, mixer_output, expand_weight, reduce_weight,
    first_gain, first_shift, second_gain, second_shift, output_bias, expand_bias, reduce_bias,
):
    ns, nd = lax.axis_size("seq"), lax.axis_size("dp")
    links = Links(ns, nd)
    seq, me = lax.axis_index("seq"), lax.axis_index("dp")
    half, near_bit, core = seq // 2, seq % 2, me % 2
    column = me // 2
    member = 2 * core + near_bit
    n_rows, width = tokens.shape[1:]
    slots = n_rows * ns
    head_dim = width // HEADS
    hidden = reduce_weight.shape[0] * nd
    group = width // 4
    my_heads = HEADS // 4

    x_low = links.swap(tokens[0])
    vectors = jnp.concatenate(
        [first_gain, first_shift, second_gain, second_shift, output_bias, reduce_bias, expand_bias]
    )
    small = width // nd
    vectors = lax.all_gather(vectors.reshape(-1, small), "dp", axis=0).astype(F32)
    gain_one, shift_one, gain_two, shift_two, output_add, reduce_add = (
        vectors[:, i].reshape(-1) for i in range(6)
    )
    expand_add = vectors[:, 6:].reshape(-1)

    def group_columns(array, which):
        return jnp.concatenate([cols(array, i * width + which * group, group) for i in range(3)], axis=1)

    for_even = group_columns(mixer_input, member)
    for_odd = group_columns(mixer_input, member ^ 2)
    small_rows = mixer_input.shape[0]
    input_full = jnp.zeros((width, 3 * group), BF)
    input_full = put(input_full, for_even, me * small_rows, 0)
    for k in range(1, nd):
        piece = links.dp(for_odd if k % 2 else for_even, k)
        input_full = put(input_full, piece, (me ^ k) * small_rows, 0)

    def gather(shard):
        high = shard.shape[0]
        full = jnp.zeros((high * nd, shard.shape[1]), BF)
        for k in range(0, nd, 2):
            piece = links.dp(shard, k) if k else shard
            full = put(full, piece, (me ^ k) * high, 0)
            full = put(full, links.core(piece), (me ^ k ^ 1) * high, 0)
        return full

    output_full = gather(mixer_output)
    expand_full = gather(expand_weight)
    reduce_full = gather(reduce_weight)
    grad_low = links.swap(cotangent[0])
    lengths_row = jnp.where(half == core, lengths[0], links.core(lengths)[0])

    entry = jnp.arange(lengths_row.shape[0])
    ends = jnp.sum(jnp.where(entry[None, :] <= entry[:, None], lengths_row[None, :], 0), axis=1)
    place = jnp.arange(slots, dtype=jnp.int32)
    passed = place[:, None] >= ends[None, :]
    starts = jnp.max(jnp.where(passed, ends[None, :], 0), axis=1)
    starts = jnp.where(place < ends[-1], starts, place).reshape(1, slots)
    live = (member * n_rows + jnp.arange(n_rows, dtype=jnp.int32) < ends[-1]).astype(F32)

    inputs = x_low.astype(F32)
    normed_one = layer_normalize(inputs, gain_one, shift_one).astype(BF)
    near_normed = links.near(normed_one)
    normed_all = jnp.zeros((slots, width), BF)
    normed_all = put(normed_all, normed_one, member * n_rows, 0)
    normed_all = put(normed_all, near_normed, (member ^ 1) * n_rows, 0)
    normed_all = put(normed_all, links.core(normed_one), (member ^ 2) * n_rows, 0)
    normed_all = put(normed_all, links.core(near_normed), (member ^ 3) * n_rows, 0)
    qkv = mm(normed_all, input_full).astype(BF)
    attended, logsum = flash_fwd(starts, qkv, my_heads, head_dim)

    moves = (lambda a: a, links.near, links.core, links.both)
    attention = jnp.zeros((n_rows, width), BF)
    for j in range(4):
        piece = moves[j](rows(attended, (member ^ j) * n_rows, n_rows))
        attention = put(attention, piece, 0, (member ^ j) * group)

    resid = inputs + mm(attention, output_full) + output_add
    normed_two = layer_normalize(resid, gain_two, shift_two).astype(BF)
    expanded = mm(normed_two, expand_full) + expand_add
    active = smooth_gate(expanded).astype(BF)
    result = (resid + mm(active, reduce_full) + reduce_add).astype(BF)
    layer_output = links.swap(result)

    def scatter(parts):
        chip = [parts(k).astype(F32) + links.core(parts(k ^ 1).astype(BF)).astype(F32) for k in range(0, nd, 2)]
        total = chip[0]
        for i in range(1, nd // 2):
            total = total + links.dp(chip[i].astype(BF), 2 * i).astype(F32)
        high = total.shape[0] // 2
        part = rows(total, near_bit * high, high)
        part = part + links.near(rows(total, (1 - near_bit) * high, high).astype(BF)).astype(F32)
        quarter = rows(part, half * (high // 2), high // 2)
        quarter = quarter + links.far(rows(part, (1 - half) * (high // 2), high // 2).astype(BF)).astype(F32)
        quarter = quarter.astype(BF)
        other = links.far(quarter)
        part = jnp.zeros((high, total.shape[1]), BF)
        part = put(part, quarter, half * (high // 2), 0)
        part = put(part, other, (1 - half) * (high // 2), 0)
        other = links.near(part)
        full = jnp.zeros(total.shape, F32)
        full = put(full, part.astype(F32), near_bit * high, 0)
        return put(full, other.astype(F32), (1 - near_bit) * high, 0)

    def scatter_rows(array):
        high = array.shape[0] // nd
        return scatter(lambda k: rows(array, (me ^ k) * high, high))

    grad_result = grad_low.astype(F32) * live[:, None]
    result_low = grad_result.astype(BF)
    reduce_sum = scatter_rows(mm_left(active, result_low).astype(BF))
    reduce_bias_sum = jnp.sum(grad_result, axis=0)
    grad_active = mm_right(result_low, reduce_full)
    _, gate_back = jax.vjp(smooth_gate, expanded)
    grad_expanded = gate_back(grad_active)[0]
    expand_bias_sum = jnp.sum(grad_expanded, axis=0)
    expanded_low = grad_expanded.astype(BF)
    expand_sum = scatter_rows(mm_left(normed_two, expanded_low).astype(BF))
    grad_normed_two = mm_right(expanded_low, expand_full)
    _, second_back = jax.vjp(layer_normalize, resid, gain_two, shift_two)
    resid_part, gain_two_sum, shift_two_sum = second_back(grad_normed_two)
    grad_resid = grad_result + resid_part
    output_bias_sum = jnp.sum(grad_resid, axis=0)
    resid_low = grad_resid.astype(BF)
    output_sum = scatter_rows(mm_left(attention, resid_low).astype(BF))
    grad_attention = mm_right(resid_low, output_full).astype(BF)

    grad_attended = jnp.zeros((slots, group), BF)
    for j in range(4):
        piece = moves[j](cols(grad_attention, (member ^ j) * group, group))
        grad_attended = put(grad_attended, piece, (member ^ j) * n_rows, 0)
    grad_mixed = jnp.concatenate(
        flash_bwd(starts, qkv, grad_attended, attended, logsum, my_heads, head_dim), axis=1
    )

    def normed_grad(j):
        return mm_right(rows(grad_mixed, (member ^ j) * n_rows, n_rows), input_full)

    near_term = normed_grad(1) + links.core(normed_grad(3).astype(BF)).astype(F32)
    near_term = links.near(near_term.astype(BF)).astype(F32)
    grad_normed_one = normed_grad(0) + links.core(normed_grad(2).astype(BF)).astype(F32) + near_term
    _, first_back = jax.vjp(layer_normalize, inputs, gain_one, shift_one)
    inputs_part, gain_one_sum, shift_one_sum = first_back(grad_normed_one)
    tokens_gradient = links.swap((grad_resid + inputs_part).astype(BF)).astype(F32)

    input_term = mm_left(normed_all, grad_mixed)
    pair_rows = 2 * small_rows
    total = rows(input_term, column * pair_rows, pair_rows)
    for i in range(1, nd // 2):
        piece = rows(input_term, (column ^ i) * pair_rows, pair_rows).astype(BF)
        total = total + links.dp(piece, 2 * i).astype(F32)
    total = bf_round(total)
    total = (total + links.far(total.astype(BF)).astype(F32)).astype(BF)
    near_total = links.near(total)
    held = [
        (member, rows(total, core * small_rows, small_rows)),
        (member ^ 1, rows(near_total, core * small_rows, small_rows)),
        (member ^ 2, links.core(rows(total, (1 - core) * small_rows, small_rows))),
        (member ^ 3, links.core(rows(near_total, (1 - core) * small_rows, small_rows))),
    ]
    input_sum = jnp.zeros((small_rows, 3 * width), F32)
    for which, piece in held:
        for i in range(3):
            part = piece[:, i * group : (i + 1) * group].astype(F32)
            input_sum = put(input_sum, part, 0, i * width + which * group)

    sums = jnp.stack([gain_one_sum, shift_one_sum, gain_two_sum, shift_two_sum, output_bias_sum, reduce_bias_sum])
    sums = jnp.concatenate([sums.reshape(-1), expand_bias_sum])
    sums = lax.psum(sums, ("seq", "dp"))
    wide = hidden // nd
    vector_sums = [lax.dynamic_slice(sums, (i * width + me * small,), (small,)) for i in range(6)]
    expand_bias_out = lax.dynamic_slice(sums, (6 * width + me * wide,), (wide,))

    return (
        layer_output[None],
        tokens_gradient[None],
        input_sum,
        output_sum,
        expand_sum,
        reduce_sum,
        vector_sums[0],
        vector_sums[1],
        vector_sums[2],
        vector_sums[3],
        vector_sums[4],
        expand_bias_out,
        vector_sums[5],
    )


def solution(mesh):
    row, vec = P("dp", None), P("dp")
    act = P("dp", "seq", None)
    return jax.shard_map(
        on_device,
        mesh=mesh,
        in_specs=(act, row, act, row, row, row, row, vec, vec, vec, vec, vec, vec, vec),
        out_specs=(act, act, row, row, row, row, vec, vec, vec, vec, vec, vec, vec),
        check_vma=False,
    )
```

time: 1520 us -> 690 us (0.45)
  waiting for transfers between devices: 975 us -> 275 us
  matrix products: 266 us -> 98 us
  starting transfers between devices: 0.65 us -> 98.7 us
  other arithmetic: 98.6 us -> 30.9 us
  Pallas kernels: 0 us -> 60.4 us
  blocking collectives: 102 us -> 54.6 us
    reduce_scatter x6 -> x0, waiting for transfers between devices: 628 us -> none  [the longest x1 145 us: on_device(): lax.psum_scatter(merge_heads(grad_keys), 'seq', scatter_dimension=0, tile...]
    ppermute x0 -> x85, waiting for transfers between devices: none -> 275 us  [go(): return lax.ppermute(array, ('seq', 'dp'), pairs)]
    all_gather x6 -> x0, waiting for transfers between devices: 191 us -> none  [the longest x1 74.9 us: on_device(): values_all = lax.all_gather(values_local, 'seq', axis=0, tiled=True)]
    dot_general x40 -> x15, matrix products: 266 us -> 98 us  [_dot(): lax.dot_general(a, b, (((ca,), (cb,)), ((), ())), preferred_element_type=...]
    psum x1 -> x0, waiting for transfers between devices: 152 us -> none  [on_device(): lax.psum((input_part, output_part, expand_part, reduce_part, gain_one_par...]
    ppermute x0 -> x85, starting transfers between devices: none -> 98.7 us  [go(): return lax.ppermute(array, ('seq', 'dp'), pairs)]
    pallas_call x0 -> x2, Pallas kernels: none -> 60.4 us  [the longest x1 30.6 us: flash_bwd(): pl.pallas_call(functools.partial(bwd_kernel, bq=bq, bk=bk, scale=d ** (-0...]
    all_gather x7 -> x1, blocking collectives: 60.8 us -> 9.03 us  [on_device(): lax.all_gather(vectors.reshape(-1, small), 'dp', axis=0).astype(F32)]
  transfers between devices with their start and end apart: 13 -> 85, of which waited for: 12 -> 32; matrix products, arithmetic and copies ran while one was open for 12% -> 19% of each run, Pallas kernels for 0% -> 9%
where the time goes in v1:
time: 690 us; the launch traced here: 686 us
  waiting for transfers between devices  275 us (40%)
  starting transfers between devices  98.7 us (14%)
  matrix products  98 us (14%)
  local copies, waits for them, and re-layouts  65.6 us (10%)
  Pallas kernels  60.4 us (9%)
  blocking collectives  54.6 us (8%)
  other arithmetic  30.9 us (4%)
    ppermute x85, waiting for transfers between devices, go(): return lax.ppermute(array, ('seq', 'dp'), pairs)  275 us
    ppermute x85, starting transfers between devices, go(): return lax.ppermute(array, ('seq', 'dp'), pairs)  98.7 us
    dot_general x15, matrix products, _dot(): lax.dot_general(a, b, (((ca,), (cb,)), ((), ())), preferred_element_type=...  98 us
    psum x1, blocking collectives, on_device(): sums = lax.psum(sums, ('seq', 'dp'))  45.6 us
    pallas_call x1, Pallas kernels, flash_bwd(): pl.pallas_call(functools.partial(bwd_kernel, bq=bq, bk=bk, scale=d ** (-0...  30.6 us
    pallas_call x1, Pallas kernels, flash_fwd(): pl.pallas_call(functools.partial(fwd_kernel, bq=bq, bk=bk, scale=d ** (-0...  29.8 us
    dynamic_update_slice x43, local copies, waits for them, and re-layouts, put(): return lax.dynamic_update_slice(array, piece, (row, col))  25.4 us
    unnamed x125, local copies, waits for them, and re-layouts  16.8 us
  transfers between devices with their start and end apart: 85, of which 32 were waited for; matrix products, arithmetic and copies ran while one was open for 19% of the time, Pallas kernels for 9%

profile of v1, /device:TPU:0, one launch (start us, length us, event | category | flops | bytes accessed | tf_op | source)
XLA Modules:
  0.0 685.5 jit_solution(17894658636648128277)
XLA Ops:
  2.4 2.6 collective-permute-start.7
  7.0 2.1 collective-permute-start.8
  10.7 9.0 %all_gather.3 = bf16[8,10,128]{2,1,0:T(8,128)(2,1)S(1)} all-gather(bf16[1,10,128]{2,1,0:T(8,128)(2,1)S(1)} %bitcast.69), channel_id=1, replica_groups=mesh['seq'=4,'dp'=8] {'dp'}, dimensions={0}, use_global_device_ids=true | all-gather | bytes 23040 | tf_op jit(solution)/shard_map/all_gather | solution.py:233
  20.3 4.4 broadcast_in_dim.110
  25.7 4.4 broadcast_in_dim.111
  41.2 4.5 collective-permute-start.18
  54.1 3.7 collective-permute-done.18
  58.4 2.5 collective-permute-start.30
  62.6 11.8 %collective-permute-start.21 = (bf16[128,1024]{1,0:T(8,128)(2,1)S(1)}, bf16[128,1024]{1,0:T(8,128)(2,1)S(1)}, u32[]{:S(2)}, u32[]{:S(2)}) collective-permute-start(bf16[128,1024]{1,0:T(8,128)(2,1)S(1)} %collective-permute-done.20), channel_id=1, source_target_pairs={{0,1},{1,0},{2,3},{3,2},{4,5},{5,4},{6,7},{7,6},{8,9},{9,8},{10,11... | collective-permute-start | bytes 786440 | tf_op jit(solution)/shard_map/ppermute | solution.py:190
  78.0 6.9 %collective-permute-done.30 = bf16[512,1024]{1,0:T(8,128)(2,1)S(1)} collective-permute-done((bf16[512,1024]{1,0:T(8,128)(2,1)S(1)}, bf16[512,1024]{1,0:T(8,128)(2,1)S(1)}, u32[]{:S(2)}, u32[]{:S(2)}) %collective-permute-start.30) | collective-permute-done | bytes 1048608 | tf_op jit(solution)/shard_map/ppermute | solution.py:190
  89.5 17.7 %collective-permute-done.23 = bf16[128,4096]{1,0:T(8,128)(2,1)S(1)} collective-permute-done((bf16[128,4096]{1,0:T(8,128)(2,1)S(1)}, bf16[128,4096]{1,0:T(8,128)(2,1)S(1)}, u32[]{:S(2)}, u32[]{:S(2)}) %collective-permute-start.23) | collective-permute-done | bytes 1048608 | tf_op jit(solution)/shard_map/ppermute | solution.py:190
  108.3 2.8 collective-permute-start.34
  116.8 51.9 %collective-permute-done.25 = bf16[128,4096]{1,0:T(8,128)(2,1)S(1)} collective-permute-done((bf16[128,4096]{1,0:T(8,128)(2,1)S(1)}, bf16[128,4096]{1,0:T(8,128)(2,1)S(1)}, u32[]{:S(2)}, u32[]{:S(2)}) %collective-permute-start.25) | collective-permute-done | bytes 1048608 | tf_op jit(solution)/shard_map/ppermute | solution.py:190
  168.7 9.8 %collective-permute-start.37 = (bf16[512,1024]{1,0:T(8,128)(2,1)}, bf16[512,1024]{1,0:T(8,128)(2,1)}, u32[]{:S(2)}, u32[]{:S(2)}) collective-permute-start(bf16[512,1024]{1,0:T(8,128)(2,1)} %bitcast.13), channel_id=1, source_target_pairs={{0,0},{1,16},{2,2},{3,18},{4,4},{5,20},{6,6},{7,22},{8,8},{9,24},{... | collective-permute-start | bytes 3145736 | tf_op jit(solution)/shard_map/ppermute | solution.py:190
  187.3 2.1 copy-done.9
  189.4 5.0 convolution_convert_fusion.2.q_ref.k_ref.v_ref
  194.4 29.8 %shard_map.237 = (bf16[2048,256]{1,0:T(8,128)(2,1)S(1)}, f32[2,2,2048]{2,1,0:T(2,128)S(1)}) custom-call(s32[1,2048]{1,0:T(1,128)S(1)} %compare_select_fusion.st_ref, bf16[2048,768]{1,0:T(8,128)(2,1)S(1)} %convolution_convert_fusion.2.q_ref.k_ref.v_ref, bf16[2048,768]{1,0:T(8,128)(2,1)S(1)} %convolution_convert_fusion.2.q_ref.k_ref.v_ref, ...), custom_call_target="tpu_custom_call" | custom-call | flops 8589934592 | bytes 4194304 | tf_op jit(solution)/shard_map/pallas_call | solution.py:69
  228.8 4.9 collective-permute-done.12
  233.8 3.9 collective-permute-done.14
  239.5 7.2 %fusion.45 = f32[512,4096]{1,0:T(8,128)S(1)} fusion(bf16[1024,4096]{1,0:T(8,128)(2,1)} %constant_dynamic-update-slice_fusion.17, f32[512,1024]{1,0:T(8,128)S(1)} %get-tuple-element.97, f32[1024]{0:T(1024)S(1)} %bitcast.66, f32[1024]{0:T(1024)S(1)} %bitcast.59, f32[512]{0:T(512)S(1)} %fusion.41, f32[512]{0:T(512)S(1)} %broadcast_multiply_fusion), kind=kOutput, calls=%fused_computation.211 | convolution fusion | flops 4297588736 | bytes 18886656 | tf_op jit(solution)/shard_map/dot_general | solution.py:18
  246.7 16.5 %fusion.53 = (f32[4096]{0:T(1024)S(1)}, bf16[512,4096]{1,0:T(8,128)(2,1)}) fusion(f32[512,4096]{1,0:T(8,128)S(1)} %fusion.45, f32[4096]{0:T(1024)S(1)} %bitcast.56, bf16[4096,1024]{1,0:T(8,128)(2,1)} %constant_dynamic-update-slice_fusion.9, bf16[512,1024]{1,0:T(8,128)(2,1)} %collective-permute-done.37, f32[512]{0:T(512)S(1)} %fusion.39), kind=kOutput, calls=%fused_computation.218 | convolution fusion | flops 4342673408 | bytes 22054912 | tf_op jit(solution)/shard_map/dot_general | solution.py:18
  263.2 8.7 %multiply_reduce_fusion = (f32[1024]{0:T(1024)S(1)}, f32[512]{0:T(512)S(1)}, f32[1024]{0:T(1024)S(1)}, f32[512,1024]{1,0:T(8,128)S(1)}) fusion(f32[512,1024]{1,0:T(8,128)S(1)} %get-tuple-element.97, f32[512]{0:T(512)S(1)} %fusion.41, f32[512]{0:T(512)S(1)} %broadcast_multiply_fusion, f32[1024]{0:T(1024)S(1)} %bitcast.60, ...), kind=kOutput, calls=%fused_computation.29 | convolution fusion | flops 4299159040 | bytes 16795648 | tf_op jit(solution)/shard_map/dot_general | solution.py:18
  271.9 7.7 %convolution_convert_fusion.1 = bf16[1024,4096]{1,0:T(8,128)(2,1)S(1)} fusion(bf16[512,4096]{1,0:T(8,128)(2,1)} %get-tuple-element.100, f32[512,1024]{1,0:T(8,128)S(1)} %get-tuple-element.97, f32[1024]{0:T(1024)S(1)} %bitcast.67, f32[1024]{0:T(1024)S(1)} %bitcast.61, f32[512]{0:T(512)S(1)} %fusion.41, f32[512]{0:T(512)S(1)} %broadcast_multiply_fusion), kind=kOutput, calls=%fused_computation.10 | convolution fusion | flops 4301783040 | bytes 14692352 | tf_op jit(solution)/shard_map/dot_general | solution.py:18
  279.6 15.3 %add_convert_fusion.8 = bf16[512,1024]{1,0:T(8,128)(2,1)} fusion(f32[512,1024]{1,0:T(8,128)S(1)} %get-tuple-element.97, bf16[4096,1024]{1,0:T(8,128)(2,1)} %constant_dynamic-update-slice_fusion.9, f32[1024]{0:T(1024)S(1)} %bitcast.65, f32[512,4096]{1,0:T(8,128)} %copy-done.53, f32[4096]{0:T(1024)S(1)} %bitcast.57), kind=kOutput, calls=%fused_computation.49 | convolution fusion | flops 4317511680 | bytes 19943424 | tf_op jit(solution)/shard_map/dot_general | solution.py:18
  296.5 2.6 convolution_convert_fusion.6
  302.2 2.8 convolution_convert_fusion.3
  306.3 13.8 %convolution_convert_fusion = bf16[4096,1024]{1,0:T(8,128)(2,1)} fusion(bf16[512,1024]{1,0:T(8,128)(2,1)} %collective-permute-done.37, f32[512]{0:T(512)S(1)} %fusion.39, f32[512,4096]{1,0:T(8,128)} %copy-done.53, f32[4096]{0:T(1024)S(1)} %bitcast.58), kind=kOutput, calls=%fused_computation.9 | convolution fusion | flops 4321705984 | bytes 17844224 | tf_op jit(solution)/shard_map/dot_general | solution.py:18
  320.1 2.2 constant_dynamic-slice_fusion.7
  322.3 2.7 copy-done.5
  331.9 30.6 %shard_map.238 = (bf16[2048,256]{1,0:T(8,128)(2,1)}, bf16[2048,256]{1,0:T(8,128)(2,1)}, bf16[2048,256]{1,0:T(8,128)(2,1)}) custom-call(s32[1,2048]{1,0:T(1,128)} %copy-done.1, bf16[2048,768]{1,0:T(8,128)(2,1)} %copy-done.2, bf16[2048,768]{1,0:T(8,128)(2,1)} %copy-done.2, bf16[2048,768]{1,0:T(8,128)(2,1)} %copy-done.2, bf16[2048,256]{1,0:T(8,128)(2,1)} %copy-done.30, ...), custom_call_target="tpu_custom_call" | custom-call | flops 21474836480 | bytes 8388608 | tf_op jit(solution)/shard_map/pallas_call | solution.py:134
  366.4 3.7 fusion.54
  370.1 2.4 fusion.26
  376.6 3.5 convolution_convert_fusion.4
  380.2 2.9 collective-permute-done.58
  383.0 4.8 collective-permute-done.56
  394.7 2.5 collective-permute-start.60
  397.3 3.5 convolution_convert_fusion.5
  400.8 2.5 collective-permute-done.47
  403.9 6.2 collective-permute-done.46
  410.1 9.8 %collective-permute-start.36 = (bf16[512,1024]{1,0:T(8,128)(2,1)}, bf16[512,1024]{1,0:T(8,128)(2,1)}, u32[]{:S(2)}, u32[]{:S(2)}) collective-permute-start(bf16[512,1024]{1,0:T(8,128)(2,1)} %add_convert_fusion.8), channel_id=1, source_target_pairs={{0,0},{1,16},{2,2},{3,18},{4,4},{5,20},{6,6},{7,22},{8,8},{9,24},{... | collective-permute-start | bytes 3145736 | tf_op jit(solution)/shard_map/ppermute | solution.py:190
  420.2 22.2 %collective-permute-done.61 = bf16[32,1024]{1,0:T(8,128)(2,1)S(1)} collective-permute-done((bf16[32,1024]{1,0:T(8,128)(2,1)S(1)}, bf16[32,1024]{1,0:T(8,128)(2,1)S(1)}, u32[]{:S(2)}, u32[]{:S(2)}) %collective-permute-start.61) | collective-permute-done | bytes 65568 | tf_op jit(solution)/shard_map/ppermute | solution.py:190
  442.6 4.9 collective-permute-done.62
  450.0 4.7 add_convert_fusion.5
  457.0 4.4 add_convert_fusion.2
  461.4 8.1 %collective-permute-done.48 = bf16[256,768]{1,0:T(8,128)(2,1)S(1)} collective-permute-done((bf16[256,768]{1,0:T(8,128)(2,1)S(1)}, bf16[256,768]{1,0:T(8,128)(2,1)S(1)}, u32[]{:S(2)}, u32[]{:S(2)}) %collective-permute-start.48) | collective-permute-done | bytes 393248 | tf_op jit(solution)/shard_map/ppermute | solution.py:190
  471.4 3.9 add_convert_fusion.7
  475.3 5.7 collective-permute-done.49
  487.7 16.7 %collective-permute-done.67 = bf16[128,4096]{1,0:T(8,128)(2,1)S(1)} collective-permute-done((bf16[128,4096]{1,0:T(8,128)(2,1)S(1)}, bf16[128,4096]{1,0:T(8,128)(2,1)S(1)}, u32[]{:S(2)}, u32[]{:S(2)}) %collective-permute-start.67) | collective-permute-done | bytes 1048608 | tf_op jit(solution)/shard_map/ppermute | solution.py:190
  505.6 4.3 collective-permute-done.65
  510.2 2.3 convert_add_fusion.2
  513.6 19.5 %collective-permute-done.80 = bf16[512,1024]{1,0:T(8,128)(2,1)S(1)} collective-permute-done((bf16[512,1024]{1,0:T(8,128)(2,1)S(1)}, bf16[512,1024]{1,0:T(8,128)(2,1)S(1)}, u32[]{:S(2)}, u32[]{:S(2)}) %collective-permute-start.80) | collective-permute-done | bytes 1048608 | tf_op jit(solution)/shard_map/ppermute | solution.py:190
  533.4 15.9 %collective-permute-done.78 = bf16[512,1024]{1,0:T(8,128)(2,1)S(1)} collective-permute-done((bf16[512,1024]{1,0:T(8,128)(2,1)S(1)}, bf16[512,1024]{1,0:T(8,128)(2,1)S(1)}, u32[]{:S(2)}, u32[]{:S(2)}) %collective-permute-start.78) | collective-permute-done | bytes 1048608 | tf_op jit(solution)/shard_map/ppermute | solution.py:190
  550.3 3.9 collective-permute-done.76
  554.1 2.6 convert_add_fusion.1
  560.1 3.2 fusion.21
  565.4 45.6 %psum.7 = f32[10240]{0:T(1024)S(1)} all-reduce(f32[10240]{0:T(1024)S(1)} %pad_maximum_fusion.2), channel_id=1, replica_groups=mesh['seq'=4,'dp'=8] {'seq','dp'}, use_global_device_ids=true, to_apply=%region_17.18 | all-reduce | flops 10240 | bytes 81920 | tf_op jit(solution)/shard_map/psum | solution.py:382
  614.6 2.2 collective-permute-start.82
  616.8 14.9 %collective-permute-done.71 = bf16[32,4096]{1,0:T(8,128)(2,1)S(1)} collective-permute-done((bf16[32,4096]{1,0:T(8,128)(2,1)S(1)}, bf16[32,4096]{1,0:T(8,128)(2,1)S(1)}, u32[]{:S(2)}, u32[]{:S(2)}) %collective-permute-start.71) | collective-permute-done | bytes 262176 | tf_op jit(solution)/shard_map/ppermute | solution.py:190
  633.2 9.8 %collective-permute-done.82 = bf16[128,1024]{1,0:T(8,128)(2,1)S(1)} collective-permute-done((bf16[128,1024]{1,0:T(8,128)(2,1)S(1)}, bf16[128,1024]{1,0:T(8,128)(2,1)S(1)}, u32[]{:S(2)}, u32[]{:S(2)}) %collective-permute-start.82) | collective-permute-done | bytes 262176 | tf_op jit(solution)/shard_map/ppermute | solution.py:190
  643.2 11.0 %collective-permute-done.72 = bf16[32,4096]{1,0:T(8,128)(2,1)S(1)} collective-permute-done((bf16[32,4096]{1,0:T(8,128)(2,1)S(1)}, bf16[32,4096]{1,0:T(8,128)(2,1)S(1)}, u32[]{:S(2)}, u32[]{:S(2)}) %collective-permute-start.72) | collective-permute-done | bytes 262176 | tf_op jit(solution)/shard_map/ppermute | solution.py:190
  654.3 5.5 collective-permute-done.83
  662.2 8.9 %collective-permute-done.73 = bf16[64,4096]{1,0:T(8,128)(2,1)S(1)} collective-permute-done((bf16[64,4096]{1,0:T(8,128)(2,1)S(1)}, bf16[64,4096]{1,0:T(8,128)(2,1)S(1)}, u32[]{:S(2)}, u32[]{:S(2)}) %collective-permute-start.73) | collective-permute-done | bytes 524320 | tf_op jit(solution)/shard_map/ppermute | solution.py:190
  671.1 11.1 %collective-permute-done.84 = bf16[256,1024]{1,0:T(8,128)(2,1)S(1)} collective-permute-done((bf16[256,1024]{1,0:T(8,128)(2,1)S(1)}, bf16[256,1024]{1,0:T(8,128)(2,1)S(1)}, u32[]{:S(2)}, u32[]{:S(2)}) %collective-permute-start.84) | collective-permute-done | bytes 524320 | tf_op jit(solution)/shard_map/ppermute | solution.py:190
  682.3 3.0 copy.105
  (391 shorter events, 116.7 us)
Async XLA Ops:
  1.9 32.2 %collective-permute-start.5 = (bf16[128,768]{1,0:T(8,128)(2,1)S(1)}, bf16[128,768]{1,0:T(8,128)(2,1)S(1)}, u32[]{:S(2)}, u32[]{:S(2)}) collective-permute-start(bf16[128,768]{1,0:T(8,128)(2,1)S(1)} %pad_maximum_fusion.1), channel_id=1, source_target_pairs={{0,1},{1,0},{2,3},{3,2},{4,5},{5,4},{6,7},{7,6},{8,9},{9,8},{10,11... | collective-permute-start | bytes 589832 | tf_op jit(solution)/shard_map/ppermute | solution.py:190
  2.4 35.6 %collective-permute-start.7 = (bf16[128,768]{1,0:T(8,128)(2,1)S(1)}, bf16[128,768]{1,0:T(8,128)(2,1)S(1)}, u32[]{:S(2)}, u32[]{:S(2)}) collective-permute-start(bf16[128,768]{1,0:T(8,128)(2,1)S(1)} %pad_maximum_fusion.1), channel_id=1, source_target_pairs={{0,3},{1,2},{2,1},{3,0},{4,7},{5,6},{6,5},{7,4},{8,11},{9,10},{10,... | collective-permute-start | bytes 589832 | tf_op jit(solution)/shard_map/ppermute | solution.py:190
  7.0 29.0 %collective-permute-start.6 = (bf16[128,768]{1,0:T(8,128)(2,1)}, bf16[128,768]{1,0:T(8,128)(2,1)S(1)}, u32[]{:S(2)}, u32[]{:S(2)}) collective-permute-start(bf16[128,768]{1,0:T(8,128)(2,1)} %get-tuple-element.82), channel_id=1, source_target_pairs={{0,2},{1,3},{2,0},{3,1},{4,6},{5,7},{6,4},{7,5},{8,10},{9,11},{10,... | collective-permute-start | bytes 589832 | tf_op jit(solution)/shard_map/ppermute | solution.py:190
  7.0 32.3 %collective-permute-start.8 = (bf16[128,768]{1,0:T(8,128)(2,1)}, bf16[128,768]{1,0:T(8,128)(2,1)S(1)}, u32[]{:S(2)}, u32[]{:S(2)}) collective-permute-start(bf16[128,768]{1,0:T(8,128)(2,1)} %get-tuple-element.82), channel_id=1, source_target_pairs={{0,4},{1,5},{2,6},{3,7},{4,0},{5,1},{6,2},{7,3},{8,12},{9,13},{10,... | collective-permute-start | bytes 589832 | tf_op jit(solution)/shard_map/ppermute | solution.py:190
  9.1 22.1 %collective-permute-start.1 = (s32[1,4]{1,0:T(1,128)S(1)}, s32[1,4]{1,0:T(1,128)S(1)}, u32[]{:S(2)}, u32[]{:S(2)}) collective-permute-start(s32[1,4]{1,0:T(1,128)S(1)} %copy-done.51), channel_id=1, source_target_pairs={{0,1},{1,0},{2,3},{3,2},{4,5},{5,4},{6,7},{7,6},{8,9},{9,8},{10,11... | collective-permute-start | bytes 56 | tf_op jit(solution)/shard_map/ppermute | solution.py:190
  36.1 11.8 %collective-permute-start.11 = (bf16[128,768]{1,0:T(8,128)(2,1)S(1)}, bf16[128,768]{1,0:T(8,128)(2,1)S(1)}, u32[]{:S(2)}, u32[]{:S(2)}) collective-permute-start(bf16[128,768]{1,0:T(8,128)(2,1)S(1)} %pad_maximum_fusion.1), channel_id=1, source_target_pairs={{0,7},{1,6},{2,5},{3,4},{4,3},{5,2},{6,1},{7,0},{8,15},{9,14},{10,... | collective-permute-start | bytes 589832 | tf_op jit(solution)/shard_map/ppermute | solution.py:190
  38.0 16.1 %collective-permute-start.15 = (bf16[128,1024]{1,0:T(8,128)(2,1)S(1)}, bf16[128,1024]{1,0:T(8,128)(2,1)S(1)}, u32[]{:S(2)}, u32[]{:S(2)}) collective-permute-start(bf16[128,1024]{1,0:T(8,128)(2,1)S(1)} %copy-done.35), channel_id=1, source_target_pairs={{0,1},{1,0},{2,3},{3,2},{4,5},{5,4},{6,7},{7,6},{8,9},{9,8},{10,11... | collective-permute-start | bytes 786440 | tf_op jit(solution)/shard_map/ppermute | solution.py:190
  39.3 12.5 %collective-permute-start.16 = (bf16[128,1024]{1,0:T(8,128)(2,1)S(1)}, bf16[128,1024]{1,0:T(8,128)(2,1)S(1)}, u32[]{:S(2)}, u32[]{:S(2)}) collective-permute-start(bf16[128,1024]{1,0:T(8,128)(2,1)S(1)} %copy-done.35), channel_id=1, source_target_pairs={{0,2},{1,3},{2,0},{3,1},{4,6},{5,7},{6,4},{7,5},{8,10},{9,11},{10,... | collective-permute-start | bytes 786440 | tf_op jit(solution)/shard_map/ppermute | solution.py:190
  41.2 16.6 %collective-permute-start.18 = (bf16[128,1024]{1,0:T(8,128)(2,1)S(1)}, bf16[128,1024]{1,0:T(8,128)(2,1)S(1)}, u32[]{:S(2)}, u32[]{:S(2)}) collective-permute-start(bf16[128,1024]{1,0:T(8,128)(2,1)S(1)} %copy-done.35), channel_id=1, source_target_pairs={{0,4},{1,5},{2,6},{3,7},{4,0},{5,1},{6,2},{7,3},{8,12},{9,13},{10,... | collective-permute-start | bytes 786440 | tf_op jit(solution)/shard_map/ppermute | solution.py:190
  45.8 16.8 %collective-permute-start = (bf16[512,1024]{1,0:T(8,128)(2,1)S(1)}, bf16[512,1024]{1,0:T(8,128)(2,1)S(1)}, u32[]{:S(2)}, u32[]{:S(2)}) collective-permute-start(bf16[512,1024]{1,0:T(8,128)(2,1)S(1)} %bitcast.70), channel_id=1, source_target_pairs={{0,0},{1,16},{2,2},{3,18},{4,4},{5,20},{6,6},{7,22},{8,8},{9,24},{... | collective-permute-start | bytes 3145736 | tf_op jit(solution)/shard_map/ppermute | solution.py:190
  47.9 13.4 %collective-permute-start.20 = (bf16[128,1024]{1,0:T(8,128)(2,1)S(1)}, bf16[128,1024]{1,0:T(8,128)(2,1)S(1)}, u32[]{:S(2)}, u32[]{:S(2)}) collective-permute-start(bf16[128,1024]{1,0:T(8,128)(2,1)S(1)} %copy-done.35), channel_id=1, source_target_pairs={{0,6},{1,7},{2,4},{3,5},{4,2},{5,3},{6,0},{7,1},{8,14},{9,15},{10,... | collective-permute-start | bytes 786440 | tf_op jit(solution)/shard_map/ppermute | solution.py:190
  54.1 33.6 %collective-permute-start.29 = (bf16[512,1024]{1,0:T(8,128)(2,1)S(1)}, bf16[512,1024]{1,0:T(8,128)(2,1)S(1)}, u32[]{:S(2)}, u32[]{:S(2)}) collective-permute-start(bf16[512,1024]{1,0:T(8,128)(2,1)S(1)} %copy-done.26), channel_id=1, source_target_pairs={{0,1},{1,0},{2,3},{3,2},{4,5},{5,4},{6,7},{7,6},{8,9},{9,8},{10,11... | collective-permute-start | bytes 3145736 | tf_op jit(solution)/shard_map/ppermute | solution.py:190
  58.4 26.5 %collective-permute-start.30 = (bf16[512,1024]{1,0:T(8,128)(2,1)S(1)}, bf16[512,1024]{1,0:T(8,128)(2,1)S(1)}, u32[]{:S(2)}, u32[]{:S(2)}) collective-permute-start(bf16[512,1024]{1,0:T(8,128)(2,1)S(1)} %copy-done.26), channel_id=1, source_target_pairs={{0,2},{1,3},{2,0},{3,1},{4,6},{5,7},{6,4},{7,5},{8,10},{9,11},{10,... | collective-permute-start | bytes 3145736 | tf_op jit(solution)/shard_map/ppermute | solution.py:190
  61.0 25.5 %collective-permute-start.22 = (bf16[128,4096]{1,0:T(8,128)(2,1)S(1)}, bf16[128,4096]{1,0:T(8,128)(2,1)S(1)}, u32[]{:S(2)}, u32[]{:S(2)}) collective-permute-start(bf16[128,4096]{1,0:T(8,128)(2,1)S(1)} %copy-done.28), channel_id=1, source_target_pairs={{0,1},{1,0},{2,3},{3,2},{4,5},{5,4},{6,7},{7,6},{8,9},{9,8},{10,11... | collective-permute-start | bytes 3145736 | tf_op jit(solution)/shard_map/ppermute | solution.py:190
  61.3 45.9 %collective-permute-start.23 = (bf16[128,4096]{1,0:T(8,128)(2,1)S(1)}, bf16[128,4096]{1,0:T(8,128)(2,1)S(1)}, u32[]{:S(2)}, u32[]{:S(2)}) collective-permute-start(bf16[128,4096]{1,0:T(8,128)(2,1)S(1)} %copy-done.28), channel_id=1, source_target_pairs={{0,2},{1,3},{2,0},{3,1},{4,6},{5,7},{6,4},{7,5},{8,10},{9,11},{10,... | collective-permute-start | bytes 3145736 | tf_op jit(solution)/shard_map/ppermute | solution.py:190
  62.6 13.6 %collective-permute-start.21 = (bf16[128,1024]{1,0:T(8,128)(2,1)S(1)}, bf16[128,1024]{1,0:T(8,128)(2,1)S(1)}, u32[]{:S(2)}, u32[]{:S(2)}) collective-permute-start(bf16[128,1024]{1,0:T(8,128)(2,1)S(1)} %collective-permute-done.20), channel_id=1, source_target_pairs={{0,1},{1,0},{2,3},{3,2},{4,5},{5,4},{6,7},{7,6},{8,9},{9,8},{10,11... | collective-permute-start | bytes 786440 | tf_op jit(solution)/shard_map/ppermute | solution.py:190
  76.2 32.2 %collective-permute-start.32 = (bf16[512,1024]{1,0:T(8,128)(2,1)S(1)}, bf16[512,1024]{1,0:T(8,128)(2,1)S(1)}, u32[]{:S(2)}, u32[]{:S(2)}) collective-permute-start(bf16[512,1024]{1,0:T(8,128)(2,1)S(1)} %copy-done.26), channel_id=1, source_target_pairs={{0,4},{1,5},{2,6},{3,7},{4,0},{5,1},{6,2},{7,3},{8,12},{9,13},{10,... | collective-permute-start | bytes 3145736 | tf_op jit(solution)/shard_map/ppermute | solution.py:190
  84.9 26.3 %collective-permute-start.2 = (bf16[512,1024]{1,0:T(8,128)(2,1)S(1)}, bf16[512,1024]{1,0:T(8,128)(2,1)S(1)}, u32[]{:S(2)}, u32[]{:S(2)}) collective-permute-start(bf16[512,1024]{1,0:T(8,128)(2,1)S(1)} %get-tuple-element.42), channel_id=1, source_target_pairs={{0,8},{1,9},{2,10},{3,11},{4,12},{5,13},{6,14},{7,15},{8,0},{9,1},... | collective-permute-start | bytes 3145736 | tf_op jit(solution)/shard_map/ppermute | solution.py:190
  86.5 26.0 %collective-permute-start.31 = (bf16[512,1024]{1,0:T(8,128)(2,1)S(1)}, bf16[512,1024]{1,0:T(8,128)(2,1)S(1)}, u32[]{:S(2)}, u32[]{:S(2)}) collective-permute-start(bf16[512,1024]{1,0:T(8,128)(2,1)S(1)} %collective-permute-done.30), channel_id=1, source_target_pairs={{0,1},{1,0},{2,3},{3,2},{4,5},{5,4},{6,7},{7,6},{8,9},{9,8},{10,11... | collective-permute-start | bytes 3145736 | tf_op jit(solution)/shard_map/ppermute | solution.py:190
  87.7 81.0 %collective-permute-start.25 = (bf16[128,4096]{1,0:T(8,128)(2,1)S(1)}, bf16[128,4096]{1,0:T(8,128)(2,1)S(1)}, u32[]{:S(2)}, u32[]{:S(2)}) collective-permute-start(bf16[128,4096]{1,0:T(8,128)(2,1)S(1)} %copy-done.28), channel_id=1, source_target_pairs={{0,4},{1,5},{2,6},{3,7},{4,0},{5,1},{6,2},{7,3},{8,12},{9,13},{10,... | collective-permute-start | bytes 3145736 | tf_op jit(solution)/shard_map/ppermute | solution.py:190
  107.2 71.3 %collective-permute-start.24 = (bf16[128,4096]{1,0:T(8,128)(2,1)S(1)}, bf16[128,4096]{1,0:T(8,128)(2,1)S(1)}, u32[]{:S(2)}, u32[]{:S(2)}) collective-permute-start(bf16[128,4096]{1,0:T(8,128)(2,1)S(1)} %collective-permute-done.23), channel_id=1, source_target_pairs={{0,1},{1,0},{2,3},{3,2},{4,5},{5,4},{6,7},{7,6},{8,9},{9,8},{10,11... | collective-permute-start | bytes 3145736 | tf_op jit(solution)/shard_map/ppermute | solution.py:190
  108.3 71.3 %collective-permute-start.34 = (bf16[512,1024]{1,0:T(8,128)(2,1)S(1)}, bf16[512,1024]{1,0:T(8,128)(2,1)S(1)}, u32[]{:S(2)}, u32[]{:S(2)}) collective-permute-start(bf16[512,1024]{1,0:T(8,128)(2,1)S(1)} %copy-done.26), channel_id=1, source_target_pairs={{0,6},{1,7},{2,4},{3,5},{4,2},{5,3},{6,0},{7,1},{8,14},{9,15},{10,... | collective-permute-start | bytes 3145736 | tf_op jit(solution)/shard_map/ppermute | solution.py:190
  111.2 69.0 %collective-permute-start.27 = (bf16[128,4096]{1,0:T(8,128)(2,1)S(1)}, bf16[128,4096]{1,0:T(8,128)(2,1)S(1)}, u32[]{:S(2)}, u32[]{:S(2)}) collective-permute-start(bf16[128,4096]{1,0:T(8,128)(2,1)S(1)} %copy-done.28), channel_id=1, source_target_pairs={{0,6},{1,7},{2,4},{3,5},{4,2},{5,3},{6,0},{7,1},{8,14},{9,15},{10,... | collective-permute-start | bytes 3145736 | tf_op jit(solution)/shard_map/ppermute | solution.py:190
  112.4 67.8 %collective-permute-start.3 = (bf16[512,1024]{1,0:T(8,128)(2,1)S(1)}, bf16[512,1024]{1,0:T(8,128)(2,1)S(1)}, u32[]{:S(2)}, u32[]{:S(2)}) collective-permute-start(bf16[512,1024]{1,0:T(8,128)(2,1)S(1)} %get-tuple-element.42), channel_id=1, source_target_pairs={{0,1},{1,0},{2,3},{3,2},{4,5},{5,4},{6,7},{7,6},{8,9},{9,8},{10,11... | collective-permute-start | bytes 3145736 | tf_op jit(solution)/shard_map/ppermute | solution.py:190
  168.7 78.0 %collective-permute-start.37 = (bf16[512,1024]{1,0:T(8,128)(2,1)}, bf16[512,1024]{1,0:T(8,128)(2,1)}, u32[]{:S(2)}, u32[]{:S(2)}) collective-permute-start(bf16[512,1024]{1,0:T(8,128)(2,1)} %bitcast.13), channel_id=1, source_target_pairs={{0,0},{1,16},{2,2},{3,18},{4,4},{5,20},{6,6},{7,22},{8,8},{9,24},{... | collective-permute-start | bytes 3145736 | tf_op jit(solution)/shard_map/ppermute | solution.py:190
  180.2 47.6 %collective-permute-start.35 = (bf16[512,1024]{1,0:T(8,128)(2,1)S(1)}, bf16[512,1024]{1,0:T(8,128)(2,1)S(1)}, u32[]{:S(2)}, u32[]{:S(2)}) collective-permute-start(bf16[512,1024]{1,0:T(8,128)(2,1)S(1)} %collective-permute-done.34), channel_id=1, source_target_pairs={{0,1},{1,0},{2,3},{3,2},{4,5},{5,4},{6,7},{7,6},{8,9},{9,8},{10,11... | collective-permute-start | bytes 3145736 | tf_op jit(solution)/shard_map/ppermute | solution.py:190
  226.0 11.7 %collective-permute-start.14 = (bf16[512,256]{1,0:T(8,128)(2,1)S(1)}, bf16[512,256]{1,0:T(8,128)(2,1)S(1)}, u32[]{:S(2)}, u32[]{:S(2)}) collective-permute-start(bf16[512,256]{1,0:T(8,128)(2,1)S(1)} %get-tuple-element.72), channel_id=1, source_target_pairs={{0,9},{1,8},{2,11},{3,10},{4,13},{5,12},{6,15},{7,14},{8,1},{9,0},... | collective-permute-start | bytes 786440 | tf_op jit(solution)/shard_map/ppermute | solution.py:190
  300.1 26.9 %collective-permute-start.38 = (bf16[512,256]{1,0:T(8,128)(2,1)}, bf16[512,256]{1,0:T(8,128)(2,1)}, u32[]{:S(2)}, u32[]{:S(2)}) collective-permute-start(bf16[512,256]{1,0:T(8,128)(2,1)} %get-tuple-element.70), channel_id=1, source_target_pairs={{0,8},{1,9},{2,10},{3,11},{4,12},{5,13},{6,14},{7,15},{8,0},{9,1},... | collective-permute-start | bytes 786440 | tf_op jit(solution)/shard_map/ppermute | solution.py:190
  300.5 27.9 %collective-permute-start.39 = (bf16[512,256]{1,0:T(8,128)(2,1)}, bf16[512,256]{1,0:T(8,128)(2,1)}, u32[]{:S(2)}, u32[]{:S(2)}) collective-permute-start(bf16[512,256]{1,0:T(8,128)(2,1)} %get-tuple-element.69), channel_id=1, source_target_pairs={{0,1},{1,0},{2,3},{3,2},{4,5},{5,4},{6,7},{7,6},{8,9},{9,8},{10,11... | collective-permute-start | bytes 786440 | tf_op jit(solution)/shard_map/ppermute | solution.py:190
  300.8 28.8 %collective-permute-start.40 = (bf16[512,256]{1,0:T(8,128)(2,1)}, bf16[512,256]{1,0:T(8,128)(2,1)}, u32[]{:S(2)}, u32[]{:S(2)}) collective-permute-start(bf16[512,256]{1,0:T(8,128)(2,1)} %get-tuple-element.68), channel_id=1, source_target_pairs={{0,9},{1,8},{2,11},{3,10},{4,13},{5,12},{6,15},{7,14},{8,1},{9,0},... | collective-permute-start | bytes 786440 | tf_op jit(solution)/shard_map/ppermute | solution.py:190
  305.8 66.8 %collective-permute-start.53 = (bf16[128,1024]{1,0:T(8,128)(2,1)}, bf16[128,1024]{1,0:T(8,128)(2,1)S(1)}, u32[]{:S(2)}, u32[]{:S(2)}) collective-permute-start(bf16[128,1024]{1,0:T(8,128)(2,1)} %get-tuple-element.64), channel_id=1, source_target_pairs={{0,1},{1,0},{2,3},{3,2},{4,5},{5,4},{6,7},{7,6},{8,9},{9,8},{10,11... | collective-permute-start | bytes 786440 | tf_op jit(solution)/shard_map/ppermute | solution.py:190
  306.2 66.4 %collective-permute-start.57 = (bf16[128,1024]{1,0:T(8,128)(2,1)S(1)}, bf16[128,1024]{1,0:T(8,128)(2,1)S(1)}, u32[]{:S(2)}, u32[]{:S(2)}) collective-permute-start(bf16[128,1024]{1,0:T(8,128)(2,1)S(1)} %get-tuple-element.62), channel_id=1, source_target_pairs={{0,1},{1,0},{2,3},{3,2},{4,5},{5,4},{6,7},{7,6},{8,9},{9,8},{10,11... | collective-permute-start | bytes 786440 | tf_op jit(solution)/shard_map/ppermute | solution.py:190
  327.0 45.5 %collective-permute-start.55 = (bf16[128,1024]{1,0:T(8,128)(2,1)S(1)}, bf16[128,1024]{1,0:T(8,128)(2,1)S(1)}, u32[]{:S(2)}, u32[]{:S(2)}) collective-permute-start(bf16[128,1024]{1,0:T(8,128)(2,1)S(1)} %get-tuple-element.63), channel_id=1, source_target_pairs={{0,1},{1,0},{2,3},{3,2},{4,5},{5,4},{6,7},{7,6},{8,9},{9,8},{10,11... | collective-permute-start | bytes 786440 | tf_op jit(solution)/shard_map/ppermute | solution.py:190
  328.4 51.8 %collective-permute-start.52 = (bf16[128,1024]{1,0:T(8,128)(2,1)S(1)}, bf16[128,1024]{1,0:T(8,128)(2,1)}, u32[]{:S(2)}, u32[]{:S(2)}) collective-permute-start(bf16[128,1024]{1,0:T(8,128)(2,1)S(1)} %get-tuple-element.61), channel_id=1, source_target_pairs={{0,1},{1,0},{2,3},{3,2},{4,5},{5,4},{6,7},{7,6},{8,9},{9,8},{10,11... | collective-permute-start | bytes 786440 | tf_op jit(solution)/shard_map/ppermute | solution.py:190
  329.6 117.9 %collective-permute-start.64 = (bf16[128,4096]{1,0:T(8,128)(2,1)}, bf16[128,4096]{1,0:T(8,128)(2,1)}, u32[]{:S(2)}, u32[]{:S(2)}) collective-permute-start(bf16[128,4096]{1,0:T(8,128)(2,1)} %get-tuple-element.53), channel_id=1, source_target_pairs={{0,1},{1,0},{2,3},{3,2},{4,5},{5,4},{6,7},{7,6},{8,9},{9,8},{10,11... | collective-permute-start | bytes 3145736 | tf_op jit(solution)/shard_map/ppermute | solution.py:190
  374.9 12.9 %collective-permute-start.56 = (bf16[128,1024]{1,0:T(8,128)(2,1)S(1)}, bf16[128,1024]{1,0:T(8,128)(2,1)S(1)}, u32[]{:S(2)}, u32[]{:S(2)}) collective-permute-start(bf16[128,1024]{1,0:T(8,128)(2,1)S(1)} %get-tuple-element.67), channel_id=1, source_target_pairs={{0,4},{1,5},{2,6},{3,7},{4,0},{5,1},{6,2},{7,3},{8,12},{9,13},{10,... | collective-permute-start | bytes 786440 | tf_op jit(solution)/shard_map/ppermute | solution.py:190
  390.3 13.1 %collective-permute-start.47 = (bf16[256,768]{1,0:T(8,128)(2,1)S(1)}, bf16[256,768]{1,0:T(8,128)(2,1)S(1)}, u32[]{:S(2)}, u32[]{:S(2)}) collective-permute-start(bf16[256,768]{1,0:T(8,128)(2,1)S(1)} %get-tuple-element.59), channel_id=1, source_target_pairs={{0,6},{1,7},{2,4},{3,5},{4,2},{5,3},{6,0},{7,1},{8,14},{9,15},{10,... | collective-permute-start | bytes 1179656 | tf_op jit(solution)/shard_map/ppermute | solution.py:190
  392.2 17.9 %collective-permute-start.46 = (bf16[256,768]{1,0:T(8,128)(2,1)S(1)}, bf16[256,768]{1,0:T(8,128)(2,1)S(1)}, u32[]{:S(2)}, u32[]{:S(2)}) collective-permute-start(bf16[256,768]{1,0:T(8,128)(2,1)S(1)} %get-tuple-element.60), channel_id=1, source_target_pairs={{0,4},{1,5},{2,6},{3,7},{4,0},{5,1},{6,2},{7,3},{8,12},{9,13},{10,... | collective-permute-start | bytes 1179656 | tf_op jit(solution)/shard_map/ppermute | solution.py:190
  393.5 26.4 %collective-permute-start.45 = (bf16[256,768]{1,0:T(8,128)(2,1)S(1)}, bf16[256,768]{1,0:T(8,128)(2,1)S(1)}, u32[]{:S(2)}, u32[]{:S(2)}) collective-permute-start(bf16[256,768]{1,0:T(8,128)(2,1)S(1)} %get-tuple-element.58), channel_id=1, source_target_pairs={{0,2},{1,3},{2,0},{3,1},{4,6},{5,7},{6,4},{7,5},{8,10},{9,11},{10,... | collective-permute-start | bytes 1179656 | tf_op jit(solution)/shard_map/ppermute | solution.py:190
  403.3 44.8 %collective-permute-start.68 = (bf16[128,4096]{1,0:T(8,128)(2,1)S(1)}, bf16[128,4096]{1,0:T(8,128)(2,1)}, u32[]{:S(2)}, u32[]{:S(2)}) collective-permute-start(bf16[128,4096]{1,0:T(8,128)(2,1)S(1)} %copy-done.22), channel_id=1, source_target_pairs={{0,1},{1,0},{2,3},{3,2},{4,5},{5,4},{6,7},{7,6},{8,9},{9,8},{10,11... | collective-permute-start | bytes 3145736 | tf_op jit(solution)/shard_map/ppermute | solution.py:190
  403.4 44.9 %collective-permute-start.66 = (bf16[128,4096]{1,0:T(8,128)(2,1)S(1)}, bf16[128,4096]{1,0:T(8,128)(2,1)S(1)}, u32[]{:S(2)}, u32[]{:S(2)}) collective-permute-start(bf16[128,4096]{1,0:T(8,128)(2,1)S(1)} %copy-done.21), channel_id=1, source_target_pairs={{0,1},{1,0},{2,3},{3,2},{4,5},{5,4},{6,7},{7,6},{8,9},{9,8},{10,11... | collective-permute-start | bytes 3145736 | tf_op jit(solution)/shard_map/ppermute | solution.py:190
  410.1 44.6 %collective-permute-start.36 = (bf16[512,1024]{1,0:T(8,128)(2,1)}, bf16[512,1024]{1,0:T(8,128)(2,1)}, u32[]{:S(2)}, u32[]{:S(2)}) collective-permute-start(bf16[512,1024]{1,0:T(8,128)(2,1)} %add_convert_fusion.8), channel_id=1, source_target_pairs={{0,0},{1,16},{2,2},{3,18},{4,4},{5,20},{6,6},{7,22},{8,8},{9,24},{... | collective-permute-start | bytes 3145736 | tf_op jit(solution)/shard_map/ppermute | solution.py:190
  419.9 22.5 %collective-permute-start.61 = (bf16[32,1024]{1,0:T(8,128)(2,1)S(1)}, bf16[32,1024]{1,0:T(8,128)(2,1)S(1)}, u32[]{:S(2)}, u32[]{:S(2)}) collective-permute-start(bf16[32,1024]{1,0:T(8,128)(2,1)S(1)} %get-tuple-element.37), channel_id=1, source_target_pairs={{0,16},{1,17},{2,18},{3,19},{4,20},{5,21},{6,22},{7,23},{8,24},{9,... | collective-permute-start | bytes 196616 | tf_op jit(solution)/shard_map/ppermute | solution.py:190
  449.2 20.3 %collective-permute-start.48 = (bf16[256,768]{1,0:T(8,128)(2,1)S(1)}, bf16[256,768]{1,0:T(8,128)(2,1)S(1)}, u32[]{:S(2)}, u32[]{:S(2)}) collective-permute-start(bf16[256,768]{1,0:T(8,128)(2,1)S(1)} %fusion.43), channel_id=1, source_target_pairs={{0,16},{1,17},{2,18},{3,19},{4,20},{5,21},{6,22},{7,23},{8,24},{9,... | collective-permute-start | bytes 1179656 | tf_op jit(solution)/shard_map/ppermute | solution.py:190
  454.7 30.6 %collective-permute-start.63 = (bf16[128,4096]{1,0:T(8,128)(2,1)S(1)}, bf16[128,4096]{1,0:T(8,128)(2,1)}, u32[]{:S(2)}, u32[]{:S(2)}) collective-permute-start(bf16[128,4096]{1,0:T(8,128)(2,1)S(1)} %copy-done.16), channel_id=1, source_target_pairs={{0,1},{1,0},{2,3},{3,2},{4,5},{5,4},{6,7},{7,6},{8,9},{9,8},{10,11... | collective-permute-start | bytes 3145736 | tf_op jit(solution)/shard_map/ppermute | solution.py:190
  454.8 30.6 %collective-permute-start.74 = (bf16[512,1024]{1,0:T(8,128)(2,1)S(1)}, bf16[512,1024]{1,0:T(8,128)(2,1)}, u32[]{:S(2)}, u32[]{:S(2)}) collective-permute-start(bf16[512,1024]{1,0:T(8,128)(2,1)S(1)} %copy-done.17), channel_id=1, source_target_pairs={{0,1},{1,0},{2,3},{3,2},{4,5},{5,4},{6,7},{7,6},{8,9},{9,8},{10,11... | collective-permute-start | bytes 3145736 | tf_op jit(solution)/shard_map/ppermute | solution.py:190
  455.2 14.9 %collective-permute-start.42 = (bf16[512,1024]{1,0:T(8,128)(2,1)}, bf16[512,1024]{1,0:T(8,128)(2,1)}, u32[]{:S(2)}, u32[]{:S(2)}) collective-permute-start(bf16[512,1024]{1,0:T(8,128)(2,1)} %convolution_convert_fusion.4), channel_id=1, source_target_pairs={{0,1},{1,0},{2,3},{3,2},{4,5},{5,4},{6,7},{7,6},{8,9},{9,8},{10,11... | collective-permute-start | bytes 3145736 | tf_op jit(solution)/shard_map/ppermute | solution.py:190
  455.3 31.6 %collective-permute-start.69 = (bf16[128,4096]{1,0:T(8,128)(2,1)}, bf16[128,4096]{1,0:T(8,128)(2,1)}, u32[]{:S(2)}, u32[]{:S(2)}) collective-permute-start(bf16[128,4096]{1,0:T(8,128)(2,1)} %get-tuple-element.55), channel_id=1, source_target_pairs={{0,6},{1,7},{2,4},{3,5},{4,2},{5,3},{6,0},{7,1},{8,14},{9,15},{10,... | collective-permute-start | bytes 3145736 | tf_op jit(solution)/shard_map/ppermute | solution.py:190
  470.2 34.3 %collective-permute-start.67 = (bf16[128,4096]{1,0:T(8,128)(2,1)S(1)}, bf16[128,4096]{1,0:T(8,128)(2,1)S(1)}, u32[]{:S(2)}, u32[]{:S(2)}) collective-permute-start(bf16[128,4096]{1,0:T(8,128)(2,1)S(1)} %copy-done.23), channel_id=1, source_target_pairs={{0,4},{1,5},{2,6},{3,7},{4,0},{5,1},{6,2},{7,3},{8,12},{9,13},{10,... | collective-permute-start | bytes 3145736 | tf_op jit(solution)/shard_map/ppermute | solution.py:190
  483.9 26.0 %collective-permute-start.65 = (bf16[128,4096]{1,0:T(8,128)(2,1)S(1)}, bf16[128,4096]{1,0:T(8,128)(2,1)S(1)}, u32[]{:S(2)}, u32[]{:S(2)}) collective-permute-start(bf16[128,4096]{1,0:T(8,128)(2,1)S(1)} %get-tuple-element.54), channel_id=1, source_target_pairs={{0,2},{1,3},{2,0},{3,1},{4,6},{5,7},{6,4},{7,5},{8,10},{9,11},{10,... | collective-permute-start | bytes 3145736 | tf_op jit(solution)/shard_map/ppermute | solution.py:190
  485.3 72.8 %collective-permute-start.41 = (bf16[512,1024]{1,0:T(8,128)(2,1)}, bf16[512,1024]{1,0:T(8,128)(2,1)S(1)}, u32[]{:S(2)}, u32[]{:S(2)}) collective-permute-start(bf16[512,1024]{1,0:T(8,128)(2,1)} %convolution_convert_fusion.5), channel_id=1, source_target_pairs={{0,1},{1,0},{2,3},{3,2},{4,5},{5,4},{6,7},{7,6},{8,9},{9,8},{10,11... | collective-permute-start | bytes 3145736 | tf_op jit(solution)/shard_map/ppermute | solution.py:190
  485.4 47.7 %collective-permute-start.80 = (bf16[512,1024]{1,0:T(8,128)(2,1)S(1)}, bf16[512,1024]{1,0:T(8,128)(2,1)S(1)}, u32[]{:S(2)}, u32[]{:S(2)}) collective-permute-start(bf16[512,1024]{1,0:T(8,128)(2,1)S(1)} %copy-done.24), channel_id=1, source_target_pairs={{0,6},{1,7},{2,4},{3,5},{4,2},{5,3},{6,0},{7,1},{8,14},{9,15},{10,... | collective-permute-start | bytes 3145736 | tf_op jit(solution)/shard_map/ppermute | solution.py:190
  486.9 62.4 %collective-permute-start.78 = (bf16[512,1024]{1,0:T(8,128)(2,1)S(1)}, bf16[512,1024]{1,0:T(8,128)(2,1)S(1)}, u32[]{:S(2)}, u32[]{:S(2)}) collective-permute-start(bf16[512,1024]{1,0:T(8,128)(2,1)S(1)} %get-tuple-element.49), channel_id=1, source_target_pairs={{0,4},{1,5},{2,6},{3,7},{4,0},{5,1},{6,2},{7,3},{8,12},{9,13},{10,... | collective-permute-start | bytes 3145736 | tf_op jit(solution)/shard_map/ppermute | solution.py:190
  504.4 49.7 %collective-permute-start.76 = (bf16[512,1024]{1,0:T(8,128)(2,1)S(1)}, bf16[512,1024]{1,0:T(8,128)(2,1)S(1)}, u32[]{:S(2)}, u32[]{:S(2)}) collective-permute-start(bf16[512,1024]{1,0:T(8,128)(2,1)S(1)} %get-tuple-element.47), channel_id=1, source_target_pairs={{0,2},{1,3},{2,0},{3,1},{4,6},{5,7},{6,4},{7,5},{8,10},{9,11},{10,... | collective-permute-start | bytes 3145736 | tf_op jit(solution)/shard_map/ppermute | solution.py:190
  509.9 48.2 %collective-permute-start.43 = (bf16[512,1024]{1,0:T(8,128)(2,1)}, bf16[512,1024]{1,0:T(8,128)(2,1)S(1)}, u32[]{:S(2)}, u32[]{:S(2)}) collective-permute-start(bf16[512,1024]{1,0:T(8,128)(2,1)} %add_convert_fusion.7), channel_id=1, source_target_pairs={{0,8},{1,9},{2,10},{3,11},{4,12},{5,13},{6,14},{7,15},{8,0},{9,1},... | collective-permute-start | bytes 3145736 | tf_op jit(solution)/shard_map/ppermute | solution.py:190
  533.1 77.9 %collective-permute-start.70 = (bf16[64,4096]{1,0:T(8,128)(2,1)}, bf16[64,4096]{1,0:T(8,128)(2,1)}, u32[]{:S(2)}, u32[]{:S(2)}) collective-permute-start(bf16[64,4096]{1,0:T(8,128)(2,1)} %dynamic-slice_convert_fusion.1), channel_id=1, source_target_pairs={{0,8},{1,9},{2,10},{3,11},{4,12},{5,13},{6,14},{7,15},{8,0},{9,1},... | collective-permute-start | bytes 1572872 | tf_op jit(solution)/shard_map/ppermute | solution.py:190
  557.8 55.5 %collective-permute-start.81 = (bf16[256,1024]{1,0:T(8,128)(2,1)}, bf16[256,1024]{1,0:T(8,128)(2,1)}, u32[]{:S(2)}, u32[]{:S(2)}) collective-permute-start(bf16[256,1024]{1,0:T(8,128)(2,1)} %dynamic-slice_convert_fusion), channel_id=1, source_target_pairs={{0,8},{1,9},{2,10},{3,11},{4,12},{5,13},{6,14},{7,15},{8,0},{9,1},... | collective-permute-start | bytes 1572872 | tf_op jit(solution)/shard_map/ppermute | solution.py:190
  563.3 97.3 %collective-permute-start.44 = (bf16[512,1024]{1,0:T(8,128)(2,1)}, bf16[512,1024]{1,0:T(8,128)(2,1)S(1)}, u32[]{:S(2)}, u32[]{:S(2)}) collective-permute-start(bf16[512,1024]{1,0:T(8,128)(2,1)} %get-tuple-element.57), channel_id=1, source_target_pairs={{0,0},{1,16},{2,2},{3,18},{4,4},{5,20},{6,6},{7,22},{8,8},{9,24},{... | collective-permute-start | bytes 3145736 | tf_op jit(solution)/shard_map/ppermute | solution.py:190
  612.5 19.2 %collective-permute-start.71 = (bf16[32,4096]{1,0:T(8,128)(2,1)S(1)}, bf16[32,4096]{1,0:T(8,128)(2,1)S(1)}, u32[]{:S(2)}, u32[]{:S(2)}) collective-permute-start(bf16[32,4096]{1,0:T(8,128)(2,1)S(1)} %dynamic-slice_convert_fusion.6), channel_id=1, source_target_pairs={{0,16},{1,17},{2,18},{3,19},{4,20},{5,21},{6,22},{7,23},{8,24},{9,... | collective-permute-start | bytes 786440 | tf_op jit(solution)/shard_map/ppermute | solution.py:190
  614.6 28.3 %collective-permute-start.82 = (bf16[128,1024]{1,0:T(8,128)(2,1)S(1)}, bf16[128,1024]{1,0:T(8,128)(2,1)S(1)}, u32[]{:S(2)}, u32[]{:S(2)}) collective-permute-start(bf16[128,1024]{1,0:T(8,128)(2,1)S(1)} %dynamic-slice_convert_fusion.5), channel_id=1, source_target_pairs={{0,16},{1,17},{2,18},{3,19},{4,20},{5,21},{6,22},{7,23},{8,24},{9,... | collective-permute-start | bytes 786440 | tf_op jit(solution)/shard_map/ppermute | solution.py:190
  631.8 22.4 %collective-permute-start.72 = (bf16[32,4096]{1,0:T(8,128)(2,1)S(1)}, bf16[32,4096]{1,0:T(8,128)(2,1)S(1)}, u32[]{:S(2)}, u32[]{:S(2)}) collective-permute-start(bf16[32,4096]{1,0:T(8,128)(2,1)S(1)} %get-tuple-element.35), channel_id=1, source_target_pairs={{0,16},{1,17},{2,18},{3,19},{4,20},{5,21},{6,22},{7,23},{8,24},{9,... | collective-permute-start | bytes 786440 | tf_op jit(solution)/shard_map/ppermute | solution.py:190
  643.1 16.7 %collective-permute-start.83 = (bf16[128,1024]{1,0:T(8,128)(2,1)S(1)}, bf16[128,1024]{1,0:T(8,128)(2,1)S(1)}, u32[]{:S(2)}, u32[]{:S(2)}) collective-permute-start(bf16[128,1024]{1,0:T(8,128)(2,1)S(1)} %get-tuple-element.33), channel_id=1, source_target_pairs={{0,16},{1,17},{2,18},{3,19},{4,20},{5,21},{6,22},{7,23},{8,24},{9,... | collective-permute-start | bytes 786440 | tf_op jit(solution)/shard_map/ppermute | solution.py:190
  654.2 16.8 %collective-permute-start.73 = (bf16[64,4096]{1,0:T(8,128)(2,1)S(1)}, bf16[64,4096]{1,0:T(8,128)(2,1)S(1)}, u32[]{:S(2)}, u32[]{:S(2)}) collective-permute-start(bf16[64,4096]{1,0:T(8,128)(2,1)S(1)} %constant_dynamic-update-slice_fusion.2), channel_id=1, source_target_pairs={{0,8},{1,9},{2,10},{3,11},{4,12},{5,13},{6,14},{7,15},{8,0},{9,1},... | collective-permute-start | bytes 1572872 | tf_op jit(solution)/shard_map/ppermute | solution.py:190
  659.9 22.3 %collective-permute-start.84 = (bf16[256,1024]{1,0:T(8,128)(2,1)S(1)}, bf16[256,1024]{1,0:T(8,128)(2,1)S(1)}, u32[]{:S(2)}, u32[]{:S(2)}) collective-permute-start(bf16[256,1024]{1,0:T(8,128)(2,1)S(1)} %constant_dynamic-update-slice_fusion), channel_id=1, source_target_pairs={{0,8},{1,9},{2,10},{3,11},{4,12},{5,13},{6,14},{7,15},{8,0},{9,1},... | collective-permute-start | bytes 1572872 | tf_op jit(solution)/shard_map/ppermute | solution.py:190
  (79 other events, 1454.8 us)

commit v2 on v1

--- a/solution.py
+++ b/solution.py
@@ -30,57 +30,351 @@
     return _dot(a, b, 1, 1)
 
 
-def fwd_kernel(st_ref, q_ref, k_ref, v_ref, o_ref, lse_ref, qt_ref, vt_ref, *, bq, bk, scale):
-    n = q_ref.shape[0]
-    d = q_ref.shape[1] // 2
-    qt_ref[...] = jnp.transpose(q_ref[...])
-    vt_ref[...] = jnp.transpose(v_ref[...])
+MESH = pl.DeviceIdType.MESH
+
+
+def front_kernel(
+    tok, cot, win, wo, we, wr, vec, st,
+    x_ref, g_ref, n1, wf, wof, wef, wrf, vecs, qkv, att, lse, attn,
+    qt, vt, win_s, win_r, vec_s, vec_r, tok_s, tok_r, tok_l, near_s, near_r, core_s, core_r, fwd_s, fwd_r,
+    cot_s, cot_r, cot_l, own_l, w_s, w_r, move_s, move_r, move_l,
+    *, ns, nd, heads, d, bq, bk, chunks,
+):
+    seq, me = lax.axis_index("seq"), lax.axis_index("dp")
+    half, nearb, core = seq // 2, seq % 2, me % 2
+    member = 2 * core + nearb
+    n_rows, width = tok.shape
+    group = width // 4
+    small_rows = win.shape[0]
+    stays = half == core
+    swap_to = (2 * core + nearb, me - core + half)
+    near_to = (seq + 1 - 2 * nearb, me)
+    core_to = (seq, me + 1 - 2 * core)
+
+    def offset(k):
+        out = me
+        bit = 1
+        while bit <= k:
+            if k & bit:
+                out = out + bit - 2 * bit * ((me // bit) % 2)
+            bit *= 2
+        return out
+
+    def rcopy(src, dst, ss, rs, dev):
+        return pltpu.make_async_remote_copy(
+            src_ref=src, dst_ref=dst, send_sem=ss, recv_sem=rs, device_id=dev, device_id_type=MESH
+        )
+
+    barrier = pltpu.get_barrier_semaphore()
+
+    def hello(dev):
+        pl.semaphore_signal(barrier, inc=1, device_id=dev, device_id_type=MESH)
+
+    for k in range(1, nd):
+        hello((seq, offset(k)))
+    hello(near_to)
+    hello((near_to[0], core_to[1]))
+
+    @pl.when(jnp.logical_not(stays))
+    def _():
+        hello(swap_to)
+        pl.semaphore_wait(barrier, nd + 2)
+
+    @pl.when(stays)
+    def _():
+        pl.semaphore_wait(barrier, nd + 1)
+
+    sends = []
+
+    step = n_rows // chunks
+    tok_remote, tok_local = [], []
+    for c in range(chunks):
+        cut = pl.ds(c * step, step)
+        tok_remote.append(rcopy(tok.at[cut], x_ref.at[cut], tok_s.at[c], tok_r.at[c], swap_to))
+        tok_local.append(pltpu.make_async_copy(tok.at[cut], x_ref.at[cut], tok_l.at[c]))
+
+    @pl.when(jnp.logical_not(stays))
+    def _():
+        for c in tok_remote:
+            c.start()
+
+    @pl.when(stays)
+    def _():
+        for c in tok_local:
+            c.start()
+
+    vec_copies, win_copies, own_copies = [], [], []
+    for k in range(1, nd):
+        c = rcopy(vec, vecs.at[me], vec_s.at[k], vec_r.at[k], (seq, offset(k)))
+        c.start()
+        vec_copies.append(c)
+    c = pltpu.make_async_copy(vec, vecs.at[me], own_l.at[0])
+    c.start()
+    vec_copies.append(c)
+    my_rows = pl.ds(pl.multiple_of(me * small_rows, small_rows), small_rows)
+    for k in range(nd):
+        target = 2 * (core if k % 2 == 0 else 1 - core) + nearb
+        for i in range(3):
+            src = win.at[:, pl.ds(pl.multiple_of(i * width + target * group, 128), group)]
+            dst = wf.at[my_rows, pl.ds(i * group, group)]
+            if k == 0:
+                c = pltpu.make_async_copy(src, dst, own_l.at[1 + i])
+            else:
+                c = rcopy(src, dst, win_s.at[k, i], win_r.at[k, i], (seq, offset(k)))
+            c.start()
+            win_copies.append(c)
+
+    pairs = ((wo, wof), (we, wef), (wr, wrf))
+
+    def at(a, k, part=None):
+        high = pairs[a][0].shape[0]
+        if part is None:
+            return pairs[a][1].at[pl.ds(pl.multiple_of(offset(k) * high, high), high)]
+        return pairs[a][1].at[pl.ds(pl.multiple_of(offset(k) * high + part * (high // 2), high // 2), high // 2)]
+
+    held = {}
+
+    def send(a, slot, src, dst, k):
+        c = rcopy(src, dst, w_s.at[a, slot], w_r.at[a, slot], (seq, offset(k)))
+        c.start()
+        held[a, slot] = c
+
+    def weights_start(a):
+        if nd == 8:
+            send(a, 0, pairs[a][0], at(a, 0), 2)
+            send(a, 1, pairs[a][0], at(a, 0), 4)
+        else:
+            for k in range(2, nd, 2):
+                send(a, k, pairs[a][0], at(a, 0), k)
+        send(a, 2 if nd == 8 else 1, pairs[a][0], at(a, 0), 1)
+        c = pltpu.make_async_copy(pairs[a][0], at(a, 0), own_l.at[4 + a])
+        c.start()
+        held[a, "own"] = c
+
+    def weights_forward(a):
+        if nd == 8:
+            held[a, 0].wait_recv()
+            send(a, 3, at(a, 2, 0), at(a, 2, 0), 4)
+            send(a, 4, at(a, 2), at(a, 2), 1)
+            held[a, 1].wait_recv()
+            send(a, 5, at(a, 4, 1), at(a, 4, 1), 2)
+            send(a, 6, at(a, 4), at(a, 4), 1)
+        else:
+            for k in range(2, nd, 2):
+                held[a, k].wait_recv()
+                send(a, k + 1, at(a, k), at(a, k), 1)
+
+    def weights_last(a):
+        if nd == 8:
+            held[a, 3].wait_recv()
+            send(a, 7, at(a, 6, 0), at(a, 6, 0), 1)
+            held[a, 5].wait_recv()
+            send(a, 8, at(a, 6, 1), at(a, 6, 1), 1)
+
+    def weights_end(a):
+        held[a, "own"].wait()
+        for slot in (2, 4, 6, 7, 8) if nd == 8 else range(1, nd, 2):
+            held[a, slot].wait_recv()
+        for slot in range(9) if nd == 8 else range(1, nd):
+            held[a, slot].wait_send()
+
+    for c in vec_copies[:-1]:
+        c.wait_recv()
+        sends.append(c)
+    vec_copies[-1].wait()
+
+    def vector(i):
+        return jnp.concatenate([vecs[k, i : i + 1, :] for k in range(nd)], axis=1).astype(F32)
+
+    gain, shift = vector(0), vector(1)
+    near_copies, core_copies = [], []
+    for c in range(chunks):
+        cut = pl.ds(c * step, step)
+
+        @pl.when(jnp.logical_not(stays))
+        def _(c=c):
+            tok_remote[c].wait_recv()
+
+        @pl.when(stays)
+        def _(c=c):
+            tok_local[c].wait()
+
+        value = x_ref[cut, :].astype(F32)
+        center = value - jnp.mean(value, axis=-1, keepdims=True)
+        spread = jnp.mean(center * center, axis=-1, keepdims=True)
+        place = pl.ds(pl.multiple_of(member * n_rows + c * step, step), step)
+        n1[place, :] = (center * lax.rsqrt(spread + EPS) * gain + shift).astype(BF)
+        r = rcopy(n1.at[place], n1.at[place], near_s.at[c], near_r.at[c], near_to)
+        r.start()
+        near_copies.append(r)
+        r = rcopy(n1.at[place], n1.at[place], core_s.at[c], core_r.at[c], core_to)
+        r.start()
+        core_copies.append(r)
+
+    for c in win_copies[:3]:
+        c.wait()
+    for c in win_copies[3:]:
+        c.wait_recv()
+        sends.append(c)
+    for a in range(3):
+        weights_start(a)
+
+    def project(block, c=None):
+        size = n_rows if c is None else step
+        place = pl.ds(pl.multiple_of(block * n_rows + (0 if c is None else c * step), size), size)
+        mixed = _dot(n1[place, :], wf[...], 1, 0).astype(BF)
+        qkv[place, :] = mixed
+        qt[:, place] = jnp.transpose(mixed[:, :group])
+        vt[:, place] = jnp.transpose(mixed[:, 2 * group :])
+
+    project(member)
+    for c in core_copies:
+        c.wait_recv()
+        sends.append(c)
+    twin = 2 * (1 - core) + nearb
+    project(twin)
+    fwd_copies = []
+    beside = 2 * core + 1 - nearb
+    across = 2 * (1 - core) + 1 - nearb
+    for c in range(chunks):
+        near_copies[c].wait_recv()
+        sends.append(near_copies[c])
+        place = pl.ds(pl.multiple_of(beside * n_rows + c * step, step), step)
+        r = rcopy(n1.at[place], n1.at[place], fwd_s.at[c], fwd_r.at[c], core_to)
+        r.start()
+        fwd_copies.append(r)
+    project(beside)
+    for c in fwd_copies:
+        c.wait_recv()
+        sends.append(c)
+    project(across)
+
+    cot_remote = rcopy(cot, g_ref, cot_s, cot_r, swap_to)
+    cot_local = pltpu.make_async_copy(cot, g_ref, cot_l)
+
+    @pl.when(jnp.logical_not(stays))
+    def _():
+        cot_remote.start()
+
+    @pl.when(stays)
+    def _():
+        cot_local.start()
+
+    n = ns * n_rows
+    scale = d**-0.5
+    w = 2 * d
+    moves = []
     for i in range(n // bq):
         cs = slice(i * bq, (i + 1) * bq)
-        st = st_ref[:, cs]
-        outs = []
-        for h in range(2):
-            row = lax.broadcasted_iota(jnp.int32, (2 * d, bq), 0)
-            qm = jnp.where((row >= h * d) & (row < (h + 1) * d), qt_ref[:, cs], jnp.zeros((), BF))
-            m = jnp.full((1, bq), NEG, F32)
-            l = jnp.zeros((1, bq), F32)
-            acc = jnp.zeros((d, bq), F32)
-            for j in range(0, (i + 1) * bq, bk):
-                s = _dot(k_ref[j : j + bk, :], qm, 1, 0) * scale
-                key = lax.broadcasted_iota(jnp.int32, (bk, bq), 0) + j
-                ok = key >= st
-                if j + bk > i * bq:
-                    ok = ok & (key <= lax.broadcasted_iota(jnp.int32, (bk, bq), 1) + i * bq)
-                s = jnp.where(ok, s, NEG)
-                mn = jnp.maximum(m, jnp.max(s, axis=0, keepdims=True))
-                p = jnp.exp(s - mn)
-                a = jnp.exp(m - mn)
-                l = a * l + jnp.sum(p, axis=0, keepdims=True)
-                acc = a * acc + _dot(vt_ref[h * d : (h + 1) * d, j : j + bk], p.astype(BF), 1, 0)
-                m = mn
-            outs.append(acc / l)
-            lse_ref[0, h : h + 1, cs] = m + jnp.log(l)
-        o_ref[cs, :] = jnp.transpose(jnp.concatenate(outs, axis=0)).astype(BF)
-
-
-def flash_fwd(starts, qkv, heads, d, bq=512, bk=512):
-    n, w, pairs = starts.shape[1], 2 * d, heads // 2
-    blk = lambda c: pl.BlockSpec((n, w), lambda p: (0, c + p))
+
+        def pair(p, carry, i=i, cs=cs):
+            lanes = pl.ds(pl.multiple_of(p * w, w), w)
+            key_lanes = pl.ds(pl.multiple_of(group + p * w, w), w)
+            outs = []
+            for h in range(2):
+                row = lax.broadcasted_iota(jnp.int32, (w, bq), 0)
+                qm = jnp.where((row >= h * d) & (row < (h + 1) * d), qt[lanes, cs], jnp.zeros((), BF))
+                m = jnp.full((1, bq), NEG, F32)
+                l = jnp.zeros((1, bq), F32)
+                acc = jnp.zeros((d, bq), F32)
+                for j in range(0, (i + 1) * bq, bk):
+                    s = _dot(qkv[j : j + bk, key_lanes], qm, 1, 0) * scale
+                    key = lax.broadcasted_iota(jnp.int32, (bk, bq), 0) + j
+                    ok = key >= st[:, cs]
+                    if j + bk > i * bq:
+                        ok = ok & (key <= lax.broadcasted_iota(jnp.int32, (bk, bq), 1) + i * bq)
+                    s = jnp.where(ok, s, NEG)
+                    mn = jnp.maximum(m, jnp.max(s, axis=0, keepdims=True))
+                    e = jnp.exp(s - mn)
+                    a = jnp.exp(m - mn)
+                    l = a * l + jnp.sum(e, axis=0, keepdims=True)
+                    rows_h = pl.ds(pl.multiple_of(p * w + h * d, d), d)
+                    acc = a * acc + _dot(vt[rows_h, j : j + bk], e.astype(BF), 1, 0)
+                    m = mn
+                outs.append(acc / l)
+                lse[p, h : h + 1, cs] = m + jnp.log(l)
+            att[cs, lanes] = jnp.transpose(jnp.concatenate(outs, axis=0)).astype(BF)
+            return carry
+
+        lax.fori_loop(0, heads // 2, pair, 0)
+        mine = attn.at[:, pl.ds(pl.multiple_of(member * group, group), group)]
+        dev = (seq - nearb + i % 2, me - core + i // 2)
+        r = rcopy(att.at[cs], mine, move_s.at[i], move_r.at[member], dev)
+        keep = pltpu.make_async_copy(att.at[cs], mine, move_l)
+        moves.append((r, keep))
+
+        @pl.when(member != i)
+        def _(r=r):
+            r.start()
+
+        @pl.when(member == i)
+        def _(keep=keep):
+            keep.start()
+
+        if i < 3:
+            weights_forward(i)
+    for a in range(3):
+        weights_last(a)
+    for a in range(3):
+        weights_end(a)
+    for i, (r, keep) in enumerate(moves):
+        source = attn.at[:, pl.ds(i * group, group)]
+        arrival = pltpu.make_async_copy(source, source, move_r.at[i])
+
+        @pl.when(member != i)
+        def _(r=r, arrival=arrival):
+            r.wait_send()
+            arrival.wait()
+
+        @pl.when(member == i)
+        def _(keep=keep):
+            keep.wait()
+
+    @pl.when(jnp.logical_not(stays))
+    def _():
+        cot_remote.wait()
+        for c in tok_remote:
+            c.wait_send()
+
+    @pl.when(stays)
+    def _():
+        cot_local.wait()
+
+    for c in sends:
+        c.wait_send()
+
+
+def front(tok, cot, win, wo, we, wr, vec, starts, ns, nd, heads, d):
+    n_rows, width = tok.shape
+    n, group, chunks = n_rows * ns, width // 4, 4
+    slots = 9 if nd == 8 else nd
+    any_, vmem = pl.BlockSpec(memory_space=pl.ANY), pl.BlockSpec(memory_space=pltpu.VMEM)
+    full = lambda a: jax.ShapeDtypeStruct((a.shape[0] * nd, a.shape[1]), BF)
+    dma = lambda *shape: pltpu.SemaphoreType.DMA(shape)
+    sds = jax.ShapeDtypeStruct
     return pl.pallas_call(
-        functools.partial(fwd_kernel, bq=bq, bk=bk, scale=d**-0.5),
-        grid=(pairs,),
-        in_specs=[pl.BlockSpec((1, n), lambda p: (0, 0)), blk(0), blk(pairs), blk(2 * pairs)],
-        out_specs=[blk(0), pl.BlockSpec((1, 2, n), lambda p: (p, 0, 0))],
+        functools.partial(front_kernel, ns=ns, nd=nd, heads=heads, d=d, bq=n_rows, bk=n_rows, chunks=chunks),
+        in_specs=[any_] * 7 + [vmem],
+        out_specs=[vmem, any_, vmem, vmem, any_, any_, any_, vmem, vmem, vmem, vmem, vmem],
         out_shape=[
-            jax.ShapeDtypeStruct((n, pairs * w), BF),
-            jax.ShapeDtypeStruct((pairs, 2, n), F32),
+            sds(tok.shape, BF), sds(tok.shape, BF), sds((n, width), BF), sds((width, 3 * group), BF),
+            full(wo), full(we), full(wr), sds((nd, *vec.shape), BF), sds((n, 3 * group), BF),
+            sds((n, group), BF), sds((heads // 2, 2, n), F32), sds(tok.shape, BF),
         ],
-        scratch_shapes=[pltpu.VMEM((w, n), BF), pltpu.VMEM((w, n), BF)],
-        compiler_params=pltpu.CompilerParams(vmem_limit_bytes=48 << 20),
+        scratch_shapes=[
+            pltpu.VMEM((group, n), BF), pltpu.VMEM((group, n), BF),
+            dma(nd, 3), dma(nd, 3), dma(nd), dma(nd), dma(chunks), dma(chunks), dma(chunks),
+            dma(chunks), dma(chunks), dma(chunks), dma(chunks), dma(chunks), dma(chunks),
+            pltpu.SemaphoreType.DMA, pltpu.SemaphoreType.DMA, pltpu.SemaphoreType.DMA,
+            dma(7), dma(3, slots), dma(3, slots), dma(4), dma(4), pltpu.SemaphoreType.DMA,
+        ],
+        compiler_params=pltpu.CompilerParams(
+            collective_id=0, has_side_effects=True, vmem_limit_bytes=52 << 20
+        ),
         cost_estimate=pl.CostEstimate(
-            flops=8 * n * n * d * heads, bytes_accessed=8 * n * w * pairs, transcendentals=n * n * heads
+            flops=8 * n * n * d * heads, bytes_accessed=60_000_000, transcendentals=n * n * heads
         ),
-    )(starts, qkv, qkv, qkv)
+    )(tok, cot, win, wo, we, wr, vec, starts)
 
 
 def bwd_kernel(
@@ -225,44 +519,7 @@
     group = width // 4
     my_heads = HEADS // 4
 
-    x_low = links.swap(tokens[0])
-    vectors = jnp.concatenate(
-        [first_gain, first_shift, second_gain, second_shift, output_bias, reduce_bias, expand_bias]
-    )
-    small = width // nd
-    vectors = lax.all_gather(vectors.reshape(-1, small), "dp", axis=0).astype(F32)
-    gain_one, shift_one, gain_two, shift_two, output_add, reduce_add = (
-        vectors[:, i].reshape(-1) for i in range(6)
-    )
-    expand_add = vectors[:, 6:].reshape(-1)
-
-    def group_columns(array, which):
-        return jnp.concatenate([cols(array, i * width + which * group, group) for i in range(3)], axis=1)
-
-    for_even = group_columns(mixer_input, member)
-    for_odd = group_columns(mixer_input, member ^ 2)
-    small_rows = mixer_input.shape[0]
-    input_full = jnp.zeros((width, 3 * group), BF)
-    input_full = put(input_full, for_even, me * small_rows, 0)
-    for k in range(1, nd):
-        piece = links.dp(for_odd if k % 2 else for_even, k)
-        input_full = put(input_full, piece, (me ^ k) * small_rows, 0)
-
-    def gather(shard):
-        high = shard.shape[0]
-        full = jnp.zeros((high * nd, shard.shape[1]), BF)
-        for k in range(0, nd, 2):
-            piece = links.dp(shard, k) if k else shard
-            full = put(full, piece, (me ^ k) * high, 0)
-            full = put(full, links.core(piece), (me ^ k ^ 1) * high, 0)
-        return full
-
-    output_full = gather(mixer_output)
-    expand_full = gather(expand_weight)
-    reduce_full = gather(reduce_weight)
-    grad_low = links.swap(cotangent[0])
     lengths_row = jnp.where(half == core, lengths[0], links.core(lengths)[0])
-
     entry = jnp.arange(lengths_row.shape[0])
     ends = jnp.sum(jnp.where(entry[None, :] <= entry[:, None], lengths_row[None, :], 0), axis=1)
     place = jnp.arange(slots, dtype=jnp.int32)
@@ -271,22 +528,25 @@
     starts = jnp.where(place < ends[-1], starts, place).reshape(1, slots)
     live = (member * n_rows + jnp.arange(n_rows, dtype=jnp.int32) < ends[-1]).astype(F32)
 
+    small, small_rows = width // nd, mixer_input.shape[0]
+    vectors = jnp.concatenate(
+        [first_gain, first_shift, second_gain, second_shift, output_bias, reduce_bias, expand_bias]
+    ).reshape(-1, small)
+    vectors = jnp.concatenate([vectors, jnp.zeros((-vectors.shape[0] % 16, small), BF)])
+    (
+        x_low, grad_low, normed_all, input_full, output_full, expand_full, reduce_full, vectors,
+        qkv, attended, logsum, attention,
+    ) = front(
+        tokens[0], cotangent[0], mixer_input, mixer_output, expand_weight, reduce_weight, vectors,
+        starts, ns, nd, my_heads, head_dim,
+    )
+    vectors = vectors.astype(F32)
+    gain_one, shift_one, gain_two, shift_two, output_add, reduce_add = (
+        vectors[:, i].reshape(-1) for i in range(6)
+    )
+    expand_add = vectors[:, 6 : 6 + hidden // nd // small].reshape(-1)
     inputs = x_low.astype(F32)
-    normed_one = layer_normalize(inputs, gain_one, shift_one).astype(BF)
-    near_normed = links.near(normed_one)
-    normed_all = jnp.zeros((slots, width), BF)
-    normed_all = put(normed_all, normed_one, member * n_rows, 0)
-    normed_all = put(normed_all, near_normed, (member ^ 1) * n_rows, 0)
-    normed_all = put(normed_all, links.core(normed_one), (member ^ 2) * n_rows, 0)
-    normed_all = put(normed_all, links.core(near_normed), (member ^ 3) * n_rows, 0)
-    qkv = mm(normed_all, input_full).astype(BF)
-    attended, logsum = flash_fwd(starts, qkv, my_heads, head_dim)
-
     moves = (lambda a: a, links.near, links.core, links.both)
-    attention = jnp.zeros((n_rows, width), BF)
-    for j in range(4):
-        piece = moves[j](rows(attended, (member ^ j) * n_rows, n_rows))
-        attention = put(attention, piece, 0, (member ^ j) * group)
 
     resid = inputs + mm(attention, output_full) + output_add
     normed_two = layer_normalize(resid, gain_two, shift_two).astype(BF)

time: 690 us -> 573 us (0.83)
  Pallas kernels: 60.4 us -> 157 us
  waiting for transfers between devices: 275 us -> 181 us
  starting transfers between devices: 98.7 us -> 43.9 us
  local copies, waits for them, and re-layouts: 65.6 us -> 31.5 us
  matrix products: 98 us -> 77.2 us
  blocking collectives: 54.6 us -> 46.4 us
    pallas_call x1, Pallas kernels: 29.8 us -> 126 us  [front(): pl.pallas_call(functools.partial(front_kernel, ns=ns, nd=nd, heads=heads,...]
    ppermute x85 -> x49, waiting for transfers between devices: 275 us -> 181 us  [go(): return lax.ppermute(array, ('seq', 'dp'), pairs)]
    ppermute x85 -> x49, starting transfers between devices: 98.7 us -> 43.9 us  [go(): return lax.ppermute(array, ('seq', 'dp'), pairs)]
    dynamic_update_slice x43 -> x6, local copies, waits for them, and re-layouts: 25.4 us -> 2.21 us  [put(): return lax.dynamic_update_slice(array, piece, (row, col))]
    dot_general x15 -> x14, matrix products: 98 us -> 77.2 us  [_dot(): lax.dot_general(a, b, (((ca,), (cb,)), ((), ())), preferred_element_type=...]
    broadcast_in_dim x6 -> x0, local copies, waits for them, and re-layouts: 10.9 us -> none  [the longest x3 9.04 us: gather(): full = jnp.zeros((high * nd, shard.shape[1]), BF)]
    all_gather x1 -> x0, blocking collectives: 9.03 us -> none  [on_device(): lax.all_gather(vectors.reshape(-1, small), 'dp', axis=0).astype(F32)]
    unnamed x125 -> x85, local copies, waits for them, and re-layouts: 16.8 us -> 17.4 us
  transfers between devices with their start and end apart: 85 -> 49, of which waited for: 32 -> 22; matrix products, arithmetic and copies ran while one was open for 19% -> 9% of each run, Pallas kernels for 9% -> 5%
where the time goes in v2:
time: 573 us; the launch traced here: 565 us
  waiting for transfers between devices  181 us (32%)
  Pallas kernels  157 us (27%)
  matrix products  77.2 us (13%)
  blocking collectives  46.4 us (8%)
  starting transfers between devices  43.9 us (8%)
  local copies, waits for them, and re-layouts  31.5 us (5%)
  other arithmetic  25.8 us (5%)
    ppermute x49, waiting for transfers between devices, go(): return lax.ppermute(array, ('seq', 'dp'), pairs)  181 us
    pallas_call x1, Pallas kernels, front(): pl.pallas_call(functools.partial(front_kernel, ns=ns, nd=nd, heads=heads,...  126 us
    dot_general x14, matrix products, _dot(): lax.dot_general(a, b, (((ca,), (cb,)), ((), ())), preferred_element_type=...  77.2 us
    psum x1, blocking collectives, on_device(): sums = lax.psum(sums, ('seq', 'dp'))  46.4 us
    ppermute x49, starting transfers between devices, go(): return lax.ppermute(array, ('seq', 'dp'), pairs)  43.9 us
    pallas_call x1, Pallas kernels, flash_bwd(): pl.pallas_call(functools.partial(bwd_kernel, bq=bq, bk=bk, scale=d ** (-0...  31 us
    unnamed x85, local copies, waits for them, and re-layouts  17.4 us
  transfers between devices with their start and end apart: 49, of which 22 were waited for; matrix products, arithmetic and copies ran while one was open for 9% of the time, Pallas kernels for 5%

profile of v2, /device:TPU:0, one launch (start us, length us, event | category | flops | bytes accessed | tf_op | source)
XLA Modules:
  0.0 564.8 jit_solution(14363205081579735463)
XLA Ops:
  11.5 126.0 %shard_map.237 = (bf16[512,1024]{1,0:T(8,128)(2,1)}, bf16[512,1024]{1,0:T(8,128)(2,1)}, bf16[2048,1024]{1,0:T(8,128)(2,1)}, bf16[1024,768]{1,0:T(8,128)(2,1)}, b...) custom-call(bf16[512,1024]{1,0:T(8,128)(2,1)} %bitcast.67, ...), custom_call_target="tpu_custom_call" | custom-call | flops 8589934592 | bytes 60000000 | tf_op jit(solution)/shard_map/pallas_call | solution.py:355
  138.2 1.4 convert_reduce_fusion
  139.6 3.7 fusion.51
  144.3 7.2 %fusion.45 = f32[512,4096]{1,0:T(8,128)} fusion(bf16[1024,4096]{1,0:T(8,128)(2,1)S(1)} %copy-done.26, f32[512,1024]{1,0:T(8,128)S(1)} %get-tuple-element.105, f32[1024]{0:T(1024)S(1)} %bitcast.63, f32[1024]{0:T(1024)S(1)} %bitcast.56, f32[512]{0:T(512)S(1)} %fusion.40, f32[512]{0:T(512)S(1)} %broadcast_multiply_fusion.1), kind=kOutput, calls=%fused_computation.157 | convolution fusion | flops 4297588736 | bytes 18886656 | tf_op jit(solution)/shard_map/dot_general | solution.py:18
  151.5 13.7 %fusion.52 = (f32[4096]{0:T(1024)S(1)}, bf16[512,4096]{1,0:T(8,128)(2,1)S(1)}) fusion(f32[512,4096]{1,0:T(8,128)} %fusion.45, f32[4096]{0:T(1024)S(1)} %bitcast.53, bf16[4096,1024]{1,0:T(8,128)(2,1)} %get-tuple-element.33, bf16[512,1024]{1,0:T(8,128)(2,1)S(1)} %copy-done.18, f32[512]{0:T(512)S(1)} %fusion.39), kind=kOutput, calls=%fused_computation.164 | convolution fusion | flops 4342673408 | bytes 22054912 | tf_op jit(solution)/shard_map/dot_general | solution.py:18
  165.2 5.0 multiply_reduce_fusion
  171.9 1.4 convolution_convert_fusion.5
  173.3 1.5 convolution_convert_fusion.2
  175.4 7.5 %convolution_convert_fusion.1 = bf16[1024,4096]{1,0:T(8,128)(2,1)} fusion(bf16[512,4096]{1,0:T(8,128)(2,1)S(1)} %copy-done.29, f32[512,1024]{1,0:T(8,128)S(1)} %get-tuple-element.105, f32[1024]{0:T(1024)S(1)} %bitcast.64, f32[1024]{0:T(1024)S(1)} %bitcast.59, f32[512]{0:T(512)S(1)} %fusion.40, f32[512]{0:T(512)S(1)} %broadcast_multiply_fusion.1), kind=kOutput, calls=%fused_computation.10 | convolution fusion | flops 4301783040 | bytes 14692352 | tf_op jit(solution)/shard_map/dot_general | solution.py:18
  183.0 10.3 %convolution_convert_fusion = bf16[4096,1024]{1,0:T(8,128)(2,1)S(1)} fusion(bf16[512,1024]{1,0:T(8,128)(2,1)} %get-tuple-element.34, f32[512]{0:T(512)S(1)} %fusion.39, f32[512,4096]{1,0:T(8,128)} %fusion.45, f32[4096]{0:T(1024)S(1)} %bitcast.54), kind=kOutput, calls=%fused_computation.9 | convolution fusion | flops 4321705984 | bytes 17844224 | tf_op jit(solution)/shard_map/dot_general | solution.py:18
  193.3 15.3 %add_convert_fusion.8 = bf16[512,1024]{1,0:T(8,128)(2,1)} fusion(f32[512,1024]{1,0:T(8,128)S(1)} %get-tuple-element.105, bf16[4096,1024]{1,0:T(8,128)(2,1)} %get-tuple-element.33, f32[1024]{0:T(1024)S(1)} %bitcast.62, f32[512,4096]{1,0:T(8,128)} %fusion.45, f32[4096]{0:T(1024)S(1)} %bitcast.55), kind=kOutput, calls=%fused_computation.45 | convolution fusion | flops 4317511680 | bytes 19943424 | tf_op jit(solution)/shard_map/dot_general | solution.py:18
  208.6 9.5 %collective-permute-start.1 = (bf16[512,1024]{1,0:T(8,128)(2,1)}, bf16[512,1024]{1,0:T(8,128)(2,1)}, u32[]{:S(2)}, u32[]{:S(2)}) collective-permute-start(bf16[512,1024]{1,0:T(8,128)(2,1)} %add_convert_fusion.8), channel_id=1, source_target_pairs={{0,0},{1,16},{2,2},{3,18},{4,4},{5,20},{6,6},{7,22},{8,8},{9,24},{... | collective-permute-start | bytes 3145736 | tf_op jit(solution)/shard_map/ppermute | solution.py:484
  220.9 1.2 collective-permute-start.4
  222.1 1.6 constant_dynamic-slice_fusion.7
  224.7 1.7 constant_dynamic-slice_fusion.3
  226.4 2.4 collective-permute-done.2
  232.5 31.0 %shard_map.238 = (bf16[2048,256]{1,0:T(8,128)(2,1)}, bf16[2048,256]{1,0:T(8,128)(2,1)}, bf16[2048,256]{1,0:T(8,128)(2,1)}) custom-call(s32[1,2048]{1,0:T(1,128)} %copy-done, bf16[2048,768]{1,0:T(8,128)(2,1)} %get-tuple-element.35.q_ref.k_ref.v_ref, bf16[2048,768]{1,0:T(8,128)(2,1)} %get-tuple-element.35.q_ref.k_ref.v_ref, ...), custom_call_target="tpu_custom_call" | custom-call | flops 21474836480 | bytes 8388608 | tf_op jit(solution)/shard_map/pallas_call | solution.py:428
  263.5 1.4 constant_dynamic-update-slice_fusion.11
  264.9 1.4 add_convert_fusion.15
  267.2 1.3 collective-permute-start.20
  268.4 1.5 collective-permute-start.18
  270.1 3.2 copy-done.24
  273.2 3.7 fusion.53
  278.0 2.7 collective-permute-done.20
  281.9 1.4 collective-permute-start.23
  283.5 1.3 collective-permute-start.11
  284.8 1.3 collective-permute-start.10
  287.1 3.0 collective-permute-start.24
  290.1 2.0 convolution_convert_fusion.3
  292.5 4.0 collective-permute-done.11
  296.5 7.1 %collective-permute-done.10 = bf16[256,768]{1,0:T(8,128)(2,1)S(1)} collective-permute-done((bf16[256,768]{1,0:T(8,128)(2,1)S(1)}, bf16[256,768]{1,0:T(8,128)(2,1)S(1)}, u32[]{:S(2)}, u32[]{:S(2)}) %collective-permute-start.10) | collective-permute-done | bytes 393248 | tf_op jit(solution)/shard_map/ppermute | solution.py:484
  303.6 1.7 collective-permute-start.25
  305.5 1.3 collective-permute-start.12
  306.8 11.6 %collective-permute-done.25 = bf16[32,1024]{1,0:T(8,128)(2,1)S(1)} collective-permute-done((bf16[32,1024]{1,0:T(8,128)(2,1)S(1)}, bf16[32,1024]{1,0:T(8,128)(2,1)S(1)}, u32[]{:S(2)}, u32[]{:S(2)}) %collective-permute-start.25) | collective-permute-done | bytes 65568 | tf_op jit(solution)/shard_map/ppermute | solution.py:484
  318.6 2.0 convolution_convert_fusion.4
  320.6 9.0 %collective-permute-done.26 = bf16[64,1024]{1,0:T(8,128)(2,1)S(1)} collective-permute-done((bf16[64,1024]{1,0:T(8,128)(2,1)S(1)}, bf16[64,1024]{1,0:T(8,128)(2,1)S(1)}, u32[]{:S(2)}, u32[]{:S(2)}) %collective-permute-start.26) | collective-permute-done | bytes 131104 | tf_op jit(solution)/shard_map/ppermute | solution.py:484
  332.4 1.6 add_convert_fusion.2
  335.4 1.5 collective-permute-done.30
  337.0 3.0 add_convert_fusion.5
  340.1 1.4 collective-permute-start.33
  341.5 2.9 add_convert_fusion.7
  344.4 2.2 collective-permute-done.13
  347.8 1.4 collective-permute-done.15
  350.3 1.7 collective-permute-start.44
  351.9 15.1 %collective-permute-done.33 = bf16[128,4096]{1,0:T(8,128)(2,1)S(1)} collective-permute-done((bf16[128,4096]{1,0:T(8,128)(2,1)S(1)}, bf16[128,4096]{1,0:T(8,128)(2,1)S(1)}, u32[]{:S(2)}, u32[]{:S(2)}) %collective-permute-start.33) | collective-permute-done | bytes 1048608 | tf_op jit(solution)/shard_map/ppermute | solution.py:484
  368.1 21.5 %collective-permute-done.31 = bf16[128,4096]{1,0:T(8,128)(2,1)S(1)} collective-permute-done((bf16[128,4096]{1,0:T(8,128)(2,1)S(1)}, bf16[128,4096]{1,0:T(8,128)(2,1)S(1)}, u32[]{:S(2)}, u32[]{:S(2)}) %collective-permute-start.31) | collective-permute-done | bytes 1048608 | tf_op jit(solution)/shard_map/ppermute | solution.py:484
  391.1 2.0 convert_add_fusion.2
  394.0 18.1 %collective-permute-done.44 = bf16[512,1024]{1,0:T(8,128)(2,1)S(1)} collective-permute-done((bf16[512,1024]{1,0:T(8,128)(2,1)S(1)}, bf16[512,1024]{1,0:T(8,128)(2,1)S(1)}, u32[]{:S(2)}, u32[]{:S(2)}) %collective-permute-start.44) | collective-permute-done | bytes 1048608 | tf_op jit(solution)/shard_map/ppermute | solution.py:484
  412.5 21.4 %collective-permute-done.42 = bf16[512,1024]{1,0:T(8,128)(2,1)S(1)} collective-permute-done((bf16[512,1024]{1,0:T(8,128)(2,1)S(1)}, bf16[512,1024]{1,0:T(8,128)(2,1)S(1)}, u32[]{:S(2)}, u32[]{:S(2)}) %collective-permute-start.42) | collective-permute-done | bytes 1048608 | tf_op jit(solution)/shard_map/ppermute | solution.py:484
  433.9 2.3 convert_add_fusion.1
  440.0 2.1 fusion.18
  442.1 1.9 collective-permute-start.8
  444.0 46.4 %psum.7 = f32[10240]{0:T(1024)S(1)} all-reduce(f32[10240]{0:T(1024)S(1)} %pad_maximum_fusion), channel_id=1, replica_groups=mesh['seq'=4,'dp'=8] {'seq','dp'}, use_global_device_ids=true, to_apply=%region_17.18 | all-reduce | flops 10240 | bytes 81920 | tf_op jit(solution)/shard_map/psum | solution.py:642
  490.4 1.3 convert_add_fusion.5
  492.6 1.2 convert_add_fusion.4
  493.8 2.2 collective-permute-start.46
  496.1 14.9 %collective-permute-done.35 = bf16[32,4096]{1,0:T(8,128)(2,1)S(1)} collective-permute-done((bf16[32,4096]{1,0:T(8,128)(2,1)S(1)}, bf16[32,4096]{1,0:T(8,128)(2,1)S(1)}, u32[]{:S(2)}, u32[]{:S(2)}) %collective-permute-start.35) | collective-permute-done | bytes 262176 | tf_op jit(solution)/shard_map/ppermute | solution.py:484
  512.4 9.8 %collective-permute-done.46 = bf16[128,1024]{1,0:T(8,128)(2,1)S(1)} collective-permute-done((bf16[128,1024]{1,0:T(8,128)(2,1)S(1)}, bf16[128,1024]{1,0:T(8,128)(2,1)S(1)}, u32[]{:S(2)}, u32[]{:S(2)}) %collective-permute-start.46) | collective-permute-done | bytes 262176 | tf_op jit(solution)/shard_map/ppermute | solution.py:484
  522.4 11.0 %collective-permute-done.36 = bf16[32,4096]{1,0:T(8,128)(2,1)S(1)} collective-permute-done((bf16[32,4096]{1,0:T(8,128)(2,1)S(1)}, bf16[32,4096]{1,0:T(8,128)(2,1)S(1)}, u32[]{:S(2)}, u32[]{:S(2)}) %collective-permute-start.36) | collective-permute-done | bytes 262176 | tf_op jit(solution)/shard_map/ppermute | solution.py:484
  533.5 5.5 collective-permute-done.47
  539.8 1.6 bitcast_convert_fusion
  541.4 8.9 %collective-permute-done.37 = bf16[64,4096]{1,0:T(8,128)(2,1)S(1)} collective-permute-done((bf16[64,4096]{1,0:T(8,128)(2,1)S(1)}, bf16[64,4096]{1,0:T(8,128)(2,1)S(1)}, u32[]{:S(2)}, u32[]{:S(2)}) %collective-permute-start.37) | collective-permute-done | bytes 524320 | tf_op jit(solution)/shard_map/ppermute | solution.py:484
  550.3 11.1 %collective-permute-done.48 = bf16[256,1024]{1,0:T(8,128)(2,1)S(1)} collective-permute-done((bf16[256,1024]{1,0:T(8,128)(2,1)S(1)}, bf16[256,1024]{1,0:T(8,128)(2,1)S(1)}, u32[]{:S(2)}, u32[]{:S(2)}) %collective-permute-start.48) | collective-permute-done | bytes 524320 | tf_op jit(solution)/shard_map/ppermute | solution.py:484
  561.5 3.0 copy.65
  (230 shorter events, 44.4 us)
Async XLA Ops:
  0.6 6.6 %collective-permute-start = (s32[1,4]{1,0:T(1,128)}, s32[1,4]{1,0:T(1,128)S(1)}, u32[]{:S(2)}, u32[]{:S(2)}) collective-permute-start(s32[1,4]{1,0:T(1,128)} %param.15), channel_id=1, source_target_pairs={{0,1},{1,0},{2,3},{3,2},{4,5},{5,4},{6,7},{7,6},{8,9},{9,8},{10,11... | collective-permute-start | bytes 56 | tf_op jit(solution)/shard_map/ppermute | solution.py:484
  9.4 128.1 %copy-start = (s32[1,2048]{1,0:T(1,128)}, s32[1,2048]{1,0:T(1,128)S(1)}, u32[]{:S(2)}) copy-start(s32[1,2048]{1,0:T(1,128)S(1)} %compare_select_fusion.st.st_ref) | copy-start | bytes 24580
  144.3 20.9 %slice-start.6 = ((s8[8388608]{0:T(1024)(128)(4,1)}), s8[4194304]{0:T(1024)(128)(4,1)S(1)}, s32[]{:S(2)}) async-start(s8[8388608]{0:T(1024)(128)(4,1)} %bitcast.69), calls=%async_computation.6 | async-start | bytes 8388608
  151.5 13.7 %slice-start.7 = ((s8[8388608]{0:T(1024)(128)(4,1)}), s8[4194304]{0:T(1024)(128)(4,1)S(1)}, s32[]{:S(2)}) async-start(s8[8388608]{0:T(1024)(128)(4,1)} %bitcast.69), calls=%async_computation.7 | async-start | bytes 8388608
  193.3 31.4 %copy-start.5 = (bf16[4096,1024]{1,0:T(8,128)(2,1)}, bf16[4096,1024]{1,0:T(8,128)(2,1)S(1)}, u32[]{:S(2)}) copy-start(bf16[4096,1024]{1,0:T(8,128)(2,1)S(1)} %convolution_convert_fusion) | copy-start | bytes 25165828
  193.3 28.8 %slice-start.2 = ((s8[8388608]{0:T(1024)(128)(4,1)}), s8[4194304]{0:T(1024)(128)(4,1)S(1)}, s32[]{:S(2)}) async-start(s8[8388608]{0:T(1024)(128)(4,1)} %bitcast.41), calls=%async_computation.2 | async-start | bytes 8388608
  193.3 28.8 %slice-start.3 = ((s8[8388608]{0:T(1024)(128)(4,1)}), s8[4194304]{0:T(1024)(128)(4,1)S(1)}, s32[]{:S(2)}) async-start(s8[8388608]{0:T(1024)(128)(4,1)} %bitcast.41), calls=%async_computation.3 | async-start | bytes 8388608
  208.6 121.1 %collective-permute-start.1 = (bf16[512,1024]{1,0:T(8,128)(2,1)}, bf16[512,1024]{1,0:T(8,128)(2,1)}, u32[]{:S(2)}, u32[]{:S(2)}) collective-permute-start(bf16[512,1024]{1,0:T(8,128)(2,1)} %add_convert_fusion.8), channel_id=1, source_target_pairs={{0,0},{1,16},{2,2},{3,18},{4,4},{5,20},{6,6},{7,22},{8,8},{9,24},{... | collective-permute-start | bytes 3145736 | tf_op jit(solution)/shard_map/ppermute | solution.py:484
  220.0 8.9 %collective-permute-start.2 = (bf16[512,256]{1,0:T(8,128)(2,1)S(1)}, bf16[512,256]{1,0:T(8,128)(2,1)S(1)}, u32[]{:S(2)}, u32[]{:S(2)}) collective-permute-start(bf16[512,256]{1,0:T(8,128)(2,1)S(1)} %get-tuple-element.89), channel_id=1, source_target_pairs={{0,8},{1,9},{2,10},{3,11},{4,12},{5,13},{6,14},{7,15},{8,0},{9,1},... | collective-permute-start | bytes 786440 | tf_op jit(solution)/shard_map/ppermute | solution.py:484
  220.9 8.7 %collective-permute-start.3 = (bf16[512,256]{1,0:T(8,128)(2,1)S(1)}, bf16[512,256]{1,0:T(8,128)(2,1)S(1)}, u32[]{:S(2)}, u32[]{:S(2)}) collective-permute-start(bf16[512,256]{1,0:T(8,128)(2,1)S(1)} %get-tuple-element.88), channel_id=1, source_target_pairs={{0,1},{1,0},{2,3},{3,2},{4,5},{5,4},{6,7},{7,6},{8,9},{9,8},{10,11... | collective-permute-start | bytes 786440 | tf_op jit(solution)/shard_map/ppermute | solution.py:484
  220.9 9.9 %collective-permute-start.4 = (bf16[512,256]{1,0:T(8,128)(2,1)S(1)}, bf16[512,256]{1,0:T(8,128)(2,1)S(1)}, u32[]{:S(2)}, u32[]{:S(2)}) collective-permute-start(bf16[512,256]{1,0:T(8,128)(2,1)S(1)} %get-tuple-element.87), channel_id=1, source_target_pairs={{0,9},{1,8},{2,11},{3,10},{4,13},{5,12},{6,15},{7,14},{8,1},{9,0},... | collective-permute-start | bytes 786440 | tf_op jit(solution)/shard_map/ppermute | solution.py:484
  224.7 40.2 %collective-permute-start.17 = (bf16[128,1024]{1,0:T(8,128)(2,1)}, bf16[128,1024]{1,0:T(8,128)(2,1)}, u32[]{:S(2)}, u32[]{:S(2)}) collective-permute-start(bf16[128,1024]{1,0:T(8,128)(2,1)} %get-tuple-element.83), channel_id=1, source_target_pairs={{0,1},{1,0},{2,3},{3,2},{4,5},{5,4},{6,7},{7,6},{8,9},{9,8},{10,11... | collective-permute-start | bytes 786440 | tf_op jit(solution)/shard_map/ppermute | solution.py:484
  228.8 36.1 %collective-permute-start.21 = (bf16[128,1024]{1,0:T(8,128)(2,1)}, bf16[128,1024]{1,0:T(8,128)(2,1)S(1)}, u32[]{:S(2)}, u32[]{:S(2)}) collective-permute-start(bf16[128,1024]{1,0:T(8,128)(2,1)} %get-tuple-element.81), channel_id=1, source_target_pairs={{0,1},{1,0},{2,3},{3,2},{4,5},{5,4},{6,7},{7,6},{8,9},{9,8},{10,11... | collective-permute-start | bytes 786440 | tf_op jit(solution)/shard_map/ppermute | solution.py:484
  229.6 35.4 %collective-permute-start.19 = (bf16[128,1024]{1,0:T(8,128)(2,1)}, bf16[128,1024]{1,0:T(8,128)(2,1)}, u32[]{:S(2)}, u32[]{:S(2)}) collective-permute-start(bf16[128,1024]{1,0:T(8,128)(2,1)} %get-tuple-element.82), channel_id=1, source_target_pairs={{0,1},{1,0},{2,3},{3,2},{4,5},{5,4},{6,7},{7,6},{8,9},{9,8},{10,11... | collective-permute-start | bytes 786440 | tf_op jit(solution)/shard_map/ppermute | solution.py:484
  230.8 47.2 %collective-permute-start.16 = (bf16[128,1024]{1,0:T(8,128)(2,1)S(1)}, bf16[128,1024]{1,0:T(8,128)(2,1)}, u32[]{:S(2)}, u32[]{:S(2)}) collective-permute-start(bf16[128,1024]{1,0:T(8,128)(2,1)S(1)} %get-tuple-element.80), channel_id=1, source_target_pairs={{0,1},{1,0},{2,3},{3,2},{4,5},{5,4},{6,7},{7,6},{8,9},{9,8},{10,11... | collective-permute-start | bytes 786440 | tf_op jit(solution)/shard_map/ppermute | solution.py:484
  266.3 11.6 %collective-permute-start.22 = (bf16[128,1024]{1,0:T(8,128)(2,1)S(1)}, bf16[128,1024]{1,0:T(8,128)(2,1)S(1)}, u32[]{:S(2)}, u32[]{:S(2)}) collective-permute-start(bf16[128,1024]{1,0:T(8,128)(2,1)S(1)} %get-tuple-element.85), channel_id=1, source_target_pairs={{0,6},{1,7},{2,4},{3,5},{4,2},{5,3},{6,0},{7,1},{8,14},{9,15},{10,... | collective-permute-start | bytes 786440 | tf_op jit(solution)/shard_map/ppermute | solution.py:484
  267.2 13.6 %collective-permute-start.20 = (bf16[128,1024]{1,0:T(8,128)(2,1)S(1)}, bf16[128,1024]{1,0:T(8,128)(2,1)S(1)}, u32[]{:S(2)}, u32[]{:S(2)}) collective-permute-start(bf16[128,1024]{1,0:T(8,128)(2,1)S(1)} %get-tuple-element.86), channel_id=1, source_target_pairs={{0,4},{1,5},{2,6},{3,7},{4,0},{5,1},{6,2},{7,3},{8,12},{9,13},{10,... | collective-permute-start | bytes 786440 | tf_op jit(solution)/shard_map/ppermute | solution.py:484
  268.4 12.3 %collective-permute-start.18 = (bf16[128,1024]{1,0:T(8,128)(2,1)S(1)}, bf16[128,1024]{1,0:T(8,128)(2,1)S(1)}, u32[]{:S(2)}, u32[]{:S(2)}) collective-permute-start(bf16[128,1024]{1,0:T(8,128)(2,1)S(1)} %get-tuple-element.84), channel_id=1, source_target_pairs={{0,2},{1,3},{2,0},{3,1},{4,6},{5,7},{6,4},{7,5},{8,10},{9,11},{10,... | collective-permute-start | bytes 786440 | tf_op jit(solution)/shard_map/ppermute | solution.py:484
  270.1 48.5 %copy-start.21 = (bf16[2048,768]{1,0:T(8,128)(2,1)}, bf16[2048,768]{1,0:T(8,128)(2,1)S(1)}, u32[]{:S(2)}) copy-start(bf16[2048,768]{1,0:T(8,128)(2,1)S(1)} %constant_dynamic-update-slice_fusion.9) | copy-start | bytes 9437188
  281.9 5.1 collective-permute-start.23
  283.5 13.0 %collective-permute-start.11 = (bf16[256,768]{1,0:T(8,128)(2,1)S(1)}, bf16[256,768]{1,0:T(8,128)(2,1)S(1)}, u32[]{:S(2)}, u32[]{:S(2)}) collective-permute-start(bf16[256,768]{1,0:T(8,128)(2,1)S(1)} %get-tuple-element.78), channel_id=1, source_target_pairs={{0,6},{1,7},{2,4},{3,5},{4,2},{5,3},{6,0},{7,1},{8,14},{9,15},{10,... | collective-permute-start | bytes 1179656 | tf_op jit(solution)/shard_map/ppermute | solution.py:484
  284.8 18.8 %collective-permute-start.10 = (bf16[256,768]{1,0:T(8,128)(2,1)S(1)}, bf16[256,768]{1,0:T(8,128)(2,1)S(1)}, u32[]{:S(2)}, u32[]{:S(2)}) collective-permute-start(bf16[256,768]{1,0:T(8,128)(2,1)S(1)} %get-tuple-element.79), channel_id=1, source_target_pairs={{0,4},{1,5},{2,6},{3,7},{4,0},{5,1},{6,2},{7,3},{8,12},{9,13},{10,... | collective-permute-start | bytes 1179656 | tf_op jit(solution)/shard_map/ppermute | solution.py:484
  286.1 19.2 %collective-permute-start.9 = (bf16[256,768]{1,0:T(8,128)(2,1)S(1)}, bf16[256,768]{1,0:T(8,128)(2,1)S(1)}, u32[]{:S(2)}, u32[]{:S(2)}) collective-permute-start(bf16[256,768]{1,0:T(8,128)(2,1)S(1)} %get-tuple-element.77), channel_id=1, source_target_pairs={{0,2},{1,3},{2,0},{3,1},{4,6},{5,7},{6,4},{7,5},{8,10},{9,11},{10,... | collective-permute-start | bytes 1179656 | tf_op jit(solution)/shard_map/ppermute | solution.py:484
  287.1 5.3 collective-permute-start.24
  290.1 42.3 %slice-start = ((s8[8388608]{0:T(1024)(128)(4,1)}), s8[4194304]{0:T(1024)(128)(4,1)S(1)}, s32[]{:S(2)}) async-start(s8[8388608]{0:T(1024)(128)(4,1)} %bitcast.39), calls=%async_computation | async-start | bytes 8388608
  292.4 37.9 %collective-permute-start.39 = (bf16[512,1024]{1,0:T(8,128)(2,1)S(1)}, bf16[512,1024]{1,0:T(8,128)(2,1)S(1)}, u32[]{:S(2)}, u32[]{:S(2)}) collective-permute-start(bf16[512,1024]{1,0:T(8,128)(2,1)S(1)} %copy-done.15), channel_id=1, source_target_pairs={{0,1},{1,0},{2,3},{3,2},{4,5},{5,4},{6,7},{7,6},{8,9},{9,8},{10,11... | collective-permute-start | bytes 3145736 | tf_op jit(solution)/shard_map/ppermute | solution.py:484
  296.5 35.2 %collective-permute-start.43 = (bf16[512,1024]{1,0:T(8,128)(2,1)S(1)}, bf16[512,1024]{1,0:T(8,128)(2,1)S(1)}, u32[]{:S(2)}, u32[]{:S(2)}) collective-permute-start(bf16[512,1024]{1,0:T(8,128)(2,1)S(1)} %copy-done.14), channel_id=1, source_target_pairs={{0,1},{1,0},{2,3},{3,2},{4,5},{5,4},{6,7},{7,6},{8,9},{9,8},{10,11... | collective-permute-start | bytes 3145736 | tf_op jit(solution)/shard_map/ppermute | solution.py:484
  303.6 14.8 %collective-permute-start.25 = (bf16[32,1024]{1,0:T(8,128)(2,1)S(1)}, bf16[32,1024]{1,0:T(8,128)(2,1)S(1)}, u32[]{:S(2)}, u32[]{:S(2)}) collective-permute-start(bf16[32,1024]{1,0:T(8,128)(2,1)S(1)} %get-tuple-element.58), channel_id=1, source_target_pairs={{0,16},{1,17},{2,18},{3,19},{4,20},{5,21},{6,22},{7,23},{8,24},{9,... | collective-permute-start | bytes 196616 | tf_op jit(solution)/shard_map/ppermute | solution.py:484
  305.3 24.3 %copy-start.13 = (bf16[512,1024]{1,0:T(8,128)(2,1)S(1)}, bf16[512,1024]{1,0:T(8,128)(2,1)}, u32[]{:S(2)}) copy-start(bf16[512,1024]{1,0:T(8,128)(2,1)} %get-tuple-element.64) | copy-start | bytes 3145732
  305.3 24.4 %copy-start.12 = (bf16[128,4096]{1,0:T(8,128)(2,1)S(1)}, bf16[128,4096]{1,0:T(8,128)(2,1)}, u32[]{:S(2)}) copy-start(bf16[128,4096]{1,0:T(8,128)(2,1)} %get-tuple-element.72) | copy-start | bytes 3145732
  305.5 24.8 %collective-permute-start.12 = (bf16[256,768]{1,0:T(8,128)(2,1)S(1)}, bf16[256,768]{1,0:T(8,128)(2,1)S(1)}, u32[]{:S(2)}, u32[]{:S(2)}) collective-permute-start(bf16[256,768]{1,0:T(8,128)(2,1)S(1)} %fusion.43), channel_id=1, source_target_pairs={{0,16},{1,17},{2,18},{3,19},{4,20},{5,21},{6,22},{7,23},{8,24},{9,... | collective-permute-start | bytes 1179656 | tf_op jit(solution)/shard_map/ppermute | solution.py:484
  318.5 13.9 %slice-start.1 = ((s8[8388608]{0:T(1024)(128)(4,1)}), s8[4194304]{0:T(1024)(128)(4,1)S(1)}, s32[]{:S(2)}) async-start(s8[8388608]{0:T(1024)(128)(4,1)} %bitcast.39), calls=%async_computation.1 | async-start | bytes 8388608
  318.5 11.1 %collective-permute-start.26 = (bf16[64,1024]{1,0:T(8,128)(2,1)S(1)}, bf16[64,1024]{1,0:T(8,128)(2,1)S(1)}, u32[]{:S(2)}, u32[]{:S(2)}) collective-permute-start(bf16[64,1024]{1,0:T(8,128)(2,1)S(1)} %constant_dynamic-update-slice_fusion.4), channel_id=1, source_target_pairs={{0,8},{1,9},{2,10},{3,11},{4,12},{5,13},{6,14},{7,15},{8,0},{9,1},... | collective-permute-start | bytes 393224 | tf_op jit(solution)/shard_map/ppermute | solution.py:484
  318.6 18.5 %slice-start.4 = ((s8[8388608]{0:T(1024)(128)(4,1)}), s8[4194304]{0:T(1024)(128)(4,1)S(1)}, s32[]{:S(2)}) async-start(s8[8388608]{0:T(1024)(128)(4,1)} %bitcast.43), calls=%async_computation.4 | async-start | bytes 8388608
  329.6 2.7 collective-permute-start.41
  329.7 4.3 collective-permute-start.28
  330.3 5.1 collective-permute-start.32
  330.4 6.5 %collective-permute-start.30 = (bf16[128,4096]{1,0:T(8,128)(2,1)S(1)}, bf16[128,4096]{1,0:T(8,128)(2,1)}, u32[]{:S(2)}, u32[]{:S(2)}) collective-permute-start(bf16[128,4096]{1,0:T(8,128)(2,1)S(1)} %get-tuple-element.71), channel_id=1, source_target_pairs={{0,1},{1,0},{2,3},{3,2},{4,5},{5,4},{6,7},{7,6},{8,9},{9,8},{10,11... | collective-permute-start | bytes 3145736 | tf_op jit(solution)/shard_map/ppermute | solution.py:484
  331.7 18.5 %collective-permute-start.27 = (bf16[128,4096]{1,0:T(8,128)(2,1)S(1)}, bf16[128,4096]{1,0:T(8,128)(2,1)}, u32[]{:S(2)}, u32[]{:S(2)}) collective-permute-start(bf16[128,4096]{1,0:T(8,128)(2,1)S(1)} %get-tuple-element.69), channel_id=1, source_target_pairs={{0,1},{1,0},{2,3},{3,2},{4,5},{5,4},{6,7},{7,6},{8,9},{9,8},{10,11... | collective-permute-start | bytes 3145736 | tf_op jit(solution)/shard_map/ppermute | solution.py:484
  332.2 18.0 %collective-permute-start.38 = (bf16[512,1024]{1,0:T(8,128)(2,1)S(1)}, bf16[512,1024]{1,0:T(8,128)(2,1)}, u32[]{:S(2)}, u32[]{:S(2)}) collective-permute-start(bf16[512,1024]{1,0:T(8,128)(2,1)S(1)} %get-tuple-element.62), channel_id=1, source_target_pairs={{0,1},{1,0},{2,3},{3,2},{4,5},{5,4},{6,7},{7,6},{8,9},{9,8},{10,11... | collective-permute-start | bytes 3145736 | tf_op jit(solution)/shard_map/ppermute | solution.py:484
  334.0 6.0 %collective-permute-start.6 = (bf16[512,1024]{1,0:T(8,128)(2,1)}, bf16[512,1024]{1,0:T(8,128)(2,1)S(1)}, u32[]{:S(2)}, u32[]{:S(2)}) collective-permute-start(bf16[512,1024]{1,0:T(8,128)(2,1)} %convolution_convert_fusion.3), channel_id=1, source_target_pairs={{0,1},{1,0},{2,3},{3,2},{4,5},{5,4},{6,7},{7,6},{8,9},{9,8},{10,11... | collective-permute-start | bytes 3145736 | tf_op jit(solution)/shard_map/ppermute | solution.py:484
  335.4 11.2 %collective-permute-start.13 = (bf16[256,768]{1,0:T(8,128)(2,1)S(1)}, bf16[256,768]{1,0:T(8,128)(2,1)S(1)}, u32[]{:S(2)}, u32[]{:S(2)}) collective-permute-start(bf16[256,768]{1,0:T(8,128)(2,1)S(1)} %add_convert_fusion.10), channel_id=1, source_target_pairs={{0,8},{1,9},{2,10},{3,11},{4,12},{5,13},{6,14},{7,15},{8,0},{9,1},... | collective-permute-start | bytes 1179656 | tf_op jit(solution)/shard_map/ppermute | solution.py:484
  336.9 10.8 %collective-permute-start.14 = (bf16[128,768]{1,0:T(8,128)(2,1)S(1)}, bf16[128,768]{1,0:T(8,128)(2,1)S(1)}, u32[]{:S(2)}, u32[]{:S(2)}) collective-permute-start(bf16[128,768]{1,0:T(8,128)(2,1)S(1)} %constant_dynamic-slice_fusion.13), channel_id=1, source_target_pairs={{0,1},{1,0},{2,3},{3,2},{4,5},{5,4},{6,7},{7,6},{8,9},{9,8},{10,11... | collective-permute-start | bytes 589832 | tf_op jit(solution)/shard_map/ppermute | solution.py:484
  340.1 27.0 %collective-permute-start.33 = (bf16[128,4096]{1,0:T(8,128)(2,1)S(1)}, bf16[128,4096]{1,0:T(8,128)(2,1)S(1)}, u32[]{:S(2)}, u32[]{:S(2)}) collective-permute-start(bf16[128,4096]{1,0:T(8,128)(2,1)S(1)} %get-tuple-element.74), channel_id=1, source_target_pairs={{0,6},{1,7},{2,4},{3,5},{4,2},{5,3},{6,0},{7,1},{8,14},{9,15},{10,... | collective-permute-start | bytes 3145736 | tf_op jit(solution)/shard_map/ppermute | solution.py:484
  346.5 43.1 %collective-permute-start.31 = (bf16[128,4096]{1,0:T(8,128)(2,1)S(1)}, bf16[128,4096]{1,0:T(8,128)(2,1)S(1)}, u32[]{:S(2)}, u32[]{:S(2)}) collective-permute-start(bf16[128,4096]{1,0:T(8,128)(2,1)S(1)} %get-tuple-element.75), channel_id=1, source_target_pairs={{0,4},{1,5},{2,6},{3,7},{4,0},{5,1},{6,2},{7,3},{8,12},{9,13},{10,... | collective-permute-start | bytes 3145736 | tf_op jit(solution)/shard_map/ppermute | solution.py:484
  347.7 1.5 collective-permute-start.15
  349.2 41.5 %collective-permute-start.29 = (bf16[128,4096]{1,0:T(8,128)(2,1)S(1)}, bf16[128,4096]{1,0:T(8,128)(2,1)S(1)}, u32[]{:S(2)}, u32[]{:S(2)}) collective-permute-start(bf16[128,4096]{1,0:T(8,128)(2,1)S(1)} %get-tuple-element.73), channel_id=1, source_target_pairs={{0,2},{1,3},{2,0},{3,1},{4,6},{5,7},{6,4},{7,5},{8,10},{9,11},{10,... | collective-permute-start | bytes 3145736 | tf_op jit(solution)/shard_map/ppermute | solution.py:484
  350.1 43.0 %copy-start.10 = (f32[128,3072]{1,0:T(8,128)}, f32[128,3072]{1,0:T(8,128)S(1)}, u32[]{:S(2)}) copy-start(f32[128,3072]{1,0:T(8,128)S(1)} %convert_dynamic-update-slice_fusion.6) | copy-start | bytes 4718596
  350.2 87.5 %collective-permute-start.5 = (bf16[512,1024]{1,0:T(8,128)(2,1)S(1)}, bf16[512,1024]{1,0:T(8,128)(2,1)S(1)}, u32[]{:S(2)}, u32[]{:S(2)}) collective-permute-start(bf16[512,1024]{1,0:T(8,128)(2,1)S(1)} %copy-done.22), channel_id=1, source_target_pairs={{0,1},{1,0},{2,3},{3,2},{4,5},{5,4},{6,7},{7,6},{8,9},{9,8},{10,11... | collective-permute-start | bytes 3145736 | tf_op jit(solution)/shard_map/ppermute | solution.py:484
  350.3 61.8 %collective-permute-start.44 = (bf16[512,1024]{1,0:T(8,128)(2,1)S(1)}, bf16[512,1024]{1,0:T(8,128)(2,1)S(1)}, u32[]{:S(2)}, u32[]{:S(2)}) collective-permute-start(bf16[512,1024]{1,0:T(8,128)(2,1)S(1)} %get-tuple-element.67), channel_id=1, source_target_pairs={{0,6},{1,7},{2,4},{3,5},{4,2},{5,3},{6,0},{7,1},{8,14},{9,15},{10,... | collective-permute-start | bytes 3145736 | tf_op jit(solution)/shard_map/ppermute | solution.py:484
  367.1 66.8 %collective-permute-start.42 = (bf16[512,1024]{1,0:T(8,128)(2,1)S(1)}, bf16[512,1024]{1,0:T(8,128)(2,1)S(1)}, u32[]{:S(2)}, u32[]{:S(2)}) collective-permute-start(bf16[512,1024]{1,0:T(8,128)(2,1)S(1)} %get-tuple-element.68), channel_id=1, source_target_pairs={{0,4},{1,5},{2,6},{3,7},{4,0},{5,1},{6,2},{7,3},{8,12},{9,13},{10,... | collective-permute-start | bytes 3145736 | tf_op jit(solution)/shard_map/ppermute | solution.py:484
  389.6 44.3 %collective-permute-start.40 = (bf16[512,1024]{1,0:T(8,128)(2,1)S(1)}, bf16[512,1024]{1,0:T(8,128)(2,1)S(1)}, u32[]{:S(2)}, u32[]{:S(2)}) collective-permute-start(bf16[512,1024]{1,0:T(8,128)(2,1)S(1)} %get-tuple-element.66), channel_id=1, source_target_pairs={{0,2},{1,3},{2,0},{3,1},{4,6},{5,7},{6,4},{7,5},{8,10},{9,11},{10,... | collective-permute-start | bytes 3145736 | tf_op jit(solution)/shard_map/ppermute | solution.py:484
  390.7 47.0 %collective-permute-start.7 = (bf16[512,1024]{1,0:T(8,128)(2,1)S(1)}, bf16[512,1024]{1,0:T(8,128)(2,1)S(1)}, u32[]{:S(2)}, u32[]{:S(2)}) collective-permute-start(bf16[512,1024]{1,0:T(8,128)(2,1)S(1)} %add_convert_fusion.7), channel_id=1, source_target_pairs={{0,8},{1,9},{2,10},{3,11},{4,12},{5,13},{6,14},{7,15},{8,0},{9,1},... | collective-permute-start | bytes 3145736 | tf_op jit(solution)/shard_map/ppermute | solution.py:484
  394.0 43.7 %copy-start.4 = (bf16[512,1024]{1,0:T(8,128)(2,1)S(1)}, bf16[512,1024]{1,0:T(8,128)(2,1)}, u32[]{:S(2)}) copy-start(bf16[512,1024]{1,0:T(8,128)(2,1)} %get-tuple-element.28) | copy-start | bytes 3145732
  412.1 78.3 %collective-permute-start.34 = (bf16[64,4096]{1,0:T(8,128)(2,1)}, bf16[64,4096]{1,0:T(8,128)(2,1)}, u32[]{:S(2)}, u32[]{:S(2)}) collective-permute-start(bf16[64,4096]{1,0:T(8,128)(2,1)} %dynamic-slice_convert_fusion.1), channel_id=1, source_target_pairs={{0,8},{1,9},{2,10},{3,11},{4,12},{5,13},{6,14},{7,15},{8,0},{9,1},... | collective-permute-start | bytes 1572872 | tf_op jit(solution)/shard_map/ppermute | solution.py:484
  437.2 55.4 %collective-permute-start.45 = (bf16[256,1024]{1,0:T(8,128)(2,1)}, bf16[256,1024]{1,0:T(8,128)(2,1)}, u32[]{:S(2)}, u32[]{:S(2)}) collective-permute-start(bf16[256,1024]{1,0:T(8,128)(2,1)} %dynamic-slice_convert_fusion), channel_id=1, source_target_pairs={{0,8},{1,9},{2,10},{3,11},{4,12},{5,13},{6,14},{7,15},{8,0},{9,1},... | collective-permute-start | bytes 1572872 | tf_op jit(solution)/shard_map/ppermute | solution.py:484
  442.1 97.7 %collective-permute-start.8 = (bf16[512,1024]{1,0:T(8,128)(2,1)}, bf16[512,1024]{1,0:T(8,128)(2,1)S(1)}, u32[]{:S(2)}, u32[]{:S(2)}) collective-permute-start(bf16[512,1024]{1,0:T(8,128)(2,1)} %get-tuple-element.76), channel_id=1, source_target_pairs={{0,0},{1,16},{2,2},{3,18},{4,4},{5,20},{6,6},{7,22},{8,8},{9,24},{... | collective-permute-start | bytes 3145736 | tf_op jit(solution)/shard_map/ppermute | solution.py:484
  491.7 19.2 %collective-permute-start.35 = (bf16[32,4096]{1,0:T(8,128)(2,1)S(1)}, bf16[32,4096]{1,0:T(8,128)(2,1)S(1)}, u32[]{:S(2)}, u32[]{:S(2)}) collective-permute-start(bf16[32,4096]{1,0:T(8,128)(2,1)S(1)} %dynamic-slice_convert_fusion.6), channel_id=1, source_target_pairs={{0,16},{1,17},{2,18},{3,19},{4,20},{5,21},{6,22},{7,23},{8,24},{9,... | collective-permute-start | bytes 786440 | tf_op jit(solution)/shard_map/ppermute | solution.py:484
  493.8 28.3 %collective-permute-start.46 = (bf16[128,1024]{1,0:T(8,128)(2,1)S(1)}, bf16[128,1024]{1,0:T(8,128)(2,1)S(1)}, u32[]{:S(2)}, u32[]{:S(2)}) collective-permute-start(bf16[128,1024]{1,0:T(8,128)(2,1)S(1)} %dynamic-slice_convert_fusion.5), channel_id=1, source_target_pairs={{0,16},{1,17},{2,18},{3,19},{4,20},{5,21},{6,22},{7,23},{8,24},{9,... | collective-permute-start | bytes 786440 | tf_op jit(solution)/shard_map/ppermute | solution.py:484
  511.0 22.4 %collective-permute-start.36 = (bf16[32,4096]{1,0:T(8,128)(2,1)S(1)}, bf16[32,4096]{1,0:T(8,128)(2,1)S(1)}, u32[]{:S(2)}, u32[]{:S(2)}) collective-permute-start(bf16[32,4096]{1,0:T(8,128)(2,1)S(1)} %get-tuple-element.56), channel_id=1, source_target_pairs={{0,16},{1,17},{2,18},{3,19},{4,20},{5,21},{6,22},{7,23},{8,24},{9,... | collective-permute-start | bytes 786440 | tf_op jit(solution)/shard_map/ppermute | solution.py:484
  522.3 16.7 %collective-permute-start.47 = (bf16[128,1024]{1,0:T(8,128)(2,1)S(1)}, bf16[128,1024]{1,0:T(8,128)(2,1)S(1)}, u32[]{:S(2)}, u32[]{:S(2)}) collective-permute-start(bf16[128,1024]{1,0:T(8,128)(2,1)S(1)} %get-tuple-element.54), channel_id=1, source_target_pairs={{0,16},{1,17},{2,18},{3,19},{4,20},{5,21},{6,22},{7,23},{8,24},{9,... | collective-permute-start | bytes 786440 | tf_op jit(solution)/shard_map/ppermute | solution.py:484
  533.4 16.8 %collective-permute-start.37 = (bf16[64,4096]{1,0:T(8,128)(2,1)S(1)}, bf16[64,4096]{1,0:T(8,128)(2,1)S(1)}, u32[]{:S(2)}, u32[]{:S(2)}) collective-permute-start(bf16[64,4096]{1,0:T(8,128)(2,1)S(1)} %constant_dynamic-update-slice_fusion.2), channel_id=1, source_target_pairs={{0,8},{1,9},{2,10},{3,11},{4,12},{5,13},{6,14},{7,15},{8,0},{9,1},... | collective-permute-start | bytes 1572872 | tf_op jit(solution)/shard_map/ppermute | solution.py:484
  539.1 22.3 %collective-permute-start.48 = (bf16[256,1024]{1,0:T(8,128)(2,1)S(1)}, bf16[256,1024]{1,0:T(8,128)(2,1)S(1)}, u32[]{:S(2)}, u32[]{:S(2)}) collective-permute-start(bf16[256,1024]{1,0:T(8,128)(2,1)S(1)} %constant_dynamic-update-slice_fusion), channel_id=1, source_target_pairs={{0,8},{1,9},{2,10},{3,11},{4,12},{5,13},{6,14},{7,15},{8,0},{9,1},... | collective-permute-start | bytes 1572872 | tf_op jit(solution)/shard_map/ppermute | solution.py:484
  550.3 14.2 %copy-start.9 = (f32[128,4096]{1,0:T(8,128)}, f32[128,4096]{1,0:T(8,128)S(1)}, u32[]{:S(2)}) copy-start(f32[128,4096]{1,0:T(8,128)S(1)} %convert_dynamic-update-slice_fusion.2) | copy-start | bytes 6291460
  (23 other events, 95.6 us)

commit v3 on v2

v3 whole, which is shorter than its diff:
```python
import functools

import jax
import jax.numpy as jnp
from jax import lax
from jax.experimental import pallas as pl
from jax.experimental.pallas import tpu as pltpu
from jax.sharding import PartitionSpec as P

HEADS = 16
EPS = 1e-05
NEG = -1e30
F32 = jnp.float32
BF = jnp.bfloat16


def _dot(a, b, ca, cb):
    return lax.dot_general(a, b, (((ca,), (cb,)), ((), ())), preferred_element_type=F32)


def mm(a, b):
    return _dot(a, b, 1, 0)


def mm_left(a, b):
    return _dot(a, b, 0, 0)


def mm_right(a, b):
    return _dot(a, b, 1, 1)


MESH = pl.DeviceIdType.MESH


def front_kernel(
    tok, cot, win, wo, we, wr, vec, st,
    x_ref, g_ref, gp_ref, n1t, wf, wof, wef, wrf, vecs, qkv, att, lse, attn,
    n1, qt, vt, win_s, win_r, vec_s, vec_r, tok_s, tok_r, tok_l, near_s, near_r, core_s, core_r, fwd_s, fwd_r,
    cot_s, cot_r, cot_l, gp_s, gp_r, own_l, w_s, w_r, move_s, move_r, move_l,
    *, ns, nd, heads, d, bq, bk, chunks,
):
    seq, me = lax.axis_index("seq"), lax.axis_index("dp")
    half, nearb, core = seq // 2, seq % 2, me % 2
    member = 2 * core + nearb
    n_rows, width = tok.shape
    group = width // 4
    small_rows = win.shape[0]
    stays = half == core
    swap_to = (2 * core + nearb, me - core + half)
    near_to = (seq + 1 - 2 * nearb, me)
    core_to = (seq, me + 1 - 2 * core)

    def offset(k):
        out = me
        bit = 1
        while bit <= k:
            if k & bit:
                out = out + bit - 2 * bit * ((me // bit) % 2)
            bit *= 2
        return out

    def rcopy(src, dst, ss, rs, dev):
        return pltpu.make_async_remote_copy(
            src_ref=src, dst_ref=dst, send_sem=ss, recv_sem=rs, device_id=dev, device_id_type=MESH
        )

    barrier = pltpu.get_barrier_semaphore()

    def hello(dev):
        pl.semaphore_signal(barrier, inc=1, device_id=dev, device_id_type=MESH)

    for k in range(1, nd):
        hello((seq, offset(k)))
    hello(near_to)
    hello((near_to[0], core_to[1]))

    @pl.when(jnp.logical_not(stays))
    def _():
        hello(swap_to)
        pl.semaphore_wait(barrier, nd + 2)

    @pl.when(stays)
    def _():
        pl.semaphore_wait(barrier, nd + 1)

    sends = []

    step = n_rows // chunks
    tok_remote, tok_local = [], []
    for c in range(chunks):
        cut = pl.ds(c * step, step)
        tok_remote.append(rcopy(tok.at[cut], x_ref.at[cut], tok_s.at[c], tok_r.at[c], swap_to))
        tok_local.append(pltpu.make_async_copy(tok.at[cut], x_ref.at[cut], tok_l.at[c]))

    @pl.when(jnp.logical_not(stays))
    def _():
        for c in tok_remote:
            c.start()

    @pl.when(stays)
    def _():
        for c in tok_local:
            c.start()

    vec_copies, win_copies, own_copies = [], [], []
    for k in range(1, nd):
        c = rcopy(vec, vecs.at[me], vec_s.at[k], vec_r.at[k], (seq, offset(k)))
        c.start()
        vec_copies.append(c)
    c = pltpu.make_async_copy(vec, vecs.at[me], own_l.at[0])
    c.start()
    vec_copies.append(c)
    my_rows = pl.ds(pl.multiple_of(me * small_rows, small_rows), small_rows)
    for k in range(nd):
        target = 2 * (core if k % 2 == 0 else 1 - core) + nearb
        for i in range(3):
            src = win.at[:, pl.ds(pl.multiple_of(i * width + target * group, 128), group)]
            dst = wf.at[my_rows, pl.ds(i * group, group)]
            if k == 0:
                c = pltpu.make_async_copy(src, dst, own_l.at[1 + i])
            else:
                c = rcopy(src, dst, win_s.at[k, i], win_r.at[k, i], (seq, offset(k)))
            c.start()
            win_copies.append(c)

    pairs = ((wo, wof), (we, wef), (wr, wrf))

    def source(a, k):
        return we.at[core if k % 2 == 0 else 1 - core] if a == 1 else pairs[a][0]

    def at(a, k, part=None):
        high = pairs[a][0].shape[-2]
        row = (offset(k) // 2 if a == 2 else offset(k)) * high
        if part is None:
            return pairs[a][1].at[pl.ds(pl.multiple_of(row, high), high)]
        return pairs[a][1].at[pl.ds(pl.multiple_of(row + part * (high // 2), high // 2), high // 2)]

    held = {}

    def send(a, slot, src, dst, k):
        c = rcopy(src, dst, w_s.at[a, slot], w_r.at[a, slot], (seq, offset(k)))
        c.start()
        held[a, slot] = c

    direct = (2, 3, 4, 5) if nd == 8 else range(2, nd)

    def weights_start(a):
        for k in direct:
            if k % 2 == 0 or a == 1:
                send(a, k, source(a, k), at(a, 0), k)
        if a < 2:
            send(a, 1, source(a, 1), at(a, 0), 1)
        c = pltpu.make_async_copy(source(a, 0), at(a, 0), own_l.at[4 + a])
        c.start()
        held[a, "own"] = c

    def weights_forward(a):
        for k in direct:
            if k % 2 == 0 or a == 1:
                held[a, k].wait_recv()
                if nd == 8:
                    send(a, 8 + k, at(a, k, k // 4), at(a, k, k // 4), 6 - k // 2 * 2)
                if a == 0:
                    send(a, k + 1 if nd > 8 else 14 + k // 2, at(a, k), at(a, k), 1)

    def weights_last(a):
        if nd == 8 and a == 0:
            for part, k in ((0, 2), (1, 4)):
                held[a, 8 + k].wait_recv()
                send(a, 3 + 2 * part, at(a, 6, part), at(a, 6, part), 1)

    def weights_end(a):
        held[a, "own"].wait()
        waited = set(direct) if a else {k for k in direct if k % 2 == 0}
        if nd == 8 and a == 0:
            waited |= {10, 12}
        for (b, slot), c in held.items():
            if b == a and slot != "own":
                if slot not in waited:
                    c.wait_recv()
                c.wait_send()

    for c in vec_copies[:-1]:
        c.wait_recv()
        sends.append(c)
    vec_copies[-1].wait()

    def vector(i):
        return jnp.concatenate([vecs[k, i : i + 1, :] for k in range(nd)], axis=1).astype(F32)

    gain, shift = vector(0), vector(1)
    near_copies, core_copies = [], []
    for c in range(chunks):
        cut = pl.ds(c * step, step)

        @pl.when(jnp.logical_not(stays))
        def _(c=c):
            tok_remote[c].wait_recv()

        @pl.when(stays)
        def _(c=c):
            tok_local[c].wait()

        value = x_ref[cut, :].astype(F32)
        center = value - jnp.mean(value, axis=-1, keepdims=True)
        spread = jnp.mean(center * center, axis=-1, keepdims=True)
        place = pl.ds(pl.multiple_of(member * n_rows + c * step, step), step)
        n1[place, :] = (center * lax.rsqrt(spread + EPS) * gain + shift).astype(BF)
        r = rcopy(n1.at[place], n1.at[place], near_s.at[c], near_r.at[c], near_to)
        r.start()
        near_copies.append(r)
        r = rcopy(n1.at[place], n1.at[place], core_s.at[c], core_r.at[c], core_to)
        r.start()
        core_copies.append(r)

    for c in win_copies[:3]:
        c.wait()
    for c in win_copies[3:]:
        c.wait_recv()
        sends.append(c)
    for a in range(3):
        weights_start(a)

    def project(block, c=None):
        size = n_rows if c is None else step
        place = pl.ds(pl.multiple_of(block * n_rows + (0 if c is None else c * step), size), size)
        mixed = _dot(n1[place, :], wf[...], 1, 0).astype(BF)
        qkv[place, :] = mixed
        n1t[:, place] = jnp.transpose(n1[place, :])
        qt[:, place] = jnp.transpose(mixed[:, :group])
        vt[:, place] = jnp.transpose(mixed[:, 2 * group :])

    project(member)
    for c in core_copies:
        c.wait_recv()
        sends.append(c)
    twin = 2 * (1 - core) + nearb
    project(twin)
    fwd_copies = []
    beside = 2 * core + 1 - nearb
    across = 2 * (1 - core) + 1 - nearb
    for c in range(chunks):
        near_copies[c].wait_recv()
        sends.append(near_copies[c])
        place = pl.ds(pl.multiple_of(beside * n_rows + c * step, step), step)
        r = rcopy(n1.at[place], n1.at[place], fwd_s.at[c], fwd_r.at[c], core_to)
        r.start()
        fwd_copies.append(r)
    project(beside)
    for c in fwd_copies:
        c.wait_recv()
        sends.append(c)
    project(across)

    cot_remote = rcopy(cot, g_ref, cot_s, cot_r, swap_to)
    cot_local = pltpu.make_async_copy(cot, g_ref, cot_l)

    @pl.when(jnp.logical_not(stays))
    def _():
        cot_remote.start()

    @pl.when(stays)
    def _():
        cot_local.start()

    n = ns * n_rows
    scale = d**-0.5
    w = 2 * d
    moves = []
    for i in range(n // bq):
        cs = slice(i * bq, (i + 1) * bq)

        def pair(p, carry, i=i, cs=cs):
            lanes = pl.ds(pl.multiple_of(p * w, w), w)
            key_lanes = pl.ds(pl.multiple_of(group + p * w, w), w)
            outs = []
            for h in range(2):
                row = lax.broadcasted_iota(jnp.int32, (w, bq), 0)
                qm = jnp.where((row >= h * d) & (row < (h + 1) * d), qt[lanes, cs], jnp.zeros((), BF))
                m = jnp.full((1, bq), NEG, F32)
                l = jnp.zeros((1, bq), F32)
                acc = jnp.zeros((d, bq), F32)
                for j in range(0, (i + 1) * bq, bk):
                    s = _dot(qkv[j : j + bk, key_lanes], qm, 1, 0) * scale
                    key = lax.broadcasted_iota(jnp.int32, (bk, bq), 0) + j
                    ok = key >= st[:, cs]
                    if j + bk > i * bq:
                        ok = ok & (key <= lax.broadcasted_iota(jnp.int32, (bk, bq), 1) + i * bq)
                    s = jnp.where(ok, s, NEG)
                    mn = jnp.maximum(m, jnp.max(s, axis=0, keepdims=True))
                    e = jnp.exp(s - mn)
                    a = jnp.exp(m - mn)
                    l = a * l + jnp.sum(e, axis=0, keepdims=True)
                    rows_h = pl.ds(pl.multiple_of(p * w + h * d, d), d)
                    acc = a * acc + _dot(vt[rows_h, j : j + bk], e.astype(BF), 1, 0)
                    m = mn
                outs.append(acc / l)
                lse[p, h : h + 1, cs] = m + jnp.log(l)
            att[cs, lanes] = jnp.transpose(jnp.concatenate(outs, axis=0)).astype(BF)
            return carry

        lax.fori_loop(0, heads // 2, pair, 0)
        mine = attn.at[:, pl.ds(pl.multiple_of(member * group, group), group)]
        dev = (seq - nearb + i % 2, me - core + i // 2)
        r = rcopy(att.at[cs], mine, move_s.at[i], move_r.at[member], dev)
        keep = pltpu.make_async_copy(att.at[cs], mine, move_l)
        moves.append((r, keep))

        @pl.when(member != i)
        def _(r=r):
            r.start()

        @pl.when(member == i)
        def _(keep=keep):
            keep.start()

        if i < 3:
            weights_forward(i)
    weights_last(0)

    @pl.when(jnp.logical_not(stays))
    def _():
        cot_remote.wait_recv()

    @pl.when(stays)
    def _():
        cot_local.wait()

    twin_cot = rcopy(g_ref, gp_ref, gp_s, gp_r, core_to)
    twin_cot.start()
    for a in range(3):
        weights_end(a)
    for i, (r, keep) in enumerate(moves):
        source = attn.at[:, pl.ds(i * group, group)]
        arrival = pltpu.make_async_copy(source, source, move_r.at[i])

        @pl.when(member != i)
        def _(r=r, arrival=arrival):
            r.wait_send()
            arrival.wait()

        @pl.when(member == i)
        def _(keep=keep):
            keep.wait()

    @pl.when(jnp.logical_not(stays))
    def _():
        cot_remote.wait_send()
        for c in tok_remote:
            c.wait_send()

    twin_cot.wait()
    for c in sends:
        c.wait_send()


def front(tok, cot, win, wo, we, wr, vec, starts, ns, nd, heads, d):
    n_rows, width = tok.shape
    n, group, chunks = n_rows * ns, width // 4, 4
    slots = 17 if nd == 8 else nd
    compact = lambda a: jax.ShapeDtypeStruct((a.shape[0] * (nd // 2), a.shape[1]), BF)
    any_, vmem = pl.BlockSpec(memory_space=pl.ANY), pl.BlockSpec(memory_space=pltpu.VMEM)
    full = lambda a: jax.ShapeDtypeStruct((a.shape[0] * nd, a.shape[1]), BF)
    dma = lambda *shape: pltpu.SemaphoreType.DMA(shape)
    sds = jax.ShapeDtypeStruct
    return pl.pallas_call(
        functools.partial(front_kernel, ns=ns, nd=nd, heads=heads, d=d, bq=n_rows, bk=n_rows, chunks=chunks),
        in_specs=[any_] * 7 + [vmem],
        out_specs=[vmem, any_, any_, vmem, vmem, any_, any_, any_, vmem, vmem, vmem, vmem, vmem],
        out_shape=[
            sds(tok.shape, BF), sds(tok.shape, BF), sds(tok.shape, BF), sds((width, n), BF), sds((width, 3 * group), BF),
            full(wo), sds((width, we.shape[2]), BF), compact(wr), sds((nd, *vec.shape), BF), sds((n, 3 * group), BF),
            sds((n, group), BF), sds((heads // 2, 2, n), F32), sds(tok.shape, BF),
        ],
        scratch_shapes=[
            pltpu.VMEM((n, width), BF), pltpu.VMEM((group, n), BF), pltpu.VMEM((group, n), BF),
            dma(nd, 3), dma(nd, 3), dma(nd), dma(nd), dma(chunks), dma(chunks), dma(chunks),
            dma(chunks), dma(chunks), dma(chunks), dma(chunks), dma(chunks), dma(chunks),
            pltpu.SemaphoreType.DMA, pltpu.SemaphoreType.DMA, pltpu.SemaphoreType.DMA,
            pltpu.SemaphoreType.DMA, pltpu.SemaphoreType.DMA, dma(7), dma(3, slots), dma(3, slots), dma(4), dma(4), pltpu.SemaphoreType.DMA,
        ],
        compiler_params=pltpu.CompilerParams(
            collective_id=0, has_side_effects=True, vmem_limit_bytes=52 << 20
        ),
        cost_estimate=pl.CostEstimate(
            flops=8 * n * n * d * heads, bytes_accessed=60_000_000, transcendentals=n * n * heads
        ),
    )(tok, cot, win, wo, we, wr, vec, starts)


def back_kernel(
    ga, qkv, att, lse, st, n1t, wf, x, gres, gain, v_in, res, dwr, dwe, dwo,
    out, tg, insum, osum, esum, rsum, vout,
    go, qt, dot, kt, dqt, delta, gm, zin, far_in, tot, tot2, near_in, core_in, cst, crc, nst, nrc, tgs,
    vmine, vrc, vz, own, fwd, r1, r2, ns_st, ns_rc, keep, fs_st, fs_rc, fb, eb,
    move_s, move_r, move_l, a_s, a_r, a_l, d_s, d_r, out_s, out_r, out_l, tg_s, tg_r, tg_l, v_s, v_r, vz_s, vz_r,
    *, ns, nd, heads, d, bq, bk, chunks,
):
    seq, me = lax.axis_index("seq"), lax.axis_index("dp")
    half, nearb, core = seq // 2, seq % 2, me % 2
    member = 2 * core + nearb
    beside, twin, across = 2 * core + 1 - nearb, 2 * (1 - core) + nearb, 2 * (1 - core) + 1 - nearb
    n_rows, width = x.shape
    n, group, ncol = ns * n_rows, width // 4, nd // 2
    stays = half == core
    swap_to = (2 * core + nearb, me - core + half)
    near_to = (seq + 1 - 2 * nearb, me)
    far_to = (seq + 2 - 4 * half, me)
    third_to = (seq + 1 - 2 * nearb + 2 - 4 * half, me)
    core_to = (seq, me + 1 - 2 * core)

    def offset(k):
        result = me
        bit = 1
        while bit <= k:
            if k & bit:
                result = result + bit - 2 * bit * ((me // bit) % 2)
            bit *= 2
        return result

    def rcopy(src, dst, ss, rs, dev):
        return pltpu.make_async_remote_copy(
            src_ref=src, dst_ref=dst, send_sem=ss, recv_sem=rs, device_id=dev, device_id_type=MESH
        )

    def row_loop(total, size, body):
        def one(t, carry):
            body(pl.multiple_of(t * size, size))
            return carry

        lax.fori_loop(0, total // size, one, 0)

    barrier = pltpu.get_barrier_semaphore()

    def hello(dev):
        pl.semaphore_signal(barrier, inc=1, device_id=dev, device_id_type=MESH)

    for k in range(1, nd):
        hello((seq, offset(k)))
    for dev in (near_to, far_to, third_to, (near_to[0], core_to[1])):
        hello(dev)

    @pl.when(jnp.logical_not(stays))
    def _():
        hello(swap_to)
        pl.semaphore_wait(barrier, nd + 4)

    @pl.when(stays)
    def _():
        pl.semaphore_wait(barrier, nd + 3)

    sends = []
    held = {}

    moves = []
    for i in range(4):
        src = ga.at[:, pl.ds(i * group, group)]
        mine = go.at[pl.ds(pl.multiple_of(member * n_rows, n_rows), n_rows)]
        dev = (seq - nearb + i % 2, me - core + i // 2)
        r = rcopy(src, mine, move_s.at[i], move_r.at[member], dev)
        stay = pltpu.make_async_copy(src, mine, move_l)
        moves.append((r, stay))

        @pl.when(member != i)
        def _(r=r):
            r.start()

        @pl.when(member == i)
        def _(stay=stay):
            stay.start()

    terms = (dwr, dwe, dwo, zin)
    high = [t.shape[0] // ncol for t in terms]
    wide = [t.shape[1] for t in terms]

    def block(a, kc, part=None):
        row = (offset(2 * kc) // 2) * high[a]
        if part is None:
            return terms[a].at[pl.ds(pl.multiple_of(row, high[a]), high[a])]
        low = high[a] // 2
        return terms[a].at[pl.ds(pl.multiple_of(row + part * low, low), low)]

    def send(a, slot, src, dst, dev):
        c = rcopy(src, dst, a_s.at[a, slot], a_r.at[a, slot], dev)
        c.start()
        held[a, slot] = c
        sends.append(c)

    def lanes(first, size):
        return pl.ds(pl.multiple_of(first, 128), size)

    def s0(a):
        local = [pltpu.make_async_copy(block(a, 0), own[a], a_l.at[a, 0])]
        if nd == 8:
            x_to, y_to = (seq, offset(2)), (seq, offset(4))
            send(a, 0, block(a, 1, 0), r1[a].at[0], x_to)
            send(a, 2, block(a, 2, 1), r1[a].at[2], y_to)
            send(a, 1, block(a, 3, 0), r1[a].at[1], x_to)
            send(a, 3, block(a, 3, 1), r1[a].at[3], y_to)
            local.append(pltpu.make_async_copy(block(a, 2, 0), fwd[a].at[0], a_l.at[a, 1]))
            local.append(pltpu.make_async_copy(block(a, 1, 1), fwd[a].at[1], a_l.at[a, 2]))
        else:
            for kc in range(1, ncol):
                send(a, kc, block(a, kc), r1[a].at[kc - 1], (seq, offset(2 * kc)))
        for c in local:
            c.start()
        held[a, "local"] = local

    def s1(a):
        for c in held[a, "local"]:
            c.wait()
        if nd == 8:
            for part, k in ((0, 4), (1, 2)):
                held[a, 1 + 2 * part].wait_recv()

                def add(t, part=part):
                    cut = pl.ds(t, 16)
                    fwd[a][part, cut, :] = (
                        fwd[a][part, cut, :].astype(F32) + r1[a][1 + 2 * part, cut, :].astype(F32)
                    ).astype(BF)

                row_loop(high[a] // 2, 16, add)
                send(a, 4 + part, fwd[a].at[part], r2[a].at[part], (seq, offset(k)))

    def s2(a):
        c, low = wide[a], high[a] // 2
        if nd == 8:
            for slot in (0, 2, 4, 5):
                held[a, slot].wait_recv()
        else:
            for kc in range(1, ncol):
                held[a, kc].wait_recv()

        def total(part, t, cs):
            if nd == 8:
                return (
                    own[a][pl.ds(part * low + t, 16), cs].astype(F32)
                    + r1[a][2 * part, pl.ds(t, 16), cs].astype(F32)
                    + r2[a][part, pl.ds(t, 16), cs].astype(F32)
                )
            value = own[a][pl.ds(part * low + t, 16), cs].astype(F32)
            for kc in range(1, ncol):
                value = value + r1[a][kc - 1, pl.ds(part * low + t, 16), cs].astype(F32)
            return value

        for part in range(2):

            def add(t, part=part):
                cut = pl.ds(part * low + t, 16)
                if a == 3:
                    tot[cut, :] = total(part, t, slice(None)).astype(BF)
                else:
                    keep[a][cut, :] = total(part, t, lanes(nearb * (c // 2), c // 2))
                    ns_st[a][cut, :] = total(part, t, lanes((1 - nearb) * (c // 2), c // 2)).astype(BF)

            row_loop(low, 16, add)
        if a == 3:
            send(a, 6, tot, far_in, far_to)
        else:
            send(a, 6, ns_st[a], ns_rc[a], near_to)

    def s3(a):
        c = wide[a]
        held[a, 6].wait_recv()
        if a == 3:

            def add(t):
                cut = pl.ds(t, 16)
                tot2[cut, :] = (tot[cut, :].astype(F32) + far_in[cut, :].astype(F32)).astype(BF)

            row_loop(high[a], 16, add)
            send(a, 7, tot2, near_in, near_to)
            return

        def add(t):
            cut, cs = pl.ds(t, 16), lanes((1 - half) * (c // 4), c // 4)
            fs_st[a][cut, :] = (keep[a][cut, cs] + ns_rc[a][cut, cs].astype(F32)).astype(BF)

        row_loop(high[a], 16, add)
        send(a, 7, fs_st[a], fs_rc[a], far_to)

    def s4(a):
        c = wide[a]
        held[a, 7].wait_recv()
        low = high[a] // 2
        theirs = pl.ds(pl.multiple_of((1 - core) * low, low), low)
        if a == 3:
            send(a, 8, tot2.at[theirs], core_in.at[0], core_to)
            send(a, 9, near_in.at[theirs], core_in.at[1], core_to)
            return
        place = lanes(nearb * (c // 2) + half * (c // 4), c // 4)

        def add(t):
            cut, cs = pl.ds(t, 16), lanes(half * (c // 4), c // 4)
            value = keep[a][cut, cs] + ns_rc[a][cut, cs].astype(F32) + fs_rc[a][cut, :].astype(F32)
            fb[a][cut, place] = value.astype(BF)

        row_loop(high[a], 16, add)
        send(a, 8, fb[a].at[:, place], fb[a].at[:, place], far_to)

    def s5(a):
        c = wide[a]
        held[a, 8].wait_recv()
        low = high[a] // 2
        ours = pl.ds(pl.multiple_of(core * low, low), low)
        if a == 3:
            held[a, 9].wait_recv()
            for which, value in (
                (member, tot2[ours, :]), (beside, near_in[ours, :]), (twin, core_in[0]), (across, core_in[1])
            ):
                for i in range(3):
                    insum[:, lanes(i * width + which * group, group)] = value[:, i * group : (i + 1) * group]
            return
        place = lanes(nearb * (c // 2), c // 2)
        send(a, 9, fb[a].at[:, place], fb[a].at[:, place], near_to)

    def s6(a):
        held[a, 9].wait_recv()
        low = high[a] // 2
        theirs = pl.ds(pl.multiple_of((1 - core) * low, low), low)
        if a == 0:
            c = pltpu.make_async_copy(fb[a], rsum, a_l.at[a, 3])
            c.start()
            held[a, "last"] = c
        else:
            send(a, 10, fb[a].at[theirs], eb[a], core_to)

    def s7(a):
        if a == 0:
            held[a, "last"].wait()
            return
        held[a, 10].wait_recv()
        low = high[a] // 2
        ours = pl.ds(pl.multiple_of(core * low, low), low)
        if a == 2:
            size = wide[a]
            osum[:, lanes(core * size, size)] = fb[a][ours, :]
            osum[:, lanes((1 - core) * size, size)] = eb[a][...]
        else:
            size = wide[a] // ncol
            for i in range(ncol):
                cs = slice(i * size, (i + 1) * size)
                a0, a1 = fb[a][ours, cs], eb[a][:, cs]
                esum[:, 2 * i * size : (2 * i + 1) * size] = jnp.where(core == 0, a0, a1)
                esum[:, (2 * i + 1) * size : (2 * i + 2) * size] = jnp.where(core == 0, a1, a0)

    for a in range(3):
        s0(a)
    out_remote = rcopy(res, out, out_s, out_r, swap_to)
    out_local = pltpu.make_async_copy(res, out, out_l)

    @pl.when(jnp.logical_not(stays))
    def _():
        out_remote.start()

    @pl.when(stays)
    def _():
        out_local.start()

    w, scale = 2 * d, d**-0.5
    for i in range(4):
        cut = slice(i * n_rows, (i + 1) * n_rows)
        qt[:, cut] = jnp.transpose(qkv[cut, :group])
        kt[:, cut] = jnp.transpose(qkv[cut, group : 2 * group])
    dqt[...] = jnp.zeros_like(dqt)
    for i in range(4):
        cut = slice(i * n_rows, (i + 1) * n_rows)
        landing = go.at[pl.ds(i * n_rows, n_rows)]
        arrival = pltpu.make_async_copy(landing, landing, move_r.at[i])
        r, stay = moves[i]

        @pl.when(member != i)
        def _(r=r, arrival=arrival):
            arrival.wait()
            r.wait_send()

        @pl.when(member == i)
        def _(stay=stay):
            stay.wait()

    for i in range(4):
        cut = slice(i * n_rows, (i + 1) * n_rows)
        dot[:, cut] = jnp.transpose(go[cut, :])
        prod = jnp.transpose(go[cut, :].astype(F32) * att[cut, :].astype(F32))
        for h in range(heads):
            delta[h // 2, h % 2 : h % 2 + 1, cut] = jnp.sum(prod[h * d : (h + 1) * d], axis=0, keepdims=True)

    zero = jnp.zeros((), BF)
    for j in range(0, n, bk):

        def pair(p, carry, j=j):
            at = lambda first: pl.ds(pl.multiple_of(first + p * w, w), w)
            kb, vb = qkv[j : j + bk, at(group)], qkv[j : j + bk, at(2 * group)]
            dk = jnp.zeros((bk, w), F32)
            dv = jnp.zeros((bk, w), F32)
            row = lax.broadcasted_iota(jnp.int32, (w, bq), 0)
            lane = lax.broadcasted_iota(jnp.int32, (bq, w), 1)
            for i in range(j // bq, n // bq):
                cs = slice(i * bq, (i + 1) * bq)
                key = lax.broadcasted_iota(jnp.int32, (bk, bq), 0) + j
                ok = key >= st[:, cs]
                if j + bk > i * bq:
                    ok = ok & (key <= lax.broadcasted_iota(jnp.int32, (bk, bq), 1) + i * bq)
                for h in range(2):
                    rows_h = (row >= h * d) & (row < (h + 1) * d)
                    lanes_h = (lane >= h * d) & (lane < (h + 1) * d)
                    s = _dot(kb, jnp.where(rows_h, qt[at(0), cs], zero), 1, 0) * scale
                    s = jnp.where(ok, s, NEG)
                    e = jnp.exp(s - lse[p, h : h + 1, cs])
                    dp = _dot(vb, jnp.where(rows_h, dot[at(0), cs], zero), 1, 0)
                    ds = (e * (dp - delta[p, h : h + 1, cs])).astype(BF)
                    dv = dv + _dot(e.astype(BF), jnp.where(lanes_h, go[cs, at(0)], zero), 1, 0)
                    dk = dk + _dot(ds, jnp.where(lanes_h, qkv[cs, at(0)], zero), 1, 0)
                    head = pl.ds(pl.multiple_of(p * w + h * d, d), d)
                    dqt[head, cs] += _dot(kt[head, j : j + bk], ds, 1, 0)
            gm[j : j + bk, at(group)] = (dk * scale).astype(BF)
            gm[j : j + bk, at(2 * group)] = dv.astype(BF)
            return carry

        lax.fori_loop(0, heads // 2, pair, 0)
        if j == 0:
            s1(0)
        elif j == bk:
            s2(0)
        elif j == 2 * bk:
            s3(0)
    for i in range(4):
        cut = slice(i * n_rows, (i + 1) * n_rows)
        gm[cut, :group] = (jnp.transpose(dqt[:, cut]) * scale).astype(BF)

    step = n_rows // chunks

    def term(b, c):
        cut = pl.ds(pl.multiple_of(b * n_rows + c * step, step), step)
        return _dot(gm[cut, :], wf[...], 1, 1)

    quad = {}

    def quad_send(slot, src, dst, dev):
        c = rcopy(src, dst, d_s.at[slot], d_r.at[slot], dev)
        c.start()
        quad[slot] = c
        sends.append(c)

    for which, b in ((1, across), (0, twin)):
        for c in range(chunks):
            cut = pl.ds(c * step, step)
            cst[which, cut, :] = term(b, c).astype(BF)
            quad_send(which * chunks + c, cst.at[which, cut], crc.at[which, cut], core_to)
    for c in range(chunks):
        cut = pl.ds(c * step, step)
        value = term(beside, c)
        quad[chunks + c].wait_recv()
        nst[cut, :] = (value + crc[1, cut, :].astype(F32)).astype(BF)
        quad_send(2 * chunks + c, nst.at[cut], nrc.at[cut], near_to)

    s1(1)
    s1(2)
    s4(0)
    for i in range(4):
        cut = slice(i * group, (i + 1) * group)
        zin[cut, :] = _dot(n1t[cut, :], gm[...], 1, 0).astype(BF)
    s0(3)
    s5(0)

    tg_remote, tg_local = [], []
    gain_sum = jnp.zeros((1, width), F32)
    shift_sum = jnp.zeros((1, width), F32)
    for c in range(chunks):
        cut = pl.ds(c * step, step)
        value = term(member, c)
        quad[c].wait_recv()
        quad[2 * chunks + c].wait_recv()
        dy = value + crc[0, cut, :].astype(F32) + nrc[cut, :].astype(F32)
        rows_in = x[cut, :].astype(F32)
        center = rows_in - jnp.mean(rows_in, axis=-1, keepdims=True)
        rstd = lax.rsqrt(jnp.mean(center * center, axis=-1, keepdims=True) + EPS)
        hat = center * rstd
        gain_sum = gain_sum + jnp.sum(dy * hat, axis=0, keepdims=True)
        shift_sum = shift_sum + jnp.sum(dy, axis=0, keepdims=True)
        dh = dy * gain[...]
        inner = dh - jnp.mean(dh, axis=-1, keepdims=True) - hat * jnp.mean(dh * hat, axis=-1, keepdims=True)
        tgs[cut, :] = (gres[cut, :] + rstd * inner).astype(BF)
        r = rcopy(tgs.at[cut], tg.at[cut], tg_s.at[c], tg_r.at[c], swap_to)
        stay = pltpu.make_async_copy(tgs.at[cut], tg.at[cut], tg_l.at[c])
        tg_remote.append(r)
        tg_local.append(stay)

        @pl.when(jnp.logical_not(stays))
        def _(r=r):
            r.start()

        @pl.when(stays)
        def _(stay=stay):
            stay.start()

    small = v_in.shape[2]
    for k in range(nd):
        vmine[k] = v_in[k]
        vmine[k, 0:1, :] = gain_sum[:, k * small : (k + 1) * small]
        vmine[k, 1:2, :] = shift_sum[:, k * small : (k + 1) * small]
    vec = []
    for k in range(1, nd):
        c = rcopy(vmine.at[offset(k)], vrc.at[k], v_s.at[k], v_r.at[k], (seq, offset(k)))
        c.start()
        vec.append(c)
        sends.append(c)

    s2(1)
    s2(2)
    s6(0)
    s1(3)
    total = vmine[me]
    for k, c in enumerate(vec):
        c.wait_recv()
        total = total + vrc[k + 1]
    vz[seq] = total
    z_copies = []
    for i, dev in enumerate((near_to, far_to, third_to)):
        c = rcopy(vz.at[seq], vz.at[seq], vz_s.at[i], vz_r.at[i], dev)
        c.start()
        z_copies.append(c)
        sends.append(c)
    s3(1)
    s3(2)
    s2(3)
    s4(1)
    s4(2)
    s3(3)
    s5(1)
    s5(2)
    s4(3)
    s6(1)
    s6(2)
    s5(3)
    for c in z_copies:
        c.wait_recv()
    total = vz[0]
    for i in range(1, ns):
        total = total + vz[i]
    vout[...] = total
    for a in range(3):
        s7(a)

    @pl.when(jnp.logical_not(stays))
    def _():
        out_remote.wait()
        for c in tg_remote:
            c.wait()

    @pl.when(stays)
    def _():
        out_local.wait()
        for c in tg_local:
            c.wait()

    for c in sends:
        c.wait_send()


def back(ga, qkv, att, lse, starts, n1t, wf, x, gres, gain, v_in, res, dwr, dwe, dwo, ns, nd, heads, d):
    n_rows, width = x.shape
    n, group, ncol, chunks = n_rows * ns, width // 4, nd // 2, 4
    any_, vmem = pl.BlockSpec(memory_space=pl.ANY), pl.BlockSpec(memory_space=pltpu.VMEM)
    dma = lambda *shape: pltpu.SemaphoreType.DMA(shape)
    one = pltpu.SemaphoreType.DMA
    sds = jax.ShapeDtypeStruct
    sizes = [(t.shape[0] // ncol, t.shape[1]) for t in (dwr, dwe, dwo)] + [(width // ncol, 3 * group)]
    vm = lambda dtype, *shape: pltpu.VMEM(shape, dtype)
    slots = max(11, nd)
    rr, cc = width // nd, 3 * group
    return pl.pallas_call(
        functools.partial(back_kernel, ns=ns, nd=nd, heads=heads, d=d, bq=n_rows // 2, bk=n_rows, chunks=chunks),
        in_specs=[vmem] * 11 + [any_] * 4,
        out_specs=[any_, any_, vmem, vmem, vmem, any_, vmem],
        out_shape=[
            sds(x.shape, BF), sds(x.shape, BF), sds((rr, 3 * width), BF), sds((rr, width), BF),
            sds((rr, 2 * dwe.shape[1]), BF), sds(sizes[0], BF), sds(v_in.shape[1:], F32),
        ],
        scratch_shapes=[
            vm(BF, n, group), vm(BF, group, n), vm(BF, group, n), vm(BF, group, n), vm(F32, group, n),
            vm(F32, heads // 2, 2, n), vm(BF, n, 3 * group), vm(BF, width, 3 * group),
            vm(BF, 2 * rr, cc), vm(BF, 2 * rr, cc), vm(BF, 2 * rr, cc), vm(BF, 2 * rr, cc), vm(BF, 2, rr, cc),
            vm(BF, 2, n_rows, width), vm(BF, 2, n_rows, width), vm(BF, n_rows, width), vm(BF, n_rows, width),
            vm(BF, n_rows, width), vm(F32, *v_in.shape), vm(F32, *v_in.shape), vm(F32, ns, *v_in.shape[1:]),
            [vm(BF, r, c) for r, c in sizes],
            [vm(BF, 2, r // 2, c) for r, c in sizes],
            [vm(BF, 4, r // 2, c) if nd == 8 else vm(BF, ncol - 1, r, c) for r, c in sizes],
            [vm(BF, 2, r // 2, c) for r, c in sizes],
            [vm(BF, r, c // 2) for r, c in sizes[:3]], [vm(BF, r, c // 2) for r, c in sizes[:3]],
            [vm(F32, r, c // 2) for r, c in sizes[:3]],
            [vm(BF, r, c // 4) for r, c in sizes[:3]], [vm(BF, r, c // 4) for r, c in sizes[:3]],
            [vm(BF, r, c) for r, c in sizes[:3]], [vm(BF, r // 2, c) for r, c in sizes[:3]],
            dma(4), dma(4), one, dma(4, slots), dma(4, slots), dma(4, 4),
            dma(3 * chunks), dma(3 * chunks), one, one, one, dma(chunks), dma(chunks), dma(chunks),
            dma(nd), dma(nd), dma(3), dma(3),
        ],
        compiler_params=pltpu.CompilerParams(
            collective_id=1, has_side_effects=True, vmem_limit_bytes=60 << 20
        ),
        cost_estimate=pl.CostEstimate(
            flops=20 * n * n * d * heads, bytes_accessed=60_000_000, transcendentals=n * n * heads
        ),
    )(ga, qkv, att, lse, starts, n1t, wf, x, gres, gain, v_in, res, dwr, dwe, dwo)


def layer_normalize(values, gain, shift):
    center = values - jnp.mean(values, axis=-1, keepdims=True)
    spread = jnp.mean(center * center, axis=-1, keepdims=True)
    return center * lax.rsqrt(spread + EPS) * gain + shift


def smooth_gate(values):
    return jax.nn.gelu(values, approximate=True)


def rows(array, start, size):
    return lax.dynamic_slice_in_dim(array, start, size, 0)


def cols(array, start, size):
    return lax.dynamic_slice_in_dim(array, start, size, 1)


def put(array, piece, row, col):
    return lax.dynamic_update_slice(array, piece, (row, col))


def bf_round(x):
    return lax.reduce_precision(x, 8, 7)


class Links:
    def __init__(self, ns, nd):
        self.ns, self.nd = ns, nd

    def go(self, array, target):
        pairs = []
        for s in range(self.ns):
            for d in range(self.nd):
                ts, td = target(s, d)
                pairs.append((s * self.nd + d, ts * self.nd + td))
        return lax.ppermute(array, ("seq", "dp"), pairs)

    def dp(self, array, k):
        return self.go(array, lambda s, d: (s, d ^ k))

    def core(self, array):
        return self.dp(array, 1)

    def near(self, array):
        return self.go(array, lambda s, d: (s ^ 1, d))

    def far(self, array):
        return self.go(array, lambda s, d: (s ^ 2, d))

    def both(self, array):
        return self.go(array, lambda s, d: (s ^ 1, d ^ 1))

    def swap(self, array):
        return self.go(array, lambda s, d: (2 * (d % 2) + s % 2, d - d % 2 + s // 2))


def on_device(
    tokens, lengths, cotangent, mixer_input, mixer_output, expand_weight, reduce_weight,
    first_gain, first_shift, second_gain, second_shift, output_bias, expand_bias, reduce_bias,
):
    ns, nd = lax.axis_size("seq"), lax.axis_size("dp")
    links = Links(ns, nd)
    seq, me = lax.axis_index("seq"), lax.axis_index("dp")
    half, near_bit, core = seq // 2, seq % 2, me % 2
    column = me // 2
    member = 2 * core + near_bit
    n_rows, width = tokens.shape[1:]
    slots = n_rows * ns
    head_dim = width // HEADS
    hidden = reduce_weight.shape[0] * nd
    group = width // 4
    my_heads = HEADS // 4

    lengths_row = jnp.where(half == core, lengths[0], links.core(lengths)[0])
    entry = jnp.arange(lengths_row.shape[0])
    ends = jnp.sum(jnp.where(entry[None, :] <= entry[:, None], lengths_row[None, :], 0), axis=1)
    place = jnp.arange(slots, dtype=jnp.int32)
    passed = place[:, None] >= ends[None, :]
    starts = jnp.max(jnp.where(passed, ends[None, :], 0), axis=1)
    starts = jnp.where(place < ends[-1], starts, place).reshape(1, slots)
    live = (member * n_rows + jnp.arange(n_rows, dtype=jnp.int32) < ends[-1]).astype(F32)

    small, small_rows = width // nd, mixer_input.shape[0]
    wide = hidden // nd
    vectors = jnp.concatenate(
        [first_gain, first_shift, second_gain, second_shift, output_bias, reduce_bias, expand_bias]
    ).reshape(-1, small)
    vectors = jnp.concatenate([vectors, jnp.zeros((-vectors.shape[0] % 16, small), BF)])
    by_core = expand_weight.reshape(small_rows, nd // 2, 2, wide).transpose(2, 0, 1, 3)
    by_core = by_core.reshape(2, small_rows, hidden // 2)
    (
        x_low, grad_low, twin_grad, normed_t, input_full, output_full, expand_half, reduce_half, vectors,
        qkv, attended, logsum, attention,
    ) = front(
        tokens[0], cotangent[0], mixer_input, mixer_output, by_core, reduce_weight, vectors,
        starts, ns, nd, my_heads, head_dim,
    )
    twin_attention = links.core(attention)
    vectors = vectors.astype(F32)
    gain_one, _, gain_two, shift_two, output_add, reduce_add = (vectors[:, i].reshape(-1) for i in range(6))
    n_wide = wide // small
    expand_add = vectors[:, 6 : 6 + n_wide].reshape(nd // 2, 2, wide)
    expand_add = lax.dynamic_index_in_dim(expand_add, core, 1, keepdims=False).reshape(-1)

    inputs = x_low.astype(F32)
    resid = inputs + mm(attention, output_full) + output_add
    normed_two = layer_normalize(resid, gain_two, shift_two).astype(BF)
    normed_two = jnp.concatenate([normed_two, links.core(normed_two)])
    expanded = mm(normed_two, expand_half) + expand_add
    active = smooth_gate(expanded).astype(BF)
    reduced = mm(active, reduce_half)
    twin_part = links.core(reduced[n_rows:].astype(BF)).astype(F32)
    result = (resid + reduced[:n_rows] + twin_part + reduce_add).astype(BF)

    twin_live = ((member ^ 2) * n_rows + jnp.arange(n_rows, dtype=jnp.int32) < ends[-1]).astype(F32)
    grad_result = grad_low.astype(F32) * live[:, None]
    result_low = jnp.concatenate([grad_result.astype(BF), (twin_grad.astype(F32) * twin_live[:, None]).astype(BF)])
    reduce_term = mm_left(active, result_low).astype(BF)
    reduce_bias_sum = jnp.sum(grad_result, axis=0)
    grad_active = mm_right(result_low, reduce_half)
    _, gate_back = jax.vjp(smooth_gate, expanded)
    grad_expanded = gate_back(grad_active)[0]
    expand_bias_sum = jnp.sum(grad_expanded, axis=0)
    expanded_low = grad_expanded.astype(BF)
    expand_term = mm_left(normed_two, expanded_low).astype(BF)
    grad_normed = mm_right(expanded_low, expand_half)
    grad_normed_two = grad_normed[:n_rows] + links.core(grad_normed[n_rows:].astype(BF)).astype(F32)
    _, second_back = jax.vjp(layer_normalize, resid, gain_two, shift_two)
    resid_part, gain_two_sum, shift_two_sum = second_back(grad_normed_two)
    grad_resid = grad_result + resid_part
    output_bias_sum = jnp.sum(grad_resid, axis=0)
    resid_low = grad_resid.astype(BF)
    grad_attention = mm_right(resid_low, output_full).astype(BF)
    both_low = jnp.concatenate([resid_low, links.core(resid_low)])
    both_low = cols(both_low, core * (width // 2), width // 2)
    output_term = mm_left(jnp.concatenate([attention, twin_attention]), both_low).astype(BF)

    sums = jnp.stack([gain_two_sum, shift_two_sum, output_bias_sum, reduce_bias_sum])
    sums = sums.reshape(4, nd, small).transpose(1, 0, 2)
    wide_sum = expand_bias_sum.reshape(nd // 2, 1, n_wide, small)
    parity = jnp.arange(2).reshape(1, 2, 1, 1)
    wide_sum = jnp.where(parity == core, wide_sum, 0.0).reshape(nd, n_wide, small)
    pad = -(6 + n_wide) % 8
    sums = jnp.concatenate([jnp.zeros((nd, 2, small)), sums, wide_sum, jnp.zeros((nd, pad, small))], axis=1)

    layer_output, tokens_gradient, input_sum, output_sum, expand_sum, reduce_sum, sums = back(
        grad_attention, qkv, attended, logsum, starts, normed_t, input_full, x_low, grad_resid,
        gain_one.reshape(1, width), sums, result, reduce_term, expand_term, output_term,
        ns, nd, my_heads, head_dim,
    )
    return (
        layer_output[None],
        tokens_gradient.astype(F32)[None],
        input_sum.astype(F32),
        output_sum.astype(F32),
        expand_sum.astype(F32),
        reduce_sum.astype(F32),
        sums[0],
        sums[1],
        sums[2],
        sums[3],
        sums[4],
        sums[6 : 6 + n_wide].reshape(-1),
        sums[5],
    )


def solution(mesh):
    row, vec = P("dp", None), P("dp")
    act = P("dp", "seq", None)
    return jax.shard_map(
        on_device,
        mesh=mesh,
        in_specs=(act, row, act, row, row, row, row, vec, vec, vec, vec, vec, vec, vec),
        out_specs=(act, act, row, row, row, row, vec, vec, vec, vec, vec, vec, vec),
        check_vma=False,
    )
```

time: 573 us -> 445 us (0.78)
  Pallas kernels: 157 us -> 340 us
  waiting for transfers between devices: 181 us -> 0.02 us
  blocking collectives: 46.4 us -> 0 us
  starting transfers between devices: 43.9 us -> 2.13 us
  local copies, waits for them, and re-layouts: 31.5 us -> 12.7 us
  matrix products: 77.2 us -> 60.1 us
    pallas_call x1, Pallas kernels: 31 us -> 226 us  [back(): pl.pallas_call(functools.partial(back_kernel, ns=ns, nd=nd, heads=heads,...]
    ppermute x49 -> x6, waiting for transfers between devices: 181 us -> 0.02 us  [go(): return lax.ppermute(array, ('seq', 'dp'), pairs)]
    psum x1 -> x0, blocking collectives: 46.4 us -> none  [on_device(): sums = lax.psum(sums, ('seq', 'dp'))]
    ppermute x49 -> x6, starting transfers between devices: 43.9 us -> 2.13 us  [go(): return lax.ppermute(array, ('seq', 'dp'), pairs)]
    dot_general x14 -> x9, matrix products: 77.2 us -> 60.1 us  [_dot(): lax.dot_general(a, b, (((ca,), (cb,)), ((), ())), preferred_element_type=...]
    unnamed x85 -> x53, local copies, waits for them, and re-layouts: 17.4 us -> 4.12 us
    pallas_call x1, Pallas kernels: 126 us -> 114 us  [front(): pl.pallas_call(functools.partial(front_kernel, ns=ns, nd=nd, heads=heads,...]
    add x6 -> x0, other arithmetic: 8.04 us -> none  [the longest x3 5.51 us: scatter(): total = total + links.dp(chip[i].astype(BF), 2 * i).astype(F32)]
  transfers between devices with their start and end apart: 49 -> 6, of which waited for: 22 -> 0; matrix products, arithmetic and copies ran while one was open for 9% -> 15% of each run, Pallas kernels for 5% -> 0%
where the time goes in v3:
time: 445 us; the launch traced here: 437 us
  Pallas kernels  340 us (76%)
  matrix products  60.1 us (14%)
  other arithmetic  20.8 us (5%)
  local copies, waits for them, and re-layouts  12.7 us (3%)
    pallas_call x1, Pallas kernels, back(): pl.pallas_call(functools.partial(back_kernel, ns=ns, nd=nd, heads=heads,...  226 us
    pallas_call x1, Pallas kernels, front(): pl.pallas_call(functools.partial(front_kernel, ns=ns, nd=nd, heads=heads,...  114 us
    dot_general x9, matrix products, _dot(): lax.dot_general(a, b, (((ca,), (cb,)), ((), ())), preferred_element_type=...  60.1 us
  transfers between devices with their start and end apart: 6, of which 0 were waited for; matrix products, arithmetic and copies ran while one was open for 15% of the time, Pallas kernels for 0%

profile of v3, /device:TPU:0, one launch (start us, length us, event | category | flops | bytes accessed | tf_op | source)
XLA Modules:
  0.0 436.6 jit_solution(8292414433566546851)
XLA Ops:
  0.7 0.5 collective-permute-start
  1.3 1.8 reshape.128
  3.1 0.4 copy.30
  3.5 1.6 reshape.129.we
  5.1 0.2 dynamic-update-slice
  5.3 0.2 dynamic-update-slice.1
  5.5 0.2 dynamic-update-slice.2
  5.7 0.2 dynamic-update-slice.3
  6.0 0.2 dynamic-update-slice.4
  6.2 0.2 dynamic-update-slice.5
  6.4 0.2 dynamic-update-slice.6
  6.6 0.0 collective-permute-done
  6.7 0.1 select_reduce_fusion.1
  6.8 0.6 slice.58
  7.4 0.1 select_reduce_fusion
  7.5 0.7 compare_select_fusion.st
  8.2 113.6 %shard_map.237 = (bf16[512,1024]{1,0:T(8,128)(2,1)}, bf16[512,1024]{1,0:T(8,128)(2,1)}, bf16[512,1024]{1,0:T(8,128)(2,1)}, bf16[1024,2048]{1,0:T(8,128)(2,1)}, b...) custom-call(bf16[512,1024]{1,0:T(8,128)(2,1)} %bitcast.72, ...), custom_call_target="tpu_custom_call" | custom-call | flops 8589934592 | bytes 60000000 | tf_op jit(solution)/shard_map/pallas_call | solution.py:367
  121.8 0.0 copy-start.3
  121.8 3.5 fusion.40
  125.4 0.3 multiply_reduce_fusion.2
  125.8 1.4 add_convert_fusion
  127.1 0.4 collective-permute-start.1
  127.5 0.1 broadcast_in_dim.94
  127.6 0.1 pad.8.clone
  127.7 0.2 collective-permute-start.4
  128.0 0.8 fusion.25
  128.8 0.8 fusion.26
  129.6 0.6 slice_bitcast_fusion.gain
  130.2 1.6 multiply_convert_fusion.1
  131.9 0.0 collective-permute-done.1
  131.9 6.2 %fusion.21 = f32[1024,2048]{1,0:T(8,128)S(1)} fusion(bf16[1024,2048]{1,0:T(8,128)(2,1)S(1)} %copy-done.20, bf16[512,1024]{1,0:T(8,128)(2,1)} %collective-permute-done.1, bf16[512,1024]{1,0:T(8,128)(2,1)} %add_convert_fusion), kind=kOutput, calls=%fused_computation.42 | convolution fusion | flops 4299161600 | bytes 14680064 | tf_op jit(solution)/shard_map/dot_general | solution.py:18
  138.1 5.4 %fusion.36 = f32[1024,1024]{1,0:T(8,128)S(1)} fusion(bf16[2048,1024]{1,0:T(8,128)(2,1)S(1)} %copy-done.22, f32[1024,2048]{1,0:T(8,128)S(1)} %fusion.21, f32[2048]{0:T(1024)S(1)} %bitcast.67), kind=kOutput, calls=%fused_computation.83 | convolution fusion | flops 4315938816 | bytes 16785408 | tf_op jit(solution)/shard_map/dot_general | solution.py:18
  143.6 13.1 %fusion.41 = (f32[2048]{0:T(1024)S(1)}, bf16[1024,2048]{1,0:T(8,128)(2,1)}) fusion(f32[1024,2048]{1,0:T(8,128)S(1)} %fusion.21, f32[2048]{0:T(1024)S(1)} %bitcast.68, bf16[2048,1024]{1,0:T(8,128)(2,1)} %get-tuple-element.35, bf16[512,1024]{1,0:T(8,128)(2,1)S(1)} %get-tuple-element.76, bf16[512,1024]{1,0:T(8,128)(2,1)S(1)} %get-tuple-element.77), kind=kOutput, calls=%fused_computation.88 | convolution fusion | flops 4345296896 | bytes 18890752 | tf_op jit(solution)/shard_map/dot_general | solution.py:18
  156.7 6.5 %fusion.14 = f32[1024,1024]{1,0:T(8,128)S(1)} fusion(bf16[1024,2048]{1,0:T(8,128)(2,1)S(1)} %copy-done.20, bf16[1024,2048]{1,0:T(8,128)(2,1)} %get-tuple-element.75), kind=kOutput, calls=%fused_computation.31 | convolution fusion | flops 4294967296 | bytes 12582912 | tf_op jit(solution)/shard_map/dot_general | solution.py:18
  163.2 0.2 slice.113
  163.4 0.2 slice.112
  163.5 0.5 collective-permute-start.3
  164.0 0.1 collective-permute-start.2
  164.1 11.8 %convolution_convert_fusion.1.dwr = bf16[2048,1024]{1,0:T(8,128)(2,1)} fusion(bf16[512,1024]{1,0:T(8,128)(2,1)S(1)} %get-tuple-element.76, bf16[512,1024]{1,0:T(8,128)(2,1)S(1)} %get-tuple-element.77, f32[1024,2048]{1,0:T(8,128)} %copy-done.19, f32[2048]{0:T(1024)S(1)} %bitcast.69), kind=kOutput, calls=%fused_computation.10 | convolution fusion | flops 4322230272 | bytes 14688256 | tf_op jit(solution)/shard_map/dot_general | solution.py:18
  175.9 0.0 collective-permute-done.2
  175.9 1.0 multiply_reduce_fusion
  176.9 0.0 collective-permute-done.3
  176.9 2.2 fusion.38
  179.1 0.5 fusion.37
  179.6 0.0 copy-start.4
  179.7 0.2 convert_element_type.91
  179.8 0.5 collective-permute-start.5
  180.3 1.8 copy-done.21
  182.1 7.8 %convolution_convert_fusion.dwe = bf16[1024,2048]{1,0:T(8,128)(2,1)} fusion(bf16[1024,2048]{1,0:T(8,128)(2,1)S(1)} %copy-done.21, bf16[512,1024]{1,0:T(8,128)(2,1)} %collective-permute-done.1, bf16[512,1024]{1,0:T(8,128)(2,1)} %add_convert_fusion), kind=kOutput, calls=%fused_computation.9 | convolution fusion | flops 4301258752 | bytes 10485760 | tf_op jit(solution)/shard_map/dot_general | solution.py:18
  189.9 0.1 bitcast_select_fusion
  190.0 0.7 maximum_maximum_fusion.v_in
  190.7 2.3 convolution_convert_fusion.2.ga
  192.9 0.0 collective-permute-done.4
  192.9 0.0 collective-permute-done.5
  192.9 3.5 fusion.18.dwo
  196.4 225.9 %shard_map.238 = (bf16[512,1024]{1,0:T(8,128)(2,1)}, bf16[512,1024]{1,0:T(8,128)(2,1)}, bf16[128,3072]{1,0:T(8,128)(2,1)}, bf16[128,1024]{1,0:T(8,128)(2,1)}, bf...) custom-call(bf16[512,1024]{1,0:T(8,128)(2,1)} %convolution_convert_fusion.2.ga, ...), custom_call_target="tpu_custom_call" | custom-call | flops 21474836480 | bytes 60000000 | tf_op jit(solution)/shard_map/pallas_call | solution.py:873
  422.4 1.4 slice_bitcast_fusion.1
  423.7 1.4 slice_bitcast_fusion.2
  425.2 1.8 convert_element_type.100
  427.0 2.5 convert_element_type.99
  429.5 2.9 bitcast_convert_fusion
  432.4 1.5 convert_element_type.101
  433.9 1.6 convert_element_type.102
  435.5 1.0 copy.39
  (61 shorter events, 0.2 us)
Async XLA Ops:
  0.6 6.0 %copy-start.16 = (s32[1,4]{1,0:T(1,128)S(1)}, s32[1,4]{1,0:T(1,128)}, u32[]{:S(2)}) copy-start(s32[1,4]{1,0:T(1,128)} %param.15) | copy-start | bytes 52
  0.7 4.5 %copy-start.10 = (bf16[128]{0:T(256)(128)(2,1)S(1)}, bf16[128]{0:T(256)(128)(2,1)}, u32[]{:S(2)}) copy-start(bf16[128]{0:T(256)(128)(2,1)} %param.21) | copy-start | bytes 772
  0.7 4.6 %copy-start.11 = (bf16[128]{0:T(256)(128)(2,1)S(1)}, bf16[128]{0:T(256)(128)(2,1)}, u32[]{:S(2)}) copy-start(bf16[128]{0:T(256)(128)(2,1)} %param.22) | copy-start | bytes 772
  0.7 4.8 %copy-start.12 = (bf16[128]{0:T(256)(128)(2,1)S(1)}, bf16[128]{0:T(256)(128)(2,1)}, u32[]{:S(2)}) copy-start(bf16[128]{0:T(256)(128)(2,1)} %param.23) | copy-start | bytes 772
  0.7 5.1 %copy-start.13 = (bf16[128]{0:T(256)(128)(2,1)S(1)}, bf16[128]{0:T(256)(128)(2,1)}, u32[]{:S(2)}) copy-start(bf16[128]{0:T(256)(128)(2,1)} %param.24) | copy-start | bytes 772
  0.7 5.3 %copy-start.14 = (bf16[128]{0:T(256)(128)(2,1)S(1)}, bf16[128]{0:T(256)(128)(2,1)}, u32[]{:S(2)}) copy-start(bf16[128]{0:T(256)(128)(2,1)} %param.25) | copy-start | bytes 772
  0.7 5.5 %copy-start.15 = (bf16[128]{0:T(256)(128)(2,1)S(1)}, bf16[128]{0:T(256)(128)(2,1)}, u32[]{:S(2)}) copy-start(bf16[128]{0:T(256)(128)(2,1)} %param.27) | copy-start | bytes 772
  0.7 5.7 %copy-start.9 = (bf16[512]{0:T(512)(128)(2,1)S(1)}, bf16[512]{0:T(512)(128)(2,1)}, u32[]{:S(2)}) copy-start(bf16[512]{0:T(512)(128)(2,1)} %param.26) | copy-start | bytes 3076
  0.7 7.4 %copy-start.2 = (bf16[128,1024]{1,0:T(8,128)(2,1)S(1)}, bf16[128,1024]{1,0:T(8,128)(2,1)}, u32[]{:S(2)}) copy-start(bf16[128,1024]{1,0:T(8,128)(2,1)} %wo.1) | copy-start | bytes 786436
  0.7 7.4 %copy-start.1 = (bf16[128,3072]{1,0:T(8,128)(2,1)S(1)}, bf16[128,3072]{1,0:T(8,128)(2,1)}, u32[]{:S(2)}) copy-start(bf16[128,3072]{1,0:T(8,128)(2,1)} %win.1) | copy-start | bytes 2359300
  0.7 5.9 %collective-permute-start = (s32[1,4]{1,0:T(1,128)}, s32[1,4]{1,0:T(1,128)S(1)}, u32[]{:S(2)}, u32[]{:S(2)}) collective-permute-start(s32[1,4]{1,0:T(1,128)} %param.15), channel_id=1, source_target_pairs={{0,1},{1,0},{2,3},{3,2},{4,5},{5,4},{6,7},{7,6},{8,9},{9,8},{10,11... | collective-permute-start | bytes 56 | tf_op jit(solution)/shard_map/ppermute | solution.py:944
  8.1 113.7 %copy-start = (s32[1,2048]{1,0:T(1,128)}, s32[1,2048]{1,0:T(1,128)S(1)}, u32[]{:S(2)}) copy-start(s32[1,2048]{1,0:T(1,128)S(1)} %compare_select_fusion.st) | copy-start | bytes 24580
  121.8 3.6 copy-start.3
  125.4 4.8 %copy-start.5 = (bf16[512,1024]{1,0:T(8,128)(2,1)S(1)}, bf16[512,1024]{1,0:T(8,128)(2,1)}, u32[]{:S(2)}) copy-start(bf16[512,1024]{1,0:T(8,128)(2,1)} %get-tuple-element.33) | copy-start | bytes 3145732
  127.1 4.7 %collective-permute-start.1 = (bf16[512,1024]{1,0:T(8,128)(2,1)}, bf16[512,1024]{1,0:T(8,128)(2,1)}, u32[]{:S(2)}, u32[]{:S(2)}) collective-permute-start(bf16[512,1024]{1,0:T(8,128)(2,1)} %add_convert_fusion), channel_id=1, source_target_pairs={{0,1},{1,0},{2,3},{3,2},{4,5},{5,4},{6,7},{7,6},{8,9},{9,8},{10,11... | collective-permute-start | bytes 3145736 | tf_op jit(solution)/shard_map/ppermute | solution.py:944
  127.7 65.2 %collective-permute-start.4 = (bf16[512,1024]{1,0:T(8,128)(2,1)}, bf16[512,1024]{1,0:T(8,128)(2,1)}, u32[]{:S(2)}, u32[]{:S(2)}) collective-permute-start(bf16[512,1024]{1,0:T(8,128)(2,1)} %get-tuple-element.37), channel_id=1, source_target_pairs={{0,1},{1,0},{2,3},{3,2},{4,5},{5,4},{6,7},{7,6},{8,9},{9,8},{10,11... | collective-permute-start | bytes 3145736 | tf_op jit(solution)/shard_map/ppermute | solution.py:944
  128.0 3.9 copy-start.20
  131.9 6.2 %copy-start.22 = (bf16[2048,1024]{1,0:T(8,128)(2,1)S(1)}, bf16[2048,1024]{1,0:T(8,128)(2,1)}, u32[]{:S(2)}) copy-start(bf16[2048,1024]{1,0:T(8,128)(2,1)} %get-tuple-element.35) | copy-start | bytes 12582916
  138.1 5.4 %copy-start.19 = (f32[1024,2048]{1,0:T(8,128)}, f32[1024,2048]{1,0:T(8,128)S(1)}, u32[]{:S(2)}) copy-start(f32[1024,2048]{1,0:T(8,128)S(1)} %fusion.21) | copy-start | bytes 25165828
  163.5 13.4 %collective-permute-start.3 = (bf16[512,1024]{1,0:T(8,128)(2,1)S(1)}, bf16[512,1024]{1,0:T(8,128)(2,1)S(1)}, u32[]{:S(2)}, u32[]{:S(2)}) collective-permute-start(bf16[512,1024]{1,0:T(8,128)(2,1)S(1)} %slice.112), channel_id=1, source_target_pairs={{0,1},{1,0},{2,3},{3,2},{4,5},{5,4},{6,7},{7,6},{8,9},{9,8},{10,11... | collective-permute-start | bytes 3145736 | tf_op jit(solution)/shard_map/ppermute | solution.py:944
  164.0 12.0 %collective-permute-start.2 = (bf16[512,1024]{1,0:T(8,128)(2,1)S(1)}, bf16[512,1024]{1,0:T(8,128)(2,1)S(1)}, u32[]{:S(2)}, u32[]{:S(2)}) collective-permute-start(bf16[512,1024]{1,0:T(8,128)(2,1)S(1)} %slice.113), channel_id=1, source_target_pairs={{0,1},{1,0},{2,3},{3,2},{4,5},{5,4},{6,7},{7,6},{8,9},{9,8},{10,11... | collective-permute-start | bytes 3145736 | tf_op jit(solution)/shard_map/ppermute | solution.py:944
  179.1 2.9 copy-start.21
  179.6 10.2 %copy-start.4 = (f32[512,1024]{1,0:T(8,128)}, f32[512,1024]{1,0:T(8,128)S(1)}, u32[]{:S(2)}) copy-start(f32[512,1024]{1,0:T(8,128)S(1)} %get-tuple-element.57.gres) | copy-start | bytes 6291460
  179.8 10.8 %copy-start.18 = (bf16[1024,1024]{1,0:T(8,128)(2,1)S(1)}, bf16[1024,1024]{1,0:T(8,128)(2,1)}, u32[]{:S(2)}) copy-start(bf16[1024,1024]{1,0:T(8,128)(2,1)} %get-tuple-element.38) | copy-start | bytes 6291460
  179.8 13.1 %collective-permute-start.5 = (bf16[512,1024]{1,0:T(8,128)(2,1)S(1)}, bf16[512,1024]{1,0:T(8,128)(2,1)S(1)}, u32[]{:S(2)}, u32[]{:S(2)}) collective-permute-start(bf16[512,1024]{1,0:T(8,128)(2,1)S(1)} %convert_element_type.91), channel_id=1, source_target_pairs={{0,1},{1,0},{2,3},{3,2},{4,5},{5,4},{6,7},{7,6},{8,9},{9,8},{10,11... | collective-permute-start | bytes 3145736 | tf_op jit(solution)/shard_map/ppermute | solution.py:944
  190.7 2.3 copy-start.17
  422.3 10.0 %copy-start.7 = (bf16[128,4096]{1,0:T(8,128)(2,1)S(1)}, bf16[128,4096]{1,0:T(8,128)(2,1)}, u32[]{:S(2)}) copy-start(bf16[128,4096]{1,0:T(8,128)(2,1)} %get-tuple-element.50) | copy-start | bytes 3145732
  427.0 6.9 %copy-start.6 = (bf16[512,1024]{1,0:T(8,128)(2,1)S(1)}, bf16[512,1024]{1,0:T(8,128)(2,1)}, u32[]{:S(2)}) copy-start(bf16[512,1024]{1,0:T(8,128)(2,1)} %get-tuple-element.51) | copy-start | bytes 3145732
  429.5 6.0 %copy-start.8 = (bf16[512,1024]{1,0:T(8,128)(2,1)S(1)}, bf16[512,1024]{1,0:T(8,128)(2,1)}, u32[]{:S(2)}) copy-start(bf16[512,1024]{1,0:T(8,128)(2,1)} %get-tuple-element.46) | copy-start | bytes 3145732
